TPU v7x, 128 devices: a whole 4x4x4 slice. The times are simulated.
128 devices in a mesh: weights: 8 (over z, core), context: 4 (over x), tensor: 4 (over y).
Axes of the slice: x: 4, y: 4, z: 4, core: 2. Of those that a mesh axis runs over, the one named last changes fastest.
Arguments:
- tokens: bfloat16 [16384, 2048], P(('weights', 'context')), may hold values from -6 to 6
- cotangent: bfloat16 [16384, 2048], P(('weights', 'context')), may hold values from -6 to 6
- token_document_ids: int32 [8, 2048], P('weights'), may hold values from 0 to 2, as said below
- sequence_adapter_index: int32 [8], P('weights'), may hold values from 0 to 7
- mixer_norm_gain: float32 [2048], replicated, may hold values from 0.1 to 1.9
- head_norm_gain: float32 [128], replicated, may hold values from 0.1 to 1.9
- feedforward_norm_gain: float32 [2048], replicated, may hold values from 0.1 to 1.9
- short_filter_kernels: float32 [3, 4, 2048], P(None, None, 'tensor'), may hold values from -3 to 3
- query_weight: bfloat16 [2048, 2048], P(('weights', 'context'), 'tensor'), may hold values from -0.125 to 0.125
- key_weight: bfloat16 [2048, 2048], P(('weights', 'context'), 'tensor'), may hold values from -0.125 to 0.125
- value_weight: bfloat16 [2048, 2048], P(('weights', 'context'), 'tensor'), may hold values from -0.125 to 0.125
- strength_weight: bfloat16 [2048, 16], P(('weights', 'context'), 'tensor'), may hold values from -0.125 to 0.125
- mixer_output_weight: bfloat16 [2048, 2048], P('tensor', ('weights', 'context')), may hold values from -0.125 to 0.125
- gate_weight: bfloat16 [2048, 5632], P(('weights', 'context'), 'tensor'), may hold values from -0.125 to 0.125
- up_weight: bfloat16 [2048, 5632], P(('weights', 'context'), 'tensor'), may hold values from -0.125 to 0.125
- down_weight: bfloat16 [5632, 2048], P('tensor', ('weights', 'context')), may hold values from -0.078125 to 0.078125
- adapter_attention_input: bfloat16 [4, 8, 2048, 16], replicated, may hold values from -0.125 to 0.125
- adapter_triple_output: bfloat16 [3, 8, 16, 2048], P(None, None, None, 'tensor'), may hold values from -1.5 to 1.5
- adapter_strength_output: bfloat16 [8, 16, 16], P(None, None, 'tensor'), may hold values from -1.5 to 1.5
- adapter_projection_input: bfloat16 [8, 2048, 16], P(None, 'tensor'), may hold values from -0.125 to 0.125
- adapter_projection_output: bfloat16 [8, 16, 2048], replicated, may hold values from -1.5 to 1.5
- adapter_feedforward_input: bfloat16 [2, 8, 2048, 16], replicated, may hold values from -0.125 to 0.125
- adapter_feedforward_output: bfloat16 [2, 8, 16, 5632], P(None, None, None, 'tensor'), may hold values from -1.5 to 1.5
- adapter_down_input: bfloat16 [8, 5632, 16], P(None, 'tensor'), may hold values from -0.078125 to 0.078125
- adapter_down_output: bfloat16 [8, 16, 2048], replicated, may hold values from -1.5 to 1.5
Outputs:
- block_out: bfloat16 [16384, 2048], P(('weights', 'context'))
- tokens_grad: float32 [16384, 2048], P(('weights', 'context'))
- grad_attn_in: float32 [4, 8, 2048, 16], replicated
- grad_qkv_out: float32 [3, 8, 16, 2048], P(None, None, None, 'tensor')
- grad_beta_out: float32 [8, 16, 16], P(None, None, 'tensor')
- grad_o_in: float32 [8, 2048, 16], P(None, 'tensor')
- grad_o_out: float32 [8, 16, 2048], replicated
- grad_ffn_in: float32 [2, 8, 2048, 16], replicated
- grad_ffn_out: float32 [2, 8, 16, 5632], P(None, None, None, 'tensor')
- grad_down_in: float32 [8, 5632, 16], P(None, 'tensor')
- grad_down_out: float32 [8, 16, 2048], replicated
Inputs may be any that keep to these rules, and one draw needn't show every extreme that they name: `token_document_ids`: segment ids never fall along a sequence.
All inputs are finite; a program needn't handle non-finite values.
Results may differ from a plain program's by a relative error of at most 0.023.
Values may be sent and summed in bfloat16 or wider, within the bound.
No kernel may reach another device: no remote copies, remote signals or barrier semaphores. Data moves between devices by JAX's collectives and lax.ppermute only.
A program may use at most 192 MiB of HBM per device.

v0:
```python
import jax
import jax.numpy as jnp
from jax import lax
from jax.sharding import PartitionSpec as P

BLOCK = 64


EXACT_ARITHMETIC = lax.Precision.HIGHEST
EPSILON = 1e-06


def from_behind(block, axis, distance):
    devices = range(lax.axis_size(axis))
    route = [(i - distance, i) for i in devices if i - distance in devices]
    return lax.ppermute(block, axis, route)


def matmul(left, right):
    return jnp.dot(left, right, preferred_element_type=jnp.float32)


def rms_scale(values, gain):
    return values * lax.rsqrt(jnp.mean(values * values, axis=-1, keepdims=True) + EPSILON) * gain


def unit_rows(values):
    return values * lax.rsqrt(jnp.sum(values * values, axis=-1, keepdims=True) + EPSILON)


def block_solve(key_unit, value_rows, beta_rate, segments):
    tile_line_batch = segments.shape[0]
    same_doc = (segments[:, None] == segments[None, :]).astype(jnp.float32)
    row_ids = jnp.arange(tile_line_batch, dtype=jnp.int32)[:, None]
    col_ids = jnp.arange(tile_line_batch, dtype=jnp.int32)[None, :]
    strict = (row_ids > col_ids).astype(jnp.float32) * same_doc
    key_rows = jnp.transpose(key_unit, (1, 0, 2))
    values_head = jnp.transpose(value_rows, (1, 0, 2))
    rates = jnp.transpose(beta_rate, (1, 0))[:, :, None]
    key_gram = jnp.einsum("hik,hjk->hij", key_rows, key_rows, precision=EXACT_ARITHMETIC)
    unit_lower = jnp.eye(tile_line_batch, dtype=jnp.float32)[None] + rates * key_gram * strict[None]
    weighted_value = jax.scipy.linalg.solve_triangular(
        unit_lower, rates * key_rows, lower=True, unit_diagonal=True
    )
    state_updates = jax.scipy.linalg.solve_triangular(
        unit_lower, rates * values_head, lower=True, unit_diagonal=True
    )
    return (weighted_value, state_updates)


def block_step(recurrent_associative_matrix, pieces):
    query_unit, key_unit, weighted_value, state_updates, segments, previous = pieces
    tile_line_batch = segments.shape[0]
    same_doc = (segments[:, None] == segments[None, :]).astype(jnp.float32)
    row_ids = jnp.arange(tile_line_batch, dtype=jnp.int32)[:, None]
    col_ids = jnp.arange(tile_line_batch, dtype=jnp.int32)[None, :]
    causal = (row_ids >= col_ids).astype(jnp.float32) * same_doc
    running_recurrent_matrix = (segments == previous).astype(jnp.float32)
    closing_segment_number = (segments == segments[tile_line_batch - 1]).astype(jnp.float32)
    query_rows = jnp.transpose(query_unit, (1, 0, 2))
    key_rows = jnp.transpose(key_unit, (1, 0, 2))
    adjusted_target_vector = state_updates - running_recurrent_matrix[None, :, None] * jnp.einsum(
        "iul,ilt->iut", weighted_value, recurrent_associative_matrix, precision=EXACT_ARITHMETIC
    )
    scores = (
        jnp.einsum("hik,hjk->hij", query_rows, key_rows, precision=EXACT_ARITHMETIC) * causal[None]
    )
    layer_outputs = running_recurrent_matrix[None, :, None] * jnp.einsum(
        "iul,ilt->iut", query_rows, recurrent_associative_matrix, precision=EXACT_ARITHMETIC
    )
    layer_outputs = layer_outputs + jnp.einsum(
        "hij,hjv->hiv", scores, adjusted_target_vector, precision=EXACT_ARITHMETIC
    )
    recurrent_associative_matrix = running_recurrent_matrix[
        tile_line_batch - 1
    ] * recurrent_associative_matrix + jnp.einsum(
        "ohk,ohz->okz",
        key_rows * closing_segment_number[None, :, None],
        adjusted_target_vector,
        precision=EXACT_ARITHMETIC,
    )
    return (recurrent_associative_matrix, jnp.transpose(layer_outputs, (1, 0, 2)))


def span_run(
    recurrent_associative_matrix,
    query_unit,
    key_unit,
    value_rows,
    beta_rate,
    segments,
    previous,
    tile_line_batch,
):
    length, heads, head_dim = query_unit.shape
    blocks = length // tile_line_batch
    key_blocks = key_unit.reshape(blocks, tile_line_batch, heads, head_dim)
    segment_blocks = segments.reshape(blocks, tile_line_batch)
    weighted_value, state_updates = jax.vmap(block_solve)(
        key_blocks,
        value_rows.reshape(blocks, tile_line_batch, heads, value_rows.shape[2]),
        beta_rate.reshape(blocks, tile_line_batch, heads),
        segment_blocks,
    )
    pieces = (
        query_unit.reshape(blocks, tile_line_batch, heads, head_dim),
        key_blocks,
        weighted_value,
        state_updates,
        segment_blocks,
        previous.reshape(blocks, tile_line_batch)[:, 0],
    )
    recurrent_associative_matrix, layer_outputs = lax.scan(
        jax.checkpoint(block_step), recurrent_associative_matrix, pieces
    )
    return (layer_outputs.reshape(length, heads, value_rows.shape[2]), recurrent_associative_matrix)


def conv_mix(extended, kernels, seg_window):
    taps = kernels.shape[0]
    length = extended.shape[0] - taps + 1
    current = seg_window[taps - 1 :]
    accumulated = jnp.zeros((length, extended.shape[1]), jnp.float32)
    for offset in range(taps):
        shifted = lax.slice_in_dim(extended, taps - 1 - offset, taps - 1 - offset + length, axis=0)
        same_doc = (
            lax.slice_in_dim(seg_window, taps - 1 - offset, taps - 1 - offset + length) == current
        ).astype(jnp.float32)
        accumulated = accumulated + kernels[offset][None, :] * shifted * same_doc[:, None]
    return accumulated


def tensor_total(parts):
    return lax.psum((parts[0], parts[1]), "tensor")


def on_device(
    tokens,
    cotangent,
    token_document_ids,
    sequence_adapter_index,
    mixer_norm_gain,
    head_norm_gain,
    feedforward_norm_gain,
    short_filter_kernels,
    query_weight,
    key_weight,
    value_weight,
    strength_weight,
    mixer_output_weight,
    gate_weight,
    up_weight,
    down_weight,
    adapter_attention_input,
    adapter_triple_output,
    adapter_strength_output,
    adapter_projection_input,
    adapter_projection_output,
    adapter_feedforward_input,
    adapter_feedforward_output,
    adapter_down_input,
    adapter_down_output,
):
    span = tokens.shape[0]
    head_dim = head_norm_gain.shape[0]
    taps = short_filter_kernels.shape[1]
    heads = strength_weight.shape[1]
    context_size = lax.axis_size("context")
    position = lax.axis_index("context")
    gathered_query, gathered_key, gathered_value, gathered_beta, gathered_out = (
        lax.all_gather(query_weight, ("weights", "context"), axis=0, tiled=True),
        lax.all_gather(key_weight, ("weights", "context"), axis=0, tiled=True),
        lax.all_gather(value_weight, ("weights", "context"), axis=0, tiled=True),
        lax.all_gather(strength_weight, ("weights", "context"), axis=0, tiled=True),
        lax.all_gather(mixer_output_weight, ("weights", "context"), axis=1, tiled=True),
    )
    gathered_gate, gathered_up, gathered_down = (
        lax.all_gather(gate_weight, ("weights", "context"), axis=0, tiled=True),
        lax.all_gather(up_weight, ("weights", "context"), axis=0, tiled=True),
        lax.all_gather(down_weight, ("weights", "context"), axis=1, tiled=True),
    )
    chosen_adapter = sequence_adapter_index[0]
    attention_input_maps = lax.dynamic_index_in_dim(
        adapter_attention_input, chosen_adapter, 1, keepdims=False
    )
    triple_output_maps = lax.dynamic_index_in_dim(
        adapter_triple_output, chosen_adapter, 1, keepdims=False
    )
    strength_output_maps = lax.dynamic_index_in_dim(
        adapter_strength_output, chosen_adapter, 0, keepdims=False
    )
    projection_input_maps = lax.dynamic_index_in_dim(
        adapter_projection_input, chosen_adapter, 0, keepdims=False
    )
    projection_output_maps = lax.dynamic_index_in_dim(
        adapter_projection_output, chosen_adapter, 0, keepdims=False
    )
    feedforward_input_maps = lax.dynamic_index_in_dim(
        adapter_feedforward_input, chosen_adapter, 1, keepdims=False
    )
    feedforward_output_maps = lax.dynamic_index_in_dim(
        adapter_feedforward_output, chosen_adapter, 1, keepdims=False
    )
    down_input_maps = lax.dynamic_index_in_dim(
        adapter_down_input, chosen_adapter, 0, keepdims=False
    )
    down_output_maps = lax.dynamic_index_in_dim(
        adapter_down_output, chosen_adapter, 0, keepdims=False
    )
    pad_ids = jnp.full((taps - 1,), -1, jnp.int32)
    seg_padded = jnp.concatenate([pad_ids, token_document_ids[0]])
    seg_window = lax.dynamic_slice_in_dim(seg_padded, position * span, span + taps - 1)
    segments = seg_window[taps - 1 :]
    previous = seg_window[taps - 2 : taps - 2 + span]
    kernels = jnp.transpose(short_filter_kernels, (1, 0, 2)).reshape(taps, -1)
    inputs = tokens.astype(jnp.float32)
    normed, norm_attn_back = jax.vjp(lambda values: rms_scale(values, mixer_norm_gain), inputs)
    normed_low = normed.astype(jnp.bfloat16)
    low_attn = jnp.einsum(
        "td,pdr->ptr", normed_low, attention_input_maps, preferred_element_type=jnp.float32
    ).astype(jnp.bfloat16)
    projected = jnp.concatenate(
        [
            matmul(normed_low, gathered_query) + matmul(low_attn[0], triple_output_maps[0]),
            matmul(normed_low, gathered_key) + matmul(low_attn[1], triple_output_maps[1]),
            matmul(normed_low, gathered_value) + matmul(low_attn[2], triple_output_maps[2]),
        ],
        axis=1,
    )
    beta_logit = matmul(normed_low, gathered_beta) + matmul(low_attn[3], strength_output_maps)
    edge_rows = from_behind(projected[span - (taps - 1) :], "context", 1)
    extended = jnp.concatenate([edge_rows, projected], axis=0)

    def prepare(extended_rows, logits):
        mixed = jax.nn.silu(conv_mix(extended_rows, kernels, seg_window))
        parts = mixed.reshape(span, 3, heads, head_dim)
        return (
            unit_rows(parts[:, 0]) * head_dim ** (-0.5),
            unit_rows(parts[:, 1]),
            parts[:, 2],
            jax.nn.sigmoid(logits),
        )

    (query_unit, key_unit, value_rows, beta_rate), prepare_back = jax.vjp(
        prepare, extended, beta_logit
    )

    def ends(recurrent_associative_matrix, values):
        return span_run(
            recurrent_associative_matrix,
            query_unit,
            key_unit,
            values,
            beta_rate,
            segments,
            previous,
            BLOCK,
        )[1]

    zero_memory = jnp.zeros((heads, head_dim, head_dim), jnp.float32)
    local_end = ends(zero_memory, value_rows)
    current = local_end
    incoming = zero_memory
    for iteration in range(context_size - 1):
        incoming = from_behind(current, "context", 1)
        if iteration + 2 < context_size:
            current = ends(incoming, value_rows)

    def attend(query_rows, keys_unit, values, rates, recurrent_associative_matrix):
        return span_run(
            recurrent_associative_matrix,
            query_rows,
            keys_unit,
            values,
            rates,
            segments,
            previous,
            BLOCK,
        )

    (attended, memory_out), attend_back = jax.vjp(
        attend, query_unit, key_unit, value_rows, beta_rate, incoming
    )
    head_out, head_back = jax.vjp(
        lambda values: rms_scale(values, head_norm_gain).reshape(span, heads * head_dim), attended
    )
    head_low = head_out.astype(jnp.bfloat16)
    branch_sum, low_o_sum = tensor_total(
        (matmul(head_low, gathered_out), matmul(head_low, projection_input_maps))
    )
    low_o = low_o_sum.astype(jnp.bfloat16)
    middle = inputs + branch_sum + matmul(low_o, projection_output_maps)
    normed_ffn, norm_ffn_back = jax.vjp(
        lambda values: rms_scale(values, feedforward_norm_gain), middle
    )
    normed_ffn_low = normed_ffn.astype(jnp.bfloat16)
    low_ffn = jnp.einsum(
        "td,pdr->ptr", normed_ffn_low, feedforward_input_maps, preferred_element_type=jnp.float32
    ).astype(jnp.bfloat16)
    gate_act = matmul(normed_ffn_low, gathered_gate) + matmul(
        low_ffn[0], feedforward_output_maps[0]
    )
    up_act = matmul(normed_ffn_low, gathered_up) + matmul(low_ffn[1], feedforward_output_maps[1])
    hidden, swiglu_back = jax.vjp(lambda gates, ups: jax.nn.silu(gates) * ups, gate_act, up_act)
    hidden_low = hidden.astype(jnp.bfloat16)
    down_sum, low_down_sum = tensor_total(
        (matmul(hidden_low, gathered_down), matmul(hidden_low, down_input_maps))
    )
    low_down = low_down_sum.astype(jnp.bfloat16)
    block_out = (middle + down_sum + matmul(low_down, down_output_maps)).astype(jnp.bfloat16)
    gathered_query, gathered_key, gathered_value, gathered_beta, gathered_out = (
        lax.all_gather(query_weight, ("weights", "context"), axis=0, tiled=True),
        lax.all_gather(key_weight, ("weights", "context"), axis=0, tiled=True),
        lax.all_gather(value_weight, ("weights", "context"), axis=0, tiled=True),
        lax.all_gather(strength_weight, ("weights", "context"), axis=0, tiled=True),
        lax.all_gather(mixer_output_weight, ("weights", "context"), axis=1, tiled=True),
    )
    gathered_gate, gathered_up, gathered_down = (
        lax.all_gather(gate_weight, ("weights", "context"), axis=0, tiled=True),
        lax.all_gather(up_weight, ("weights", "context"), axis=0, tiled=True),
        lax.all_gather(down_weight, ("weights", "context"), axis=1, tiled=True),
    )
    grad_down_out = matmul(low_down.T, cotangent)
    grad_low_down = matmul(cotangent, down_output_maps.T).astype(jnp.bfloat16)
    grad_down_in = matmul(hidden_low.T, grad_low_down)
    grad_hidden = matmul(cotangent, gathered_down.T) + matmul(grad_low_down, down_input_maps.T)
    grad_gate, grad_up = swiglu_back(grad_hidden)
    grad_gate_low = grad_gate.astype(jnp.bfloat16)
    grad_up_low = grad_up.astype(jnp.bfloat16)
    grad_ffn_out = jnp.stack(
        [matmul(low_ffn[0].T, grad_gate_low), matmul(low_ffn[1].T, grad_up_low)]
    )
    normed_ffn_part = matmul(grad_gate_low, gathered_gate.T) + matmul(grad_up_low, gathered_up.T)
    low_ffn_part = jnp.stack(
        [
            matmul(grad_gate_low, feedforward_output_maps[0].T),
            matmul(grad_up_low, feedforward_output_maps[1].T),
        ]
    )
    normed_ffn_sum, low_ffn_sum = tensor_total((normed_ffn_part, low_ffn_part))
    grad_low_ffn = low_ffn_sum.astype(jnp.bfloat16)
    grad_normed_ffn = normed_ffn_sum + jnp.einsum(
        "ptr,pdr->td", grad_low_ffn, feedforward_input_maps, preferred_element_type=jnp.float32
    )
    grad_ffn_in = jnp.einsum(
        "td,ptr->pdr", normed_ffn_low, grad_low_ffn, preferred_element_type=jnp.float32
    )
    grad_middle = cotangent.astype(jnp.float32) + norm_ffn_back(grad_normed_ffn)[0]
    grad_attn_low = grad_middle.astype(jnp.bfloat16)
    grad_o_out = matmul(low_o.T, grad_attn_low)
    grad_low_o = matmul(grad_attn_low, projection_output_maps.T).astype(jnp.bfloat16)
    grad_o_in = matmul(head_low.T, grad_low_o)
    grad_head_out = matmul(grad_attn_low, gathered_out.T) + matmul(
        grad_low_o, projection_input_maps.T
    )
    grad_attended = head_back(grad_head_out)[0]
    own_grad = attend_back((grad_attended, zero_memory))[4]
    unused_end, linear_back = jax.vjp(
        lambda recurrent_associative_matrix: ends(recurrent_associative_matrix, value_rows),
        incoming,
    )
    current_grad = own_grad
    received = zero_memory
    for iteration in range(context_size - 1):
        received = from_behind(current_grad.astype(jnp.bfloat16), "context", -1).astype(
            current_grad.dtype
        )
        if iteration + 2 < context_size:
            current_grad = own_grad + linear_back(received)[0]
    grad_query, grad_key, grad_value, grad_beta, unused_grad = attend_back(
        (grad_attended, received)
    )
    grad_extended, grad_logit = prepare_back((grad_query, grad_key, grad_value, grad_beta))
    returned = from_behind(grad_extended[: taps - 1], "context", -1)
    grad_projected = grad_extended[taps - 1 :].at[span - (taps - 1) :].add(returned)
    grad_projected_low = grad_projected.astype(jnp.bfloat16)
    grad_logit_low = grad_logit.astype(jnp.bfloat16)
    width = projected.shape[1] // 3
    columns = [grad_projected_low[:, part * width : (part + 1) * width] for part in range(3)]
    grad_qkv_out = jnp.stack([matmul(low_attn[part].T, columns[part]) for part in range(3)])
    grad_beta_out = matmul(low_attn[3].T, grad_logit_low)
    normed_part = (
        matmul(columns[0], gathered_query.T)
        + matmul(columns[1], gathered_key.T)
        + matmul(columns[2], gathered_value.T)
        + matmul(grad_logit_low, gathered_beta.T)
    )
    low_attn_part = jnp.stack(
        [matmul(columns[part], triple_output_maps[part].T) for part in range(3)]
        + [matmul(grad_logit_low, strength_output_maps.T)]
    )
    normed_sum, low_attn_sum = tensor_total((normed_part, low_attn_part))
    grad_low_attn = low_attn_sum.astype(jnp.bfloat16)
    grad_normed = normed_sum + jnp.einsum(
        "ptr,pdr->td", grad_low_attn, attention_input_maps, preferred_element_type=jnp.float32
    )
    grad_attn_in = jnp.einsum(
        "td,ptr->pdr", normed_low, grad_low_attn, preferred_element_type=jnp.float32
    )
    tokens_grad = grad_middle + norm_attn_back(grad_normed)[0]
    adapter_onehot = (
        jnp.arange(adapter_attention_input.shape[1], dtype=jnp.int32) == chosen_adapter
    ).astype(jnp.float32)
    totals = (
        lax.psum(
            (adapter_onehot[None, :, None, None] * grad_attn_in[:, None]).astype(jnp.bfloat16),
            ("weights", "context"),
        ).astype(jnp.float32),
        lax.psum(
            (adapter_onehot[None, :, None, None] * grad_qkv_out[:, None]).astype(jnp.bfloat16),
            ("weights", "context"),
        ).astype(jnp.float32),
        lax.psum(
            (adapter_onehot[:, None, None] * grad_beta_out[None]).astype(jnp.bfloat16),
            ("weights", "context"),
        ).astype(jnp.float32),
        lax.psum(
            (adapter_onehot[:, None, None] * grad_o_in[None]).astype(jnp.bfloat16),
            ("weights", "context"),
        ).astype(jnp.float32),
        lax.psum(
            (adapter_onehot[:, None, None] * grad_o_out[None]).astype(jnp.bfloat16),
            ("weights", "context"),
        ).astype(jnp.float32),
        lax.psum(
            (adapter_onehot[None, :, None, None] * grad_ffn_in[:, None]).astype(jnp.bfloat16),
            ("weights", "context"),
        ).astype(jnp.float32),
        lax.psum(
            (adapter_onehot[None, :, None, None] * grad_ffn_out[:, None]).astype(jnp.bfloat16),
            ("weights", "context"),
        ).astype(jnp.float32),
        lax.psum(
            (adapter_onehot[:, None, None] * grad_down_in[None]).astype(jnp.bfloat16),
            ("weights", "context"),
        ).astype(jnp.float32),
        lax.psum(
            (adapter_onehot[:, None, None] * grad_down_out[None]).astype(jnp.bfloat16),
            ("weights", "context"),
        ).astype(jnp.float32),
    )
    return (
        block_out,
        tokens_grad,
        totals[0],
        totals[1],
        totals[2],
        totals[3],
        totals[4],
        totals[5],
        totals[6],
        totals[7],
        totals[8],
    )


def solution(mesh):
    return jax.shard_map(
        on_device,
        mesh=mesh,
        in_specs=(
            P(("weights", "context"), None),
            P(("weights", "context"), None),
            P("weights", None),
            P("weights"),
            P(),
            P(),
            P(),
            P(None, None, "tensor"),
            P(("weights", "context"), "tensor"),
            P(("weights", "context"), "tensor"),
            P(("weights", "context"), "tensor"),
            P(("weights", "context"), "tensor"),
            P("tensor", ("weights", "context")),
            P(("weights", "context"), "tensor"),
            P(("weights", "context"), "tensor"),
            P("tensor", ("weights", "context")),
            P(),
            P(None, None, None, "tensor"),
            P(None, None, "tensor"),
            P(None, "tensor", None),
            P(),
            P(),
            P(None, None, None, "tensor"),
            P(None, "tensor", None),
            P(),
        ),
        out_specs=(
            P(("weights", "context"), None),
            P(("weights", "context"), None),
            P(),
            P(None, None, None, "tensor"),
            P(None, None, "tensor"),
            P(None, "tensor", None),
            P(),
            P(),
            P(None, None, None, "tensor"),
            P(None, "tensor", None),
            P(),
        ),
        check_vma=False,
    )
```

profile of v0, /device:TPU:28, one launch (start us, length us, event | category | flops | bytes accessed | tf_op | source)
XLA Modules:
  0.0 1793.6 jit_solution(17084636816840174650)
XLA Ops:
  10.1 39.1 %all-gather = bf16[32,64,4]{1,2,0:T(4,128)(2,1)S(1)} all-gather(bf16[1,64,4]{1,2,0:T(4,128)(2,1)} %bitcast.832), channel_id=1, replica_groups=mesh['weights'=8,'context'=4,'tensor'=4] {'weights','context'}, dimensions={0}, use_global_device_ids=true | all-gather | bytes 16896 | tf_op jit(solution)/shard_map/all_gather | solution.py:174
  59.2 3.6 fusion.270
  63.9 37.2 %all-gather.11.cloned.1.call-done = bf16[2048,512]{1,0:T(8,128)(2,1)} async-done(((bf16[64,512]{1,0:T(8,128)(2,1)}), bf16[2048,512]{1,0:T(8,128)(2,1)}) %all-gather.11.cloned.1.call-update) | async-done | bytes 2097168 | tf_op jit(solution)/shard_map/all_gather | solution.py:172
  101.2 3.6 fusion.267
  106.8 39.9 %all-gather.13.cloned.1.call-done = bf16[2048,512]{1,0:T(8,128)(2,1)} async-done(((bf16[64,512]{1,0:T(8,128)(2,1)}), bf16[2048,512]{1,0:T(8,128)(2,1)}) %all-gather.13.cloned.1.call-update) | async-done | bytes 2097168 | tf_op jit(solution)/shard_map/all_gather | solution.py:173
  146.7 3.7 fusion.265
  155.6 3.5 collective-permute-start
  166.6 5.3 fusion.111
  181.9 158.7 %custom-call.12 = f32[8,4,1,64,64]{3,4,2,1,0:T(8,128)} custom-call(f32[8,4,1,64,64]{4,3,2,1,0:T(8,128)} %add_bitcast_fusion), custom_call_target="InvertDiagBlocksLowerTriangular" | custom-call | tf_op jit(solution)/shard_map/vmap(jit(_solve_triangular))/vmap()/triangular_solve/custom-call.1 | solution.py:45
  340.5 4.3 fusion.156
  347.5 4.6 fusion.148
  352.1 46.0 %while.118 = (s32[]{:T(128)}, f32[4,128,128]{2,1,0:T(8,128)S(1)}, s32[8,64]{1,0:T(8,128)S(1)}, s32[8]{0:T(128)S(1)}, f32[8,64,4,128]{3,1,2,0:T(8,128)S(1)}, /*in...) while((s32[]{:T(128)}, f32[4,128,128]{2,1,0:T(8,128)S(1)}, ...), condition=%wide.region_3.5_spmd.clone, body=%wide.region_2.4_spmd.clone.sunk | while | flops 101024000 | bytes 1445016 | solution.py:113
  407.4 59.5 %while.112 = (s32[]{:T(128)}, f32[4,128,128]{2,1,0:T(8,128)}, s32[8,64]{1,0:T(8,128)S(1)}, s32[8]{0:T(128)S(1)}, f32[8,64,4,128]{3,1,2,0:T(8,128)S(1)}, /*index=...) while((s32[]{:T(128)}, f32[4,128,128]{2,1,0:T(8,128)}, s32[8,64]{1,0:T(8,128)S(1)}, ...), condition=%wide.region_5.7_spmd, body=%wide.region_4.6_spmd.sunk | while | flops 100892928 | bytes 1444997 | solution.py:113
  471.8 3.6 collective-permute-done.2
  475.4 46.1 %while.113 = (s32[]{:T(128)}, f32[4,128,128]{2,1,0:T(8,128)S(1)}, s32[8,64]{1,0:T(8,128)S(1)}, s32[8]{0:T(128)S(1)}, f32[8,64,4,128]{3,1,2,0:T(8,128)S(1)}, /*in...) while((s32[]{:T(128)}, f32[4,128,128]{2,1,0:T(8,128)S(1)}, s32[8,64]{1,0:T(8,128)S(1)}, ...), condition=%wide.region_7.9_spmd, body=%wide.region_6.8_spmd.sunk | while | flops 100892928 | bytes 1444997 | solution.py:113
  531.8 80.0 %while.117 = (s32[]{:T(128)}, f32[4,128,128]{2,1,0:T(8,128)S(1)}, f32[8,64,4,128]{3,1,2,0:T(8,128)}, f32[8,4,128,128]{3,2,1,0:T(8,128)}, s32[8,64]{1,0:T(8,128)S...) while((s32[]{:T(128)}, f32[4,128,128]{2,1,0:T(8,128)S(1)}, ...), condition=%wide.region_10.12_spmd.clone, body=%wide.region_9.11_spmd.clone.sunk | while | flops 201654528 | bytes 3332253 | solution.py:113
  619.4 5.1 fusion.279
  631.9 14.9 psum.120
  646.8 68.9 %all-reduce.17.cloned.1.call-done = f32[512,2048]{1,0:T(8,128)} async-done(((f32[512,2048]{1,0:T(8,128)}), f32[512,2048]{1,0:T(8,128)}) %all-reduce.17.cloned.1.call-update) | async-done | bytes 4194320 | tf_op jit(solution)/shard_map/psum | solution.py:134
  715.7 3.8 multiply_reduce_fusion.1
  724.5 42.4 %all-gather.19.cloned.1.call-done = bf16[2048,1408]{1,0:T(8,128)(2,1)} async-done(((bf16[64,1408]{1,0:T(8,128)(2,1)}), bf16[2048,1408]{1,0:T(8,128)(2,1)}) %all-gather.19.cloned.1.call-update) | async-done | bytes 5767184 | tf_op jit(solution)/shard_map/all_gather | solution.py:179
  766.9 6.4 fusion.281
  776.3 40.6 %all-gather.17.cloned.1.call-done = bf16[2048,1408]{1,0:T(8,128)(2,1)} async-done(((bf16[64,1408]{1,0:T(8,128)(2,1)}), bf16[2048,1408]{1,0:T(8,128)(2,1)}) %all-gather.17.cloned.1.call-update) | async-done | bytes 5767184 | tf_op jit(solution)/shard_map/all_gather | solution.py:178
  816.9 6.4 fusion.280
  826.2 40.6 %all-gather.21.cloned.1.call-done = bf16[1408,2048]{0,1:T(8,128)(2,1)} async-done(((bf16[1408,64]{0,1:T(8,128)(2,1)}), bf16[1408,2048]{0,1:T(8,128)(2,1)}) %all-gather.21.cloned.1.call-update) | async-done | bytes 5767184 | tf_op jit(solution)/shard_map/all_gather | solution.py:180
  866.8 6.5 fusion.283
  873.4 3.8 multiply_convert_fusion.2
  877.1 6.5 fusion.284
  883.7 5.0 convolution_add_fusion.16
  894.9 16.7 psum.124
  920.5 60.5 %all-reduce.19.cloned.1.call-done = f32[512,2048]{1,0:T(8,128)} async-done(((f32[512,2048]{1,0:T(8,128)}), f32[512,2048]{1,0:T(8,128)}) %all-reduce.19.cloned.1.call-update) | async-done | bytes 4194320 | tf_op jit(solution)/shard_map/psum | solution.py:134
  980.9 4.5 multiply_reduce_fusion
  1000.9 127.9 %while.119 = (s32[]{:T(128)}, f32[4,128,128]{2,1,0:T(8,128)}, f32[8,64,4,128]{3,1,2,0:T(8,128)}, f32[8,64,4,128]{3,1,2,0:T(8,128)S(1)}, f32[8,4,64,128]{3,2,1,0:...) while((s32[]{:T(128)}, f32[4,128,128]{2,1,0:T(8,128)}, ...), condition=%wide.region_22.24_spmd.clone, body=%wide.region_21.23_spmd.clone.sunk | while | flops 201785600 | bytes 4491707 | solution.py:113
  1136.9 56.6 %while.114 = (s32[]{:T(128)}, f32[4,128,128]{2,1,0:T(8,128)S(1)}, f32[8,64,4,128]{3,1,2,0:T(8,128)S(1)}, f32[8,4,64,128]{3,2,1,0:T(8,128)}, s32[8,64]{1,0:T(8,128)}, /*index=5*/s32[8]{0:T(128)}, s32[]{:T(128)}, s32[]{:T(128)}) while((s32[]{:T(128)}, f32[4,128,128]{2,1,0:T(8,128)S(1)}, f32[8,64,4,128]{3,1,2,0:T(8,128)S(1)}, ...), condition=%wide.region_24.26_spmd, body=%wide.region_23.25_spmd.sunk | while | flops 100892928 | bytes 1836949 | solution.py:113
  1201.3 56.6 %while.115 = (s32[]{:T(128)}, f32[4,128,128]{2,1,0:T(8,128)S(1)}, f32[8,64,4,128]{3,1,2,0:T(8,128)S(1)}, f32[8,4,64,128]{3,2,1,0:T(8,128)}, s32[8,64]{1,0:T(8,128)}, /*index=5*/s32[8]{0:T(128)}, s32[]{:T(128)}, s32[]{:T(128)}) while((s32[]{:T(128)}, f32[4,128,128]{2,1,0:T(8,128)S(1)}, f32[8,64,4,128]{3,1,2,0:T(8,128)S(1)}, ...), condition=%wide.region_26.28_spmd, body=%wide.region_25.27_spmd.sunk | while | flops 100892928 | bytes 1836949 | solution.py:113
  1270.2 138.8 %while.116 = (s32[]{:T(128)}, f32[4,128,128]{2,1,0:T(8,128)S(1)}, f32[8,64,4,128]{3,1,0,2:T(8,128)}, f32[8,64,4,128]{3,1,2,0:T(8,128)}, f32[8,4,64,128]{3,2,1,0:...) while((s32[]{:T(128)}, f32[4,128,128]{2,1,0:T(8,128)S(1)}, ...), condition=%wide.region_28.30_spmd, body=%wide.region_27.29_spmd.sunk | while | flops 478822656 | bytes 8375789 | solution.py:113
  1409.1 3.5 fusion.149
  1431.5 3.6 copy.170
  1435.2 3.7 multiply_multiply_fusion.2
  1443.6 4.5 pad_add_fusion
  1458.6 4.8 scatter-add.4
  1471.1 17.3 all-reduce.24
  1497.9 7.8 fusion.282
  1514.5 62.3 %psum.129 = bf16[8,16,4]{1,2,0:T(4,128)(2,1)S(1)} all-reduce(bf16[8,16,4]{1,2,0:T(4,128)(2,1)S(1)} %multiply_convert_fusion.12), channel_id=1, replica_groups=mesh['weights'=8,'context'=4,'tensor'=4] {'weights','context'}, use_global_device_ids=true, to_apply=%region_39.42 | all-reduce | flops 512 | bytes 2048 | tf_op jit(solution)/shard_map/psum | solution.py:413
  1577.4 36.4 %all-reduce.23.cloned.1.call-done = (bf16[4,8,2048,16]{2,3,1,0:T(8,128)(2,1)}, bf16[3,8,16,512]{3,2,1,0:T(8,128)(2,1)}, bf16[8,512,16]{1,2,0:T(8,128)(2,1)}, bf1...) async-done(((bf16[4,8,2048,16]{2,3,1,0:T(8,128)(2,1)}, ...) | async-done | bytes 5799952 | tf_op jit(solution)/shard_map/psum | solution.py:405
  1613.8 4.2 convert_element_type.410
  1625.5 149.5 %all-reduce.21.cloned.1.call-done = (f32[512,2048]{1,0:T(8,128)}, f32[512,2048]{1,0:T(8,128)}) async-done(((f32[512,2048]{1,0:T(8,128)}, f32[512,2048]{1,0:T(8,128)}), (f32[512,2048]{1,0:T(8,128)}, f32[512,2048]{1,0:T(8,128)})) %all-reduce.21.cloned.1.call-update) | async-done | bytes 8388624 | tf_op jit(solution)/shard_map/psum | solution.py:134
  1775.1 4.0 fusion.100
  (1146 shorter events, 832.2 us)
Async XLA Ops:
  7.2 49.4 %copy-start = (bf16[4,8,2048,16]{2,3,1,0:T(8,128)(2,1)S(1)}, bf16[4,8,2048,16]{2,3,1,0:T(8,128)(2,1)}, u32[]{:S(2)}) copy-start(bf16[4,8,2048,16]{2,3,1,0:T(8,128)(2,1)} %param.65) | copy-start | bytes 6291460
  7.2 52.0 %all-gather.9.cloned.1.call-start = ((), (), s32[]{:S(2)}) async-start(), calls=%async_computation | async-start | bytes 2162688 | tf_op jit(solution)/shard_map/all_gather | solution.py:171
  7.9 93.2 %all-gather.11.cloned.1.call-start = ((), (), s32[]{:S(2)}) async-start(), calls=%async_computation.1 | async-start | bytes 2162688 | tf_op jit(solution)/shard_map/all_gather | solution.py:172
  8.7 138.0 %all-gather.13.cloned.1.call-start = ((), (), s32[]{:S(2)}) async-start(), calls=%async_computation.2 | async-start | bytes 2162688 | tf_op jit(solution)/shard_map/all_gather | solution.py:173
  9.4 610.0 %all-gather.15.cloned.1.call-start = ((), (), s32[]{:S(2)}) async-start(), calls=%async_computation.3 | async-start | bytes 2162688 | tf_op jit(solution)/shard_map/all_gather | solution.py:175
  49.3 8.1 copy-start.84
  53.5 93.2 %copy-start.108 = (f32[512]{0:T(512)}, f32[512]{0:T(512)S(1)}, u32[]{:S(2)}) copy-start(f32[512]{0:T(512)S(1)} %fusion.253) | copy-start | bytes 6148
  57.5 92.9 %copy-start.58 = (bf16[4,512,16]{1,2,0:T(8,128)(2,1)}, bf16[4,512,16]{1,2,0:T(8,128)(2,1)S(1)}, u32[]{:S(2)}) copy-start(bf16[4,512,16]{1,2,0:T(8,128)(2,1)S(1)} %fusion.130) | copy-start | bytes 196612
  58.3 101.5 %copy-start.88 = (f32[512,4]{0,1:T(4,128)}, f32[512,4]{0,1:T(4,128)S(1)}, u32[]{:S(2)}) copy-start(f32[512,4]{0,1:T(4,128)S(1)} %fusion.142) | copy-start | bytes 24580
  58.4 121.2 %copy-start.62 = (pred[64,64]{1,0:T(8,128)(4,1)}, pred[64,64]{1,0:T(8,128)(4,1)S(1)}, u32[]{:S(2)}) copy-start(pred[64,64]{1,0:T(8,128)(4,1)S(1)} %get-tuple-element.1332) | copy-start | bytes 12292
  155.6 6.0 collective-permute-start
  352.1 49.8 %copy-start.114 = (f32[128]{0:T(128)S(1)}, f32[128]{0:T(128)}, u32[]{:S(2)}) copy-start(f32[128]{0:T(128)} %param.54) | copy-start | bytes 1540
  398.1 9.3 collective-permute-start.1
  401.4 314.3 %all-reduce.17.cloned.1.call-start = ((), (), s32[]{:S(2)}) async-start(), calls=%async_computation.4 | async-start | bytes 8388608 | tf_op jit(solution)/shard_map/psum | solution.py:134
  466.9 8.6 collective-permute-start.2
  522.3 8.5 collective-permute-start.3
  616.3 8.2 copy-start.60
  616.4 12.6 copy-start.54
  624.5 142.4 %all-gather.19.cloned.1.call-start = ((), (), s32[]{:S(2)}) async-start(), calls=%async_computation.6 | async-start | bytes 5947392 | tf_op jit(solution)/shard_map/all_gather | solution.py:179
  625.1 191.8 %all-gather.17.cloned.1.call-start = ((), (), s32[]{:S(2)}) async-start(), calls=%async_computation.5 | async-start | bytes 5947392 | tf_op jit(solution)/shard_map/all_gather | solution.py:178
  625.9 241.0 %all-gather.21.cloned.1.call-start = ((), (), s32[]{:S(2)}) async-start(), calls=%async_computation.7 | async-start | bytes 5947392 | tf_op jit(solution)/shard_map/all_gather | solution.py:180
  626.6 354.3 %all-reduce.19.cloned.1.call-start = ((), (), s32[]{:S(2)}) async-start(), calls=%async_computation.8 | async-start | bytes 8388608 | tf_op jit(solution)/shard_map/psum | solution.py:134
  628.9 244.4 %copy-start.83 = (bf16[16,512]{1,0:T(8,128)(2,1)}, bf16[16,512]{1,0:T(8,128)(2,1)S(1)}, u32[]{:S(2)}) copy-start(bf16[16,512]{1,0:T(8,128)(2,1)S(1)} %convolution_convert_fusion.1) | copy-start | bytes 49156
  646.8 72.7 %copy-start.56 = (bf16[512,16]{0,1:T(8,128)(2,1)}, bf16[512,16]{0,1:T(8,128)(2,1)S(1)}, u32[]{:S(2)}) copy-start(bf16[512,16]{0,1:T(8,128)(2,1)S(1)} %psum.120) | copy-start | bytes 49156
  646.8 72.8 %copy-start.86 = (f32[2048]{0:T(1024)S(1)}, f32[2048]{0:T(1024)}, u32[]{:S(2)}) copy-start(f32[2048]{0:T(1024)} %param.55) | copy-start | bytes 24580
  866.8 16.9 slice-start
  873.4 10.3 slice-start.1
  888.7 725.0 %all-reduce.23.cloned.1.call-start = ((), (), s32[]{:S(2)}) async-start(), calls=%async_computation.10 | async-start | bytes 11599872 | tf_op jit(solution)/shard_map/psum | solution.py:405
  915.2 65.8 %copy-start.53 = (bf16[2,512,16]{1,2,0:T(8,128)(2,1)S(1)}, bf16[2,512,16]{1,2,0:T(8,128)(2,1)}, u32[]{:S(2)}) copy-start(bf16[2,512,16]{1,2,0:T(8,128)(2,1)} %psum.124) | copy-start | bytes 98308
  915.2 65.8 %copy-start.87 = (f32[2048]{0:T(1024)S(1)}, f32[2048]{0:T(1024)}, u32[]{:S(2)}) copy-start(f32[2048]{0:T(1024)} %param.55) | copy-start | bytes 24580
  920.5 65.0 %copy-start.105 = (f32[512]{0:T(512)S(1)}, f32[512]{0:T(512)}, u32[]{:S(2)}) copy-start(f32[512]{0:T(512)} %copy-done.104) | copy-start | bytes 6148
  920.5 65.1 %copy-start.101 = (f32[512]{0:T(512)S(1)}, f32[512]{0:T(512)}, u32[]{:S(2)}) copy-start(f32[512]{0:T(512)} %copy-done.100) | copy-start | bytes 6148
  1129.8 7.1 collective-permute-start.4
  1194.5 6.9 collective-permute-start.5
  1258.9 6.9 collective-permute-start.6
  1448.2 7.7 copy-start.106
  1448.5 7.4 collective-permute-start.7
  1456.2 10.9 copy-start.59
  1458.6 12.4 copy-start.90
  1458.6 12.4 copy-start.65
  1463.4 27.0 %copy-start.92 = (f32[8]{0:T(128)S(1)}, f32[8]{0:T(128)}, u32[]{:S(2)}) copy-start(f32[8]{0:T(128)} %compare_convert_fusion.16) | copy-start | bytes 100
  1464.6 26.6 %copy-start.109 = (f32[512]{0:T(512)S(1)}, f32[512]{0:T(512)}, u32[]{:S(2)}) copy-start(f32[512]{0:T(512)} %copy-done.108) | copy-start | bytes 6148
  1464.6 26.6 %copy-start.112 = (f32[2048]{0:T(1024)S(1)}, f32[2048]{0:T(1024)}, u32[]{:S(2)}) copy-start(f32[2048]{0:T(1024)} %param.53) | copy-start | bytes 24580
  1496.6 278.5 %all-reduce.21.cloned.1.call-start = ((), (), s32[]{:S(2)}) async-start(), calls=%async_computation.9 | async-start | bytes 16777216 | tf_op jit(solution)/shard_map/psum | solution.py:134
  1497.9 7.8 copy-start.14
  1497.9 7.8 copy-start.43
  1620.8 154.3 %copy-start.82 = (bf16[4,512,16]{1,2,0:T(8,128)(2,1)S(1)}, bf16[4,512,16]{1,2,0:T(8,128)(2,1)}, u32[]{:S(2)}) copy-start(bf16[4,512,16]{1,2,0:T(8,128)(2,1)} %copy-done.81) | copy-start | bytes 196612
  1620.8 154.3 %copy-start.113 = (f32[2048]{0:T(1024)S(1)}, f32[2048]{0:T(1024)}, u32[]{:S(2)}) copy-start(f32[2048]{0:T(1024)} %param.53) | copy-start | bytes 24580
  (91 other events, 340.3 us)
Sparse Core Ops, SparseCore 0:
  10.3 45.4 all-gather.8
  58.1 43.0 all-gather.10
  103.4 43.2 all-gather.12
  401.5 43.0 all-gather.14
  624.6 90.9 all-reduce.16
  718.0 48.8 all-gather.18
  769.4 47.4 all-gather.16
  819.4 47.4 all-gather.20
  888.9 92.0 all-reduce.18
  1496.7 117.0 all-reduce.22
  1616.5 158.5 all-reduce.20
where the time goes:
time: 1810 us; the launch traced here: 1790 us
  waiting for transfers between devices  538 us (30%)
  matrix products  423 us (23%)
  other arithmetic  335 us (19%)
  local copies, waits for them, and re-layouts  302 us (17%)
  blocking collectives  150 us (8%)
  starting transfers between devices  24.2 us (1%)
    psum x3, waiting for transfers between devices, tensor_total(): return lax.psum((parts[0], parts[1]), 'tensor')  279 us
    another operation x5, other arithmetic, block_solve(): jax.scipy.linalg.solve_triangular(unit_lower, rates * values_head, lower=...  160 us
    dot_general x46, matrix products, matmul(): return jnp.dot(left, right, preferred_element_type=jnp.float32)  121 us
    dot_general x80, matrix products, block_step(): jnp.einsum('iul,ilt->iut', weighted_value, recurrent_associative_matrix,...  99.7 us
    squeeze x120, local copies, waits for them, and re-layouts, span_run(): lax.scan(jax.checkpoint(block_step), recurrent_associative_matrix, pieces)  98.6 us
    dot_general x72, matrix products, block_step(): jnp.einsum('ohk,ohz->okz', key_rows * closing_segment_number[None, :, Non...  84.4 us
    psum x1, blocking collectives, on_device(): lax.psum((adapter_onehot[:, None, None] * grad_beta_out[None]).astype(jnp...  62.3 us
    dynamic_slice x64, local copies, waits for them, and re-layouts, span_run(): lax.scan(jax.checkpoint(block_step), recurrent_associative_matrix, pieces)  59.2 us
  transfers between devices with their start and end apart: 19, of which 16 were waited for; matrix products, arithmetic and copies ran while one was open for 17% of the time, Pallas kernels for 0%

commit v1 on v0

v1 whole, which is shorter than its diff:
```python
import functools

import jax
import jax.numpy as jnp
from jax import lax
from jax.experimental import pallas as pl
from jax.experimental.pallas import tpu as pltpu
from jax.sharding import PartitionSpec as P

EPSILON = 1e-06
HALO = 8
CHUNK = 128
LANES = 128
F32 = jnp.float32
BF16 = jnp.bfloat16
VMEM_LIMIT = 48 * 1024 * 1024


def dot_low(left, right, left_dim=1, right_dim=0):
    return lax.dot_general(
        left.astype(BF16),
        right.astype(BF16),
        (((left_dim,), (right_dim,)), ((), ())),
        preferred_element_type=F32,
    )


def split(values):
    high = values.astype(BF16)
    return high, (values - high.astype(F32)).astype(BF16)


def dot_fine(left, right, left_dim=1, right_dim=0):
    left_high, left_low = split(left)
    right_high, right_low = split(right)
    dims = (((left_dim,), (right_dim,)), ((), ()))
    product = functools.partial(lax.dot_general, dimension_numbers=dims, preferred_element_type=F32)
    return product(left_high, right_high) + (
        product(left_high, right_low) + product(left_low, right_high)
    )


def conv_rows(x_ref, columns, taps_ref, seg_ref, span):
    here = seg_ref[HALO : HALO + span, :]
    total = taps_ref[0:1, columns] * x_ref[HALO : HALO + span, columns]
    for tap in range(1, taps_ref.shape[0]):
        same = (seg_ref[HALO - tap : HALO - tap + span, :] == here).astype(F32)
        total = total + taps_ref[tap : tap + 1, columns] * (
            x_ref[HALO - tap : HALO - tap + span, columns] * same
        )
    return total


def inverse_norm(values):
    return lax.rsqrt(jnp.sum(values * values, axis=-1, keepdims=True) + EPSILON)


def head_column(array, head):
    lane = lax.broadcasted_iota(jnp.int32, array.shape, 1)
    return jnp.sum(jnp.where(lane == head, array, 0.0), axis=1, keepdims=True)


def chunk_masks(seg_ref, row_ref, chunk):
    start = HALO + chunk * CHUNK
    column = seg_ref[start : start + CHUNK, :]
    row = row_ref[chunk : chunk + 1, :]
    before = seg_ref[start - 1 : start, :]
    last = seg_ref[start + CHUNK - 1 : start + CHUNK, :]
    same = column == row
    row_ids = lax.broadcasted_iota(jnp.int32, (CHUNK, CHUNK), 0)
    col_ids = lax.broadcasted_iota(jnp.int32, (CHUNK, CHUNK), 1)
    strict = (same & (row_ids > col_ids)).astype(F32)
    causal = (same & (row_ids >= col_ids)).astype(F32)
    running = (column == before).astype(F32)
    closing = (column == last).astype(F32)
    carried = (before == last).astype(F32)
    return strict, causal, running, closing, carried


def unit_lower_inverses(lowers):
    size = lowers[0].shape[0]
    row_ids = lax.broadcasted_iota(jnp.int32, (size, size), 0)
    col_ids = lax.broadcasted_iota(jnp.int32, (size, size), 1)
    identity = (row_ids == col_ids).astype(F32)
    pair = (row_ids >> 1) == (col_ids >> 1)
    inverses = [identity - jnp.where(pair, lower, 0.0) for lower in lowers]
    bits = 2
    while (1 << bits) <= size:
        joined = ((row_ids >> bits) == (col_ids >> bits)) & (
            (row_ids >> (bits - 1)) != (col_ids >> (bits - 1))
        )
        inner = [
            dot_fine(jnp.where(joined, lower, 0.0), inverse)
            for lower, inverse in zip(lowers, inverses)
        ]
        inverses = [
            inverse - dot_fine(inverse, part) for inverse, part in zip(inverses, inner)
        ]
        bits += 1
    return inverses


def delta_local_kernel(
    q_ref, k_ref, v_ref, logit_ref, taps_q, taps_k, taps_v, seg_ref, row_ref,
    qp_ref, op_ref, map_ref, inverse_ref, prefix_ref, *, span, head_dim, group,
):
    chunks = span // CHUNK
    step = pl.program_id(0)
    masks = [chunk_masks(seg_ref, row_ref, chunk) for chunk in range(chunks)]
    rates_all = jax.nn.sigmoid(logit_ref[HALO : HALO + span, :])
    work = []
    for local in range(group):
        columns = slice(local * head_dim, (local + 1) * head_dim)
        queries = jax.nn.silu(conv_rows(q_ref, columns, taps_q, seg_ref, span))
        queries = queries * (inverse_norm(queries) * head_dim**-0.5)
        keys = jax.nn.silu(conv_rows(k_ref, columns, taps_k, seg_ref, span))
        keys = keys * inverse_norm(keys)
        values = jax.nn.silu(conv_rows(v_ref, columns, taps_v, seg_ref, span))
        rates = head_column(rates_all, step * group + local)
        for chunk in range(chunks):
            rows = slice(chunk * CHUNK, (chunk + 1) * CHUNK)
            work.append((local, chunk, queries[rows], keys[rows], values[rows], rates[rows]))
    lowers = [
        dot_fine(keys, keys, 1, 1) * (rates * masks[chunk][0])
        for _, chunk, _, keys, _, rates in work
    ]
    inverses = unit_lower_inverses(lowers)
    prefix = None
    for (local, chunk, queries, keys, values, rates), inverse in zip(work, inverses):
        columns = slice(local * head_dim, (local + 1) * head_dim)
        rows = slice(chunk * CHUNK, (chunk + 1) * CHUNK)
        strict, causal, running, closing, carried = masks[chunk]
        inverse_ref[local, rows, :] = inverse
        solved = dot_fine(inverse, jnp.concatenate([rates * values, rates * keys], axis=1))
        updates = solved[:, :head_dim]
        weighted = running * solved[:, head_dim:]
        both = jnp.concatenate([updates, weighted], axis=1)
        scores = dot_low(queries, keys, 1, 1) * causal
        near = dot_low(scores, both)
        ends = dot_low(closing * keys, both, 0, 0)
        reach = running * queries - near[:, head_dim:]
        if chunk == 0:
            row_ids = lax.broadcasted_iota(jnp.int32, (head_dim, head_dim), 0)
            col_ids = lax.broadcasted_iota(jnp.int32, (head_dim, head_dim), 1)
            identity = (row_ids == col_ids).astype(F32)
            prefix = jnp.concatenate([jnp.zeros((head_dim, head_dim), F32), identity], axis=1)
        prefix_ref[local, chunk * head_dim : (chunk + 1) * head_dim, :] = prefix
        seen = dot_low(reach, prefix)
        op_ref[rows, columns] = near[:, :head_dim] + seen[:, :head_dim]
        qp_ref[rows, columns] = seen[:, head_dim:].astype(BF16)
        moved = carried * prefix - dot_low(ends[:, head_dim:], prefix)
        prefix = jnp.concatenate(
            [moved[:, :head_dim] + ends[:, :head_dim], moved[:, head_dim:]], axis=1
        )
        if chunk == chunks - 1:
            map_ref[local] = prefix.astype(BF16)


def delta_local(projected, taps, seg_column, seg_rows, heads, head_dim, span, group):
    rows = projected.shape[0]
    width = group * head_dim
    steps = heads // group
    third = lambda part: pl.BlockSpec((rows, width), lambda i: (0, part * steps + i))
    tap_third = lambda part: pl.BlockSpec((taps.shape[0], width), lambda i: (0, part * steps + i))
    whole = lambda array: pl.BlockSpec(array.shape, lambda i: (0,) * array.ndim)
    chunks = span // CHUNK
    return pl.pallas_call(
        functools.partial(delta_local_kernel, span=span, head_dim=head_dim, group=group),
        grid=(steps,),
        in_specs=[
            third(0), third(1), third(2),
            pl.BlockSpec((rows, LANES), lambda i: (0, 3 * heads * head_dim // LANES)),
            tap_third(0), tap_third(1), tap_third(2), whole(seg_column), whole(seg_rows),
        ],
        out_specs=[
            pl.BlockSpec((span, width), lambda i: (0, i)),
            pl.BlockSpec((span, width), lambda i: (0, i)),
            pl.BlockSpec((group, head_dim, 2 * head_dim), lambda i: (i, 0, 0)),
            pl.BlockSpec((group, span, CHUNK), lambda i: (i, 0, 0)),
            pl.BlockSpec((group, chunks * head_dim, 2 * head_dim), lambda i: (i, 0, 0)),
        ],
        out_shape=[
            jax.ShapeDtypeStruct((span, heads * head_dim), BF16),
            jax.ShapeDtypeStruct((span, heads * head_dim), F32),
            jax.ShapeDtypeStruct((heads, head_dim, 2 * head_dim), BF16),
            jax.ShapeDtypeStruct((heads, span, CHUNK), F32),
            jax.ShapeDtypeStruct((heads, chunks * head_dim, 2 * head_dim), F32),
        ],
        compiler_params=pltpu.CompilerParams(vmem_limit_bytes=VMEM_LIMIT),
        name="delta_local",
    )(projected, projected, projected, projected, taps, taps, taps, seg_column, seg_rows)


def attend_kernel(op_ref, qp_ref, one_ref, two_ref, three_ref, gain_ref, out_ref, att_ref, state_ref):
    heads, head_dim = one_ref.shape[0], one_ref.shape[1]
    for head in range(heads):
        columns = slice(head * head_dim, (head + 1) * head_dim)
        state = two_ref[head, :, :head_dim].astype(F32) + dot_low(
            two_ref[head, :, head_dim:], three_ref[head]
        )
        state = one_ref[head, :, :head_dim].astype(F32) + dot_low(
            one_ref[head, :, head_dim:], state
        )
        state_ref[head] = state
        attended = op_ref[:, columns] + dot_low(qp_ref[:, columns], state)
        att_ref[:, columns] = attended
        scale = lax.rsqrt(jnp.mean(attended * attended, axis=-1, keepdims=True) + EPSILON)
        out_ref[:, columns] = (attended * scale * gain_ref[...]).astype(BF16)


def attend(op, qp, one, two, three, gain):
    heads, head_dim = one.shape[0], one.shape[1]
    return pl.pallas_call(
        attend_kernel,
        out_shape=[
            jax.ShapeDtypeStruct(op.shape, BF16),
            jax.ShapeDtypeStruct(op.shape, F32),
            jax.ShapeDtypeStruct((heads, head_dim, head_dim), F32),
        ],
        compiler_params=pltpu.CompilerParams(vmem_limit_bytes=VMEM_LIMIT),
        name="attend",
    )(op, qp, one, two, three, gain)


def attend_back_kernel(grad_ref, att_ref, qp_ref, gain_ref, out_ref, own_ref):
    heads, head_dim = own_ref.shape[0], own_ref.shape[1]
    for head in range(heads):
        columns = slice(head * head_dim, (head + 1) * head_dim)
        attended = att_ref[:, columns]
        scale = lax.rsqrt(jnp.mean(attended * attended, axis=-1, keepdims=True) + EPSILON)
        gained = grad_ref[:, columns] * gain_ref[...]
        along = jnp.mean(attended * gained, axis=-1, keepdims=True)
        grad = scale * gained - attended * (scale * scale * scale * along)
        out_ref[:, columns] = grad
        own_ref[head] = dot_low(qp_ref[:, columns], grad, 0, 0).astype(BF16)


def attend_back(grad, attended, qp, gain, heads, head_dim):
    return pl.pallas_call(
        attend_back_kernel,
        out_shape=[
            jax.ShapeDtypeStruct(grad.shape, F32),
            jax.ShapeDtypeStruct((heads, head_dim, head_dim), BF16),
        ],
        compiler_params=pltpu.CompilerParams(vmem_limit_bytes=VMEM_LIMIT),
        name="attend_back",
    )(grad, attended, qp, gain)


def delta_back_kernel(
    q_ref, k_ref, v_ref, logit_ref, taps_q, taps_k, taps_v, seg_ref, row_ref,
    inverse_ref, prefix_ref, state_ref, grad_ref,
    own_one, own_two, own_three, map_one, map_two,
    out_ref, halo_ref, tail_ref, dz_ref, *, span, heads, head_dim, group,
):
    chunks = span // CHUNK
    step = pl.program_id(0)
    features = heads * head_dim
    masks = [chunk_masks(seg_ref, row_ref, chunk) for chunk in range(chunks)]
    rates_all = jax.nn.sigmoid(logit_ref[HALO : HALO + span, :])
    lane = lax.broadcasted_iota(jnp.int32, (CHUNK, LANES), 1)
    dz_ref[0:HALO, :] = jnp.zeros((HALO, head_dim), F32)
    dz_ref[HALO + span :, :] = jnp.zeros((HALO, head_dim), F32)

    @pl.when(step == 0)
    def _():
        out_ref[:, 3 * features :] = jnp.zeros((span, LANES), BF16)

    for local in range(group):
        columns = slice(local * head_dim, (local + 1) * head_dim)
        conv_q = conv_rows(q_ref, columns, taps_q, seg_ref, span)
        conv_k = conv_rows(k_ref, columns, taps_k, seg_ref, span)
        conv_v = conv_rows(v_ref, columns, taps_v, seg_ref, span)
        raw_q = jax.nn.silu(conv_q)
        raw_k = jax.nn.silu(conv_k)
        values_all = jax.nn.silu(conv_v)
        scale_q = inverse_norm(raw_q)
        scale_k = inverse_norm(raw_k)
        queries_all = raw_q * (scale_q * head_dim**-0.5)
        keys_all = raw_k * scale_k
        head = step * group + local
        rates_head = head_column(rates_all, head)
        entry = state_ref[local]
        kept = []
        for chunk in range(chunks):
            rows = slice(chunk * CHUNK, (chunk + 1) * CHUNK)
            strict, causal, running, closing, carried = masks[chunk]
            queries, keys, values = queries_all[rows], keys_all[rows], values_all[rows]
            rates = rates_head[rows]
            inverse = inverse_ref[local, rows, :]
            gram = dot_low(keys, keys, 1, 1)
            solved = dot_fine(inverse, jnp.concatenate([rates * values, rates * keys], axis=1))
            weighted = running * solved[:, head_dim:]
            prefix = prefix_ref[local, chunk * head_dim : (chunk + 1) * head_dim, :]
            state = prefix[:, :head_dim] + dot_low(prefix[:, head_dim:], entry)
            errors = solved[:, :head_dim] - dot_low(weighted, state)
            scores = dot_low(queries, keys, 1, 1) * causal
            grad = grad_ref[rows, columns]
            near = dot_low(scores, grad, 0, 0)
            far = dot_low(running * queries, grad, 0, 0)
            grad_scores = dot_low(grad, errors, 1, 1) * causal
            kept.append((queries, keys, values, rates, inverse, gram, solved, weighted, state,
                         errors, grad, near, far, grad_scores))
        leaving = own_two[local].astype(F32) + dot_low(
            map_two[local, :, head_dim:], own_three[local], 0, 0
        )
        leaving = own_one[local].astype(F32) + dot_low(
            map_one[local, :, head_dim:], leaving, 0, 0
        )
        leavings = [None] * chunks
        grad_errors_all = [None] * chunks
        for chunk in reversed(range(chunks)):
            strict, causal, running, closing, carried = masks[chunk]
            keys, weighted, near, far = (kept[chunk][i] for i in (1, 7, 11, 12))
            leavings[chunk] = leaving
            grad_errors = near + closing * dot_low(keys, leaving)
            grad_errors_all[chunk] = grad_errors
            leaving = carried * leaving + far - dot_low(weighted, grad_errors, 0, 0)
        grads = [[], [], []]
        for chunk in range(chunks):
            rows = slice(chunk * CHUNK, (chunk + 1) * CHUNK)
            strict, causal, running, closing, carried = masks[chunk]
            (queries, keys, values, rates, inverse, gram, solved, weighted, state,
             errors, grad, near, far, grad_scores) = kept[chunk]
            grad_errors, leaving = grad_errors_all[chunk], leavings[chunk]
            grad_queries = running * dot_low(grad, state, 1, 1) + dot_low(grad_scores, keys)
            grad_keys = dot_low(grad_scores, queries, 0, 0) + closing * dot_low(
                errors, leaving, 1, 1
            )
            grad_weighted = -running * dot_low(grad_errors, state, 1, 1)
            grad_right = dot_fine(
                inverse, jnp.concatenate([grad_errors, grad_weighted], axis=1), 0, 0
            )
            right_v, right_k = grad_right[:, :head_dim], grad_right[:, head_dim:]
            grad_lower = -dot_low(grad_right, solved, 1, 1) * strict
            grad_rates = (
                jnp.sum(right_v * values, axis=1, keepdims=True)
                + jnp.sum(right_k * keys, axis=1, keepdims=True)
                + jnp.sum(grad_lower * gram, axis=1, keepdims=True)
            )
            grad_gram = rates * grad_lower
            grad_keys = (
                grad_keys
                + rates * right_k
                + dot_low(grad_gram, keys)
                + dot_low(grad_gram, keys, 0, 0)
            )
            grad_logit = grad_rates * rates * (1.0 - rates)
            previous = out_ref[rows, 3 * features :].astype(F32)
            out_ref[rows, 3 * features :] = jnp.where(lane == head, grad_logit, previous).astype(BF16)
            grads[0].append(grad_queries)
            grads[1].append(grad_keys)
            grads[2].append(rates * right_v)
        here = seg_ref[0 : HALO + span, :]
        for part, (conv, raw, scale, taps) in enumerate(
            ((conv_q, raw_q, scale_q, taps_q), (conv_k, raw_k, scale_k, taps_k), (conv_v, None, None, taps_v))
        ):
            grad = jnp.concatenate(grads[part], axis=0)
            if part < 2:
                if part == 0:
                    grad = grad * head_dim**-0.5
                unit = raw * scale
                grad = scale * (grad - unit * jnp.sum(unit * grad, axis=-1, keepdims=True))
            sig = jax.nn.sigmoid(conv)
            dz_ref[HALO : HALO + span, :] = grad * (sig * (1.0 + conv * (1.0 - sig)))
            total = taps[0:1, columns] * dz_ref[0 : HALO + span, :]
            for tap in range(1, taps.shape[0]):
                same = (seg_ref[tap : tap + HALO + span, :] == here).astype(F32)
                total = total + taps[tap : tap + 1, columns] * (
                    dz_ref[tap : tap + HALO + span, :] * same
                )
            place = pl.ds(pl.multiple_of(part * features + head * head_dim, LANES), head_dim)
            halo_ref[:, place] = total[:HALO]
            tail_ref[:, place] = total[span:]
            out_ref[:, place] = total[HALO:].astype(BF16)


def delta_back(
    projected, taps, seg_column, seg_rows, inverse, prefix, state, grad,
    owns, maps, heads, head_dim, span, group,
):
    rows = projected.shape[0]
    width = group * head_dim
    steps = heads // group
    chunks = span // CHUNK
    third = lambda part: pl.BlockSpec((rows, width), lambda i: (0, part * steps + i))
    tap_third = lambda part: pl.BlockSpec((taps.shape[0], width), lambda i: (0, part * steps + i))
    whole = lambda array: pl.BlockSpec(array.shape, lambda i: (0,) * array.ndim)
    by_head = lambda array: pl.BlockSpec((group,) + array.shape[1:], lambda i: (i, 0, 0))
    total = 3 * heads * head_dim
    return pl.pallas_call(
        functools.partial(
            delta_back_kernel, span=span, heads=heads, head_dim=head_dim, group=group
        ),
        grid=(steps,),
        in_specs=[
            third(0), third(1), third(2),
            pl.BlockSpec((rows, LANES), lambda i: (0, total // LANES)),
            tap_third(0), tap_third(1), tap_third(2), whole(seg_column), whole(seg_rows),
            by_head(inverse), by_head(prefix), by_head(state),
            pl.BlockSpec((span, width), lambda i: (0, i)),
            by_head(owns[0]), by_head(owns[1]), by_head(owns[2]),
            by_head(maps[0]), by_head(maps[1]),
        ],
        out_specs=[
            pl.BlockSpec((span, total + LANES), lambda i: (0, 0)),
            pl.BlockSpec((HALO, total), lambda i: (0, 0)),
            pl.BlockSpec((HALO, total), lambda i: (0, 0)),
        ],
        out_shape=[
            jax.ShapeDtypeStruct((span, total + LANES), BF16),
            jax.ShapeDtypeStruct((HALO, total), F32),
            jax.ShapeDtypeStruct((HALO, total), F32),
        ],
        scratch_shapes=[pltpu.VMEM((span + 2 * HALO, head_dim), F32)],
        compiler_params=pltpu.CompilerParams(vmem_limit_bytes=VMEM_LIMIT),
        name="delta_back",
    )(
        projected, projected, projected, projected, taps, taps, taps, seg_column, seg_rows,
        inverse, prefix, state, grad, *owns, *maps,
    )


def shifted(block, axis, distance, wrap=True):
    size = lax.axis_size(axis)
    if wrap:
        route = [(i, (i + distance) % size) for i in range(size)]
    else:
        route = [(i, i + distance) for i in range(size) if 0 <= i + distance < size]
    return lax.ppermute(block, axis, route)


def order_of(size):
    return sorted(range(1, size), key=lambda k: -min(k, size - k))


def sum_to_owners(parts, axis):
    size = len(parts)
    received = {k: shifted(parts[k].astype(BF16), axis, k) for k in order_of(size)}
    total = parts[0].astype(F32)
    for k in range(1, size):
        total = total + received[k].astype(F32)
    return total


def blocks_of_others(block, axis):
    size = lax.axis_size(axis)
    received = {k: shifted(block, axis, -k) for k in order_of(size)}
    return [block] + [received[k] for k in range(1, size)]


def paired_sum(block, axis):
    blocks = [part.astype(F32) for part in blocks_of_others(block, axis)]
    half = len(blocks) // 2
    while half:
        blocks = [blocks[i] + blocks[i + half] for i in range(half)]
        half //= 2
    return blocks[0]


def dot(left, right):
    return jnp.dot(left, right, preferred_element_type=F32)


def dot_nt(left, right):
    return lax.dot_general(left, right, (((1,), (1,)), ((), ())), preferred_element_type=F32)


def dot_tn(left, right):
    return lax.dot_general(left, right, (((0,), (0,)), ((), ())), preferred_element_type=F32)


def rms_scale(values, gain):
    return values * lax.rsqrt(jnp.mean(values * values, axis=-1, keepdims=True) + EPSILON) * gain


def rms_back(values, gain, grad):
    scale = lax.rsqrt(jnp.mean(values * values, axis=-1, keepdims=True) + EPSILON)
    gained = gain * grad
    return scale * gained - values * (scale**3) * jnp.mean(values * gained, axis=-1, keepdims=True)


def pad_columns(array, width):
    return jnp.pad(array, ((0, 0), (0, width - array.shape[1])))


def pad_rows(array, height):
    return jnp.pad(array, ((0, height - array.shape[0]), (0, 0)))


def on_device(
    tokens,
    cotangent,
    token_document_ids,
    sequence_adapter_index,
    mixer_norm_gain,
    head_norm_gain,
    feedforward_norm_gain,
    short_filter_kernels,
    query_weight,
    key_weight,
    value_weight,
    strength_weight,
    mixer_output_weight,
    gate_weight,
    up_weight,
    down_weight,
    adapter_attention_input,
    adapter_triple_output,
    adapter_strength_output,
    adapter_projection_input,
    adapter_projection_output,
    adapter_feedforward_input,
    adapter_feedforward_output,
    adapter_down_input,
    adapter_down_output,
):
    span, model = tokens.shape
    head_dim = head_norm_gain.shape[0]
    taps = short_filter_kernels.shape[1]
    heads = strength_weight.shape[1]
    features = heads * head_dim
    hidden_units = gate_weight.shape[1]
    adapters = adapter_attention_input.shape[1]
    rank = adapter_attention_input.shape[3]
    owners = lax.axis_size("tensor")
    place = lax.axis_index("tensor")
    position = lax.axis_index("context")
    share = span // owners
    everyone = ("weights", "context")

    def chunk_at(array, k):
        start = lax.rem(place + k, owners) * share
        return lax.dynamic_slice_in_dim(array, start, share, axis=0)

    mixer_pack = jnp.concatenate(
        [query_weight, key_weight, value_weight, pad_columns(strength_weight, LANES),
         mixer_output_weight.T], axis=1
    )
    ffn_pack = jnp.concatenate([gate_weight, up_weight, down_weight.T], axis=1)
    mixer_all = lax.all_gather(mixer_pack, everyone, axis=0, tiled=True)
    ffn_all = lax.all_gather(ffn_pack, everyone, axis=0, tiled=True)
    triple = 3 * features + LANES
    weight_in = mixer_all[:, :triple]
    weight_out = mixer_all[:, triple:]

    chosen = sequence_adapter_index[0]
    take = lambda table, axis: lax.dynamic_index_in_dim(table, chosen, axis, keepdims=False)
    attention_in = jnp.swapaxes(take(adapter_attention_input, 1), 1, 2).reshape(4 * rank, model)
    triple_out = take(adapter_triple_output, 1)
    strength_out = take(adapter_strength_output, 0)
    projection_in = jnp.swapaxes(take(adapter_projection_input, 0), 0, 1)
    projection_out = take(adapter_projection_output, 0)
    feedforward_in = jnp.swapaxes(take(adapter_feedforward_input, 1), 1, 2).reshape(2 * rank, model)
    feedforward_out = take(adapter_feedforward_output, 1)
    down_in = jnp.swapaxes(take(adapter_down_input, 0), 0, 1)
    down_out = take(adapter_down_output, 0)
    low_in = jnp.concatenate(
        [
            jnp.pad(triple_out[part], ((0, 0), (part * features, (2 - part) * features + LANES)))
            for part in range(3)
        ]
        + [jnp.pad(strength_out, ((0, 0), (3 * features, LANES - heads)))],
        axis=0,
    )

    padded_ids = jnp.concatenate(
        [jnp.full((HALO,), -1, jnp.int32), token_document_ids[0], jnp.full((HALO,), -2, jnp.int32)]
    )
    window = lax.dynamic_slice_in_dim(padded_ids, position * span, span + 2 * HALO)
    window = jnp.where(
        jnp.arange(span + 2 * HALO) < span + HALO, window, jnp.full_like(window, -2)
    )
    seg_column = window[:, None]
    seg_rows = window[HALO : HALO + span].reshape(span // CHUNK, CHUNK)
    kernels = jnp.transpose(short_filter_kernels, (1, 0, 2)).reshape(taps, -1)

    edge = shifted(tokens[span - HALO :], "context", 1, wrap=False)
    inputs_ext = jnp.concatenate([edge, tokens], axis=0).astype(F32)
    normed_ext = rms_scale(inputs_ext, mixer_norm_gain).astype(BF16)
    low_ext = dot_nt(normed_ext, attention_in).astype(BF16)
    projected = dot(normed_ext, weight_in) + dot(low_ext, low_in)
    normed = normed_ext[HALO:]
    low_attn = low_ext[HALO:]

    group = 1
    qp, op, maps, inverse, prefix = delta_local(
        projected, kernels, seg_column, seg_rows, heads, head_dim, span, group
    )
    three = shifted(maps[:, :, :head_dim], "context", 3, wrap=False)
    two = shifted(maps, "context", 2, wrap=False)
    one = shifted(maps, "context", 1, wrap=False)
    map_two = shifted(maps, "context", -2, wrap=False)
    map_one = shifted(maps, "context", -1, wrap=False)
    gain_row = head_norm_gain[None, :]
    head_low, attended, state = attend(op, qp, one, two, three, gain_row)

    out_ext = jnp.concatenate([weight_out, pad_rows(projection_in, LANES)], axis=0)
    branch = sum_to_owners(
        [dot_nt(chunk_at(head_low, k), out_ext) for k in range(owners)], "tensor"
    )
    low_o = branch[:, model : model + rank].astype(BF16)
    inputs_own = chunk_at(tokens, 0).astype(F32)
    middle = inputs_own + branch[:, :model] + dot(low_o, projection_out)
    normed_ffn = rms_scale(middle, feedforward_norm_gain).astype(BF16)
    low_ffn = dot_nt(normed_ffn, feedforward_in).astype(BF16)
    ffn_in = blocks_of_others(
        jnp.concatenate([normed_ffn, pad_columns(low_ffn, LANES)], axis=1), "tensor"
    )

    ffn_low = jnp.concatenate(
        [
            jnp.pad(feedforward_out[0], ((0, 0), (0, hidden_units))),
            jnp.pad(feedforward_out[1], ((0, 0), (hidden_units, 0))),
        ],
        axis=0,
    )
    gate_up_ext = jnp.concatenate([ffn_all[:, : 2 * hidden_units], pad_rows(ffn_low, LANES)], axis=0)
    down_ext = jnp.concatenate([ffn_all[:, 2 * hidden_units :], pad_rows(down_in, LANES)], axis=0)
    cot_own = chunk_at(cotangent, 0)
    low_grad_down = dot_nt(cotangent, down_out).astype(BF16)
    cot_ext = jnp.concatenate([cotangent, pad_columns(low_grad_down, LANES)], axis=1)
    grad_hidden_all = dot(cot_ext, down_ext)

    down_parts, back_parts, hidden_blocks, ffn_grads = [None] * owners, [None] * owners, [], []
    grad_down_in = 0.0
    grad_ffn_out = 0.0
    for k in [0, 1, 3, 2] if owners == 4 else range(owners):
        both = dot(ffn_in[k], gate_up_ext)
        gate_act, up_act = both[:, :hidden_units], both[:, hidden_units:]
        sig = jax.nn.sigmoid(gate_act)
        silu = gate_act * sig
        hidden = (silu * up_act).astype(BF16)
        grad_hidden = chunk_at(grad_hidden_all, k)
        grad_gate = (grad_hidden * up_act * (sig * (1.0 + gate_act * (1.0 - sig)))).astype(BF16)
        grad_up = (grad_hidden * silu).astype(BF16)
        grads = jnp.concatenate([grad_gate, grad_up], axis=1)
        back_parts[k] = dot_nt(grads, gate_up_ext)
        down_parts[k] = (hidden, grads)
        grad_down_in = grad_down_in + dot_tn(chunk_at(low_grad_down, k), hidden)
        grad_ffn_out = grad_ffn_out + dot_tn(ffn_in[k][:, model : model + 2 * rank], grads)
    back = sum_to_owners(back_parts, "tensor")
    low_grad_ffn = back[:, model : model + 2 * rank].astype(BF16)
    grad_normed_ffn = back[:, :model] + dot(low_grad_ffn, feedforward_in)
    grad_middle = cot_own.astype(F32) + rms_back(middle, feedforward_norm_gain, grad_normed_ffn)

    grad_attn = grad_middle.astype(BF16)
    low_grad_o = dot_nt(grad_attn, projection_out).astype(BF16)
    grad_blocks = blocks_of_others(
        jnp.concatenate([grad_attn, pad_columns(low_grad_o, LANES)], axis=1), "tensor"
    )
    grad_head = jnp.zeros((span, features), F32)
    grad_o_in = 0.0
    for k in range(owners):
        start = lax.rem(place + k, owners) * share
        grad_head = lax.dynamic_update_slice_in_dim(
            grad_head, dot(grad_blocks[k], out_ext), start, axis=0
        )
        grad_o_in = grad_o_in + dot_tn(
            grad_blocks[k][:, model : model + rank], chunk_at(head_low, k)
        )

    grad_attended, own = attend_back(grad_head, attended, qp, gain_row, heads, head_dim)
    own_three = shifted(own, "context", -3, wrap=False)
    own_two = shifted(own, "context", -2, wrap=False)
    own_one = shifted(own, "context", -1, wrap=False)

    down_sum = sum_to_owners([dot_nt(down_parts[k][0], down_ext) for k in range(owners)], "tensor")
    low_down = down_sum[:, model : model + rank].astype(BF16)
    block_own = (middle + down_sum[:, :model] + dot(low_down, down_out)).astype(BF16)
    block_parts = blocks_of_others(block_own, "tensor")

    def in_place(blocks, kind):
        whole = jnp.zeros((span, model), kind)
        for k in range(owners):
            start = lax.rem(place + k, owners) * share
            whole = lax.dynamic_update_slice_in_dim(whole, blocks[k].astype(kind), start, axis=0)
        return whole

    block_out = in_place(block_parts, BF16)

    def for_owner(items):
        parts = [
            lax.dynamic_index_in_dim(items, lax.rem(place + k, owners), 0, keepdims=False)
            for k in range(owners)
        ]
        return sum_to_owners(parts, "tensor")

    def gathered(block):
        block = paired_sum(block.astype(BF16), "context").astype(BF16)
        return lax.all_gather(block, ("weights", "tensor"), axis=0, tiled=False)

    shared_items = jnp.stack(
        [
            dot_tn(low_o, grad_attn),
            dot_tn(low_grad_ffn[:, :rank], normed_ffn),
            dot_tn(low_grad_ffn[:, rank:], normed_ffn),
            dot_tn(low_down, cot_own),
        ]
    )
    early = gathered(
        jnp.concatenate(
            [
                for_owner(shared_items),
                grad_o_in,
                grad_ffn_out[:rank, :hidden_units],
                grad_ffn_out[rank:, hidden_units:],
                grad_down_in,
            ],
            axis=1,
        )
    )

    grad_projected, halo, tail = delta_back(
        projected, kernels, seg_column, seg_rows, inverse, prefix, state, grad_attended,
        (own_one, own_two, own_three), (map_one, map_two), heads, head_dim, span, group,
    )
    returned = shifted(halo, "context", -1, wrap=False)
    grad_projected = lax.dynamic_update_slice(
        grad_projected, (tail + returned).astype(BF16), (span - HALO, 0)
    )

    low_part = dot_nt(grad_projected, low_in)
    low_grad_attn = paired_sum(low_part.astype(BF16), "tensor").astype(BF16)
    grad_low_in = dot_tn(low_attn, grad_projected)
    normed_sum = sum_to_owners(
        [dot_nt(chunk_at(grad_projected, k), weight_in) for k in range(owners)], "tensor"
    )
    grad_normed = normed_sum + dot(chunk_at(low_grad_attn, 0), attention_in)
    grad_tokens = grad_middle + rms_back(inputs_own, mixer_norm_gain, grad_normed)
    tokens_grad = in_place(blocks_of_others(grad_tokens.astype(BF16), "tensor"), F32)

    attn_items = dot_tn(low_grad_attn, normed)
    attn_item = lax.dynamic_slice_in_dim(attn_items, place * rank, rank, axis=0)
    late = gathered(
        jnp.concatenate(
            [attn_item]
            + [
                grad_low_in[part * rank : (part + 1) * rank, part * features : (part + 1) * features]
                for part in range(3)
            ]
            + [grad_low_in[3 * rank :, 3 * features :]],
            axis=1,
        )
    )

    indices = lax.all_gather(sequence_adapter_index, "weights", axis=0, tiled=True)
    onehot = (
        indices[:, None] == jnp.arange(adapters, dtype=jnp.int32)[None, :]
    ).astype(BF16)
    sequences = indices.shape[0]

    def totals(terms):
        return lax.dot_general(
            onehot, terms, (((0,), (0,)), ((), ())), preferred_element_type=F32
        )

    early = early.reshape(sequences, owners, rank, -1)
    late = late.reshape(sequences, owners, rank, -1)
    early_own = lax.dynamic_index_in_dim(early, place, 1, keepdims=False)
    late_own = lax.dynamic_index_in_dim(late, place, 1, keepdims=False)
    cuts = [model, model + features, model + features + hidden_units,
            model + features + 2 * hidden_units, model + features + 3 * hidden_units]
    flip = lambda array: jnp.swapaxes(array, -1, -2)
    grad_attn_in = jnp.stack([flip(totals(late[:, p, :, :model])) for p in range(4)])
    grad_qkv_out = jnp.stack(
        [
            totals(late_own[:, :, model + p * features : model + (p + 1) * features])
            for p in range(3)
        ]
    )
    grad_beta_out = totals(late_own[:, :, model + 3 * features :])[:, :, :heads]
    grad_o_out = totals(early[:, 0, :, :model])
    grad_ffn_in = jnp.stack([flip(totals(early[:, p, :, :model])) for p in (1, 2)])
    grad_down_out = totals(early[:, 3, :, :model])
    grad_o_in_out = flip(totals(early_own[:, :, cuts[0] : cuts[1]]))
    grad_ffn_out_out = jnp.stack(
        [
            totals(early_own[:, :, cuts[1] : cuts[2]]),
            totals(early_own[:, :, cuts[2] : cuts[3]]),
        ]
    )
    grad_down_in_out = flip(totals(early_own[:, :, cuts[3] : cuts[4]]))
    return (
        block_out,
        tokens_grad,
        grad_attn_in,
        grad_qkv_out,
        grad_beta_out,
        grad_o_in_out,
        grad_o_out,
        grad_ffn_in,
        grad_ffn_out_out,
        grad_down_in_out,
        grad_down_out,
    )


def solution(mesh):
    rows = P(("weights", "context"), None)
    return jax.shard_map(
        on_device,
        mesh=mesh,
        in_specs=(
            rows,
            rows,
            P("weights", None),
            P("weights"),
            P(),
            P(),
            P(),
            P(None, None, "tensor"),
            P(("weights", "context"), "tensor"),
            P(("weights", "context"), "tensor"),
            P(("weights", "context"), "tensor"),
            P(("weights", "context"), "tensor"),
            P("tensor", ("weights", "context")),
            P(("weights", "context"), "tensor"),
            P(("weights", "context"), "tensor"),
            P("tensor", ("weights", "context")),
            P(),
            P(None, None, None, "tensor"),
            P(None, None, "tensor"),
            P(None, "tensor", None),
            P(),
            P(),
            P(None, None, None, "tensor"),
            P(None, "tensor", None),
            P(),
        ),
        out_specs=(
            rows,
            rows,
            P(),
            P(None, None, None, "tensor"),
            P(None, None, "tensor"),
            P(None, "tensor", None),
            P(),
            P(),
            P(None, None, None, "tensor"),
            P(None, "tensor", None),
            P(),
        ),
        check_vma=False,
    )
```

time: 1810 us -> 568 us (0.31)
  the two profiles are of different devices: /device:TPU:28 before, /device:TPU:120 now
where the time goes in v1:
time: 568 us; the launch traced here: 558 us
  waiting for transfers between devices  187 us (33%)
  matrix products  128 us (23%)
  starting transfers between devices  69.7 us (12%)
  local copies, waits for them, and re-layouts  67.8 us (12%)
  Pallas kernels  49.1 us (9%)
  other arithmetic  27.4 us (5%)
  between operations  16.1 us (3%)
  blocking collectives  12.5 us (2%)
    ppermute x46, waiting for transfers between devices, shifted(): return lax.ppermute(block, axis, route)  150 us
    dot_general x21, matrix products, dot_nt(): lax.dot_general(left, right, (((1,), (1,)), ((), ())), preferred_element_...  70.8 us
    ppermute x46, starting transfers between devices, shifted(): return lax.ppermute(block, axis, route)  69.6 us
    dot_general x15, matrix products, dot(): return jnp.dot(left, right, preferred_element_type=F32)  36.9 us
    all_gather x1, waiting for transfers between devices, on_device(): mixer_all = lax.all_gather(mixer_pack, everyone, axis=0, tiled=True)  36.8 us
    unnamed x203, local copies, waits for them, and re-layouts  33.5 us
    pallas_call x1, Pallas kernels, delta_back(): pl.pallas_call(functools.partial(delta_back_kernel, span=span, heads=head...  25.8 us
    pallas_call x1, Pallas kernels, delta_local(): pl.pallas_call(functools.partial(delta_local_kernel, span=span, head_dim=...  20.3 us
  transfers between devices with their start and end apart: 50, of which 29 were waited for; matrix products, arithmetic and copies ran while one was open for 34% of the time, Pallas kernels for 9%

profile of v1, /device:TPU:120, one launch (start us, length us, event | category | flops | bytes accessed | tf_op | source)
XLA Modules:
  0.0 557.7 jit_solution(1461721479458359237)
XLA Ops:
  15.1 3.4 collective-permute-start
  30.5 36.8 %all-gather.7.cloned.1.call-done = bf16[2048,2176]{1,0:T(8,128)(2,1)} async-done(((bf16[64,2176]{1,0:T(8,128)(2,1)}), bf16[2048,2176]{1,0:T(8,128)(2,1)}) %all-gather.7.cloned.1.call-update) | async-done | bytes 8912912 | tf_op jit(solution)/shard_map/all_gather | solution.py:541
  67.4 9.0 %fusion.23.q_ref.k_ref.v_ref.logit_ref = f32[520,1664]{1,0:T(8,128)} fusion(f32[520,1664]{1,0:T(8,128)} %fusion.228, bf16[520,2048]{1,0:T(8,128)(2,1)S(1)} %fusion.8, bf16[2048,2176]{1,0:T(8,128)(2,1)} %all-gather.7.cloned.1.call-done), kind=kOutput, calls=%fused_computation.42 | convolution fusion | flops 3545052160 | bytes 15867904 | tf_op jit(solution)/shard_map/dot_general | solution.py:462
  76.4 20.3 %delta_local.1 = (bf16[512,512]{1,0:T(8,128)(2,1)S(1)}, f32[512,512]{1,0:T(8,128)S(1)}, bf16[4,128,256]{2,1,0:T(8,128)(2,1)}, f32[4,512,128]{2,1,0:T(8,128)S(1)}, f32[4,512,256]{2,1,0:T(8,128)S(1)}) custom-call(f32[520,1664]{1,0:T(8,128)} %fusion.23.q_ref.k_ref.v_ref.logit_ref, f32[520,1664]{1,0:T(8,128)} %fusion.23.q_ref.k_ref.v_ref.logit_ref, ...), custom_call_target="tpu_custom_call" | custom-call | tf_op jit(solution)/shard_map/delta_local/pallas_call | solution.py:167
  100.1 4.8 collective-permute-start.2
  112.5 4.0 collective-permute-done.3.three_ref
  117.2 3.6 collective-permute-done.2.two_ref
  126.2 3.0 collective-permute-start.5
  134.3 6.1 %collective-permute-done.4 = bf16[128,2176]{1,0:T(8,128)(2,1)S(1)} collective-permute-done((bf16[128,2176]{1,0:T(8,128)(2,1)S(1)}, bf16[128,2176]{1,0:T(8,128)(2,1)S(1)}, u32[]{:S(2)}, u32[]{:S(2)}) %collective-permute-start.4) | collective-permute-done | bytes 557088 | tf_op jit(solution)/shard_map/ppermute | solution.py:430
  140.4 3.4 collective-permute-done.5
  143.8 8.7 %collective-permute-done.6 = bf16[128,2176]{1,0:T(8,128)(2,1)S(1)} collective-permute-done((bf16[128,2176]{1,0:T(8,128)(2,1)S(1)}, bf16[128,2176]{1,0:T(8,128)(2,1)S(1)}, u32[]{:S(2)}, u32[]{:S(2)}) %collective-permute-start.6) | collective-permute-done | bytes 557088 | tf_op jit(solution)/shard_map/ppermute | solution.py:430
  162.5 4.3 slice-done
  166.8 8.6 %fusion.1 = bf16[2176,2816]{1,0:T(8,128)(2,1)S(1)} fusion(bf16[32,2816]{1,0:T(8,128)(2,1)S(1)} %copy-done.55, bf16[2048,2816]{1,0:T(8,128)(2,1)S(1)} %slice-done), kind=kLoop, calls=%fused_computation.2 | loop fusion | flops 36765696 | bytes 23969792 | tf_op jit(solution)/shard_map/concatenate | solution.py:618
  175.4 7.4 %slice.261 = bf16[2048,1408]{1,0:T(8,128)(2,1)S(1)} slice(bf16[2048,4224]{1,0:T(8,128)(2,1)} %all-gather.9.cloned.1.call-done), slice={[0:2048], [2816:4224]} | slice | bytes 11534336 | tf_op jit(solution)/shard_map/slice | solution.py:619
  182.9 7.0 %fusion.53 = f32[512,1408]{1,0:T(8,128)S(1)} fusion(bf16[512,16]{1,0:T(8,128)(2,1)S(1)} %copy-done.67, bf16[512,2048]{1,0:T(8,128)(2,1)} %param.26, bf16[16,1408]{1,0:T(8,128)(2,1)S(1)} %dynamic-slice_bitcast_fusion.2, bf16[2048,1408]{1,0:T(8,128)(2,1)S(1)} %slice.261), kind=kOutput, calls=%fused_computation.71 | convolution fusion | flops 3162406912 | bytes 10809344 | tf_op jit(solution)/shard_map/dot_general | solution.py:462
  191.8 3.3 fusion.251
  195.1 2.9 fusion.253
  199.0 2.9 fusion.252
  202.0 3.0 multiply_convert_fusion.8
  205.0 6.1 %convolution_convert_fusion.2 = bf16[128,2176]{1,0:T(8,128)(2,1)} fusion(bf16[2176,2816]{1,0:T(8,128)(2,1)S(1)} %fusion.1, bf16[128,1408]{1,0:T(8,128)(2,1)} %get-tuple-element.85, bf16[128,1408]{1,0:T(8,128)(2,1)} %get-tuple-element.86), kind=kOutput, calls=%fused_computation.21 | convolution fusion | flops 1570390016 | bytes 13533184 | tf_op jit(solution)/shard_map/dot_general | solution.py:466
  211.1 4.8 convolution_convert_fusion.1
  217.4 5.9 %convolution_convert_fusion = bf16[128,2176]{1,0:T(8,128)(2,1)} fusion(bf16[2176,2816]{1,0:T(8,128)(2,1)S(1)} %fusion.1, bf16[128,1408]{1,0:T(8,128)(2,1)} %get-tuple-element.81, bf16[128,1408]{1,0:T(8,128)(2,1)} %get-tuple-element.82), kind=kOutput, calls=%fused_computation.19 | convolution fusion | flops 1570390016 | bytes 13533184 | tf_op jit(solution)/shard_map/dot_general | solution.py:466
  224.9 5.4 convolution_convert_fusion.5
  230.4 5.5 convolution_convert_fusion.3
  235.8 7.5 %collective-permute-done.18 = bf16[128,2176]{1,0:T(8,128)(2,1)S(1)} collective-permute-done((bf16[128,2176]{1,0:T(8,128)(2,1)}, bf16[128,2176]{1,0:T(8,128)(2,1)S(1)}, u32[]{:S(2)}, u32[]{:S(2)}) %collective-permute-start.18) | collective-permute-done | bytes 557088 | tf_op jit(solution)/shard_map/ppermute | solution.py:430
  243.3 8.9 %fusion.250 = (bf16[128,2176]{1,0:T(8,128)(2,1)S(1)}, f32[128,2176]{1,0:T(8,128)S(1)}) fusion(bf16[128,2176]{1,0:T(8,128)(2,1)S(1)} %collective-permute-done.18, bf16[128,2176]{1,0:T(8,128)(2,1)} %collective-permute-done.17, bf16[128,2176]{1,0:T(8,128)(2,1)} %collective-permute-done.16, bf16[2176,2816]{1,0:T(8,128)(2,1)} %copy-done.15, ...), kind=kOutput, calls=%fused_computation.357 | convolution fusion | flops 1572061184 | bytes 16318464 | tf_op jit(solution)/shard_map/dot_general | solution.py:466
  258.8 3.3 collective-permute-start.21
  262.8 22.4 %collective-permute-done.19 = bf16[128,2176]{1,0:T(8,128)(2,1)S(1)} collective-permute-done((bf16[128,2176]{1,0:T(8,128)(2,1)S(1)}, bf16[128,2176]{1,0:T(8,128)(2,1)S(1)}, u32[]{:S(2)}, u32[]{:S(2)}) %collective-permute-start.19) | collective-permute-done | bytes 557088 | tf_op jit(solution)/shard_map/ppermute | solution.py:430
  296.6 3.6 collective-permute-done.23.own_two
  304.8 25.8 %delta_back.1 = (bf16[512,1664]{1,0:T(8,128)(2,1)S(1)}, f32[8,1536]{1,0:T(8,128)S(1)}, f32[8,1536]{1,0:T(8,128)S(1)}) custom-call(f32[520,1664]{1,0:T(8,128)} %fusion.23.q_ref.k_ref.v_ref.logit_ref, f32[520,1664]{1,0:T(8,128)} %fusion.23.q_ref.k_ref.v_ref.logit_ref, f32[520,1664]{1,0:T(8,128)} %fusion.23.q_ref.k_ref.v_ref.logit_ref, ...), custom_call_target="tpu_custom_call" | custom-call | tf_op jit(solution)/shard_map/delta_back/pallas_call | solution.py:391
  332.1 4.3 convolution_convert_fusion.4
  340.7 3.2 collective-permute-start.33
  344.4 9.9 %collective-permute-done.31 = bf16[512,64]{0,1:T(8,128)(2,1)S(1)} collective-permute-done((bf16[512,64]{0,1:T(8,128)(2,1)S(1)}, bf16[512,64]{0,1:T(8,128)(2,1)S(1)}, u32[]{:S(2)}, u32[]{:S(2)}) %collective-permute-start.31) | collective-permute-done | bytes 65568 | tf_op jit(solution)/shard_map/ppermute | solution.py:430
  357.6 3.2 collective-permute-start.38
  373.8 3.9 collective-permute-done.12
  377.6 5.1 convert_add_fusion.2
  400.0 3.1 collective-permute-start.44
  403.1 3.0 collective-permute-done.43
  407.4 2.8 collective-permute-done.45
  412.4 12.5 %all-reduce.13 = s32[8]{0:T(128)S(1)} all-reduce(s32[8]{0:T(128)S(1)} %dynamic-update-slice), channel_id=1, replica_groups=mesh['weights'=8,'context'=4,'tensor'=4] {'weights'}, use_global_device_ids=true, to_apply=%add.13 | all-reduce | flops 8 | bytes 64
  424.9 5.5 fusion.41
  432.3 5.3 fusion.44
  454.1 17.4 %collective-permute-done.30 = bf16[128,2048]{1,0:T(8,128)(2,1)S(1)} collective-permute-done((bf16[128,2048]{1,0:T(8,128)(2,1)S(1)}, bf16[128,2048]{1,0:T(8,128)(2,1)S(1)}, u32[]{:S(2)}, u32[]{:S(2)}) %collective-permute-start.30) | collective-permute-done | bytes 524320 | tf_op jit(solution)/shard_map/ppermute | solution.py:430
  480.5 7.2 %collective-permute-done.13 = bf16[128,2048]{1,0:T(8,128)(2,1)S(1)} collective-permute-done((bf16[128,2048]{1,0:T(8,128)(2,1)S(1)}, bf16[128,2048]{1,0:T(8,128)(2,1)S(1)}, u32[]{:S(2)}, u32[]{:S(2)}) %collective-permute-start.13) | collective-permute-done | bytes 524320 | tf_op jit(solution)/shard_map/ppermute | solution.py:430
  488.5 13.3 %collective-permute-done.14 = bf16[128,2048]{1,0:T(8,128)(2,1)S(1)} collective-permute-done((bf16[128,2048]{1,0:T(8,128)(2,1)S(1)}, bf16[128,2048]{1,0:T(8,128)(2,1)S(1)}, u32[]{:S(2)}, u32[]{:S(2)}) %collective-permute-start.14) | collective-permute-done | bytes 524320 | tf_op jit(solution)/shard_map/ppermute | solution.py:430
  504.8 8.0 %collective-permute-done.34 = bf16[128,2048]{1,0:T(8,128)(2,1)S(1)} collective-permute-done((bf16[128,2048]{1,0:T(8,128)(2,1)S(1)}, bf16[128,2048]{1,0:T(8,128)(2,1)S(1)}, u32[]{:S(2)}, u32[]{:S(2)}) %collective-permute-start.34) | collective-permute-done | bytes 524320 | tf_op jit(solution)/shard_map/ppermute | solution.py:430
  513.9 7.5 %collective-permute-done.35 = bf16[128,2048]{1,0:T(8,128)(2,1)S(1)} collective-permute-done((bf16[128,2048]{1,0:T(8,128)(2,1)S(1)}, bf16[128,2048]{1,0:T(8,128)(2,1)S(1)}, u32[]{:S(2)}, u32[]{:S(2)}) %collective-permute-start.35) | collective-permute-done | bytes 524320 | tf_op jit(solution)/shard_map/ppermute | solution.py:430
  529.9 4.4 copy.79
  (402 shorter events, 180.3 us)
Async XLA Ops:
  7.2 60.2 %all-gather.7.cloned.1.call-start = ((), (), s32[]{:S(2)}) async-start(), calls=%async_computation | async-start | bytes 9191424 | tf_op jit(solution)/shard_map/all_gather | solution.py:541
  12.3 150.2 %all-gather.9.cloned.1.call-start = ((), (), s32[]{:S(2)}) async-start(), calls=%async_computation.1 | async-start | bytes 17842176 | tf_op jit(solution)/shard_map/all_gather | solution.py:542
  14.3 509.2 %all-gather.11.cloned.1.call-start = ((), (), s32[]{:S(2)}) async-start(), calls=%async_computation.2 | async-start | bytes 3919872 | tf_op jit(solution)/shard_map/all_gather | solution.py:691
  15.1 9.8 %collective-permute-start = (bf16[8,2048]{1,0:T(8,128)(2,1)S(1)}, bf16[8,2048]{1,0:T(8,128)(2,1)S(1)}, u32[]{:S(2)}, u32[]{:S(2)}) collective-permute-start(bf16[8,2048]{1,0:T(8,128)(2,1)S(1)} %slice.195), channel_id=1, source_target_pairs={{0,4},{4,8},{8,12},{1,5},{5,9},{9,13},{2,6},{6,10},{10,14},{3,7},{... | collective-permute-start | bytes 98312 | tf_op jit(solution)/shard_map/ppermute | solution.py:430
  98.0 18.5 %collective-permute-start.1 = (bf16[4,128,256]{2,1,0:T(8,128)(2,1)}, bf16[4,128,256]{2,1,0:T(8,128)(2,1)S(1)}, u32[]{:S(2)}, u32[]{:S(2)}) collective-permute-start(bf16[4,128,256]{2,1,0:T(8,128)(2,1)} %get-tuple-element.26), channel_id=1, source_target_pairs={{0,4},{4,8},{8,12},{1,5},{5,9},{9,13},{2,6},{6,10},{10,14},{3,7},{... | collective-permute-start | bytes 786440 | tf_op jit(solution)/shard_map/ppermute | solution.py:430
  100.1 20.7 %collective-permute-start.2 = (bf16[4,128,256]{2,1,0:T(8,128)(2,1)}, bf16[4,128,256]{2,1,0:T(8,128)(2,1)}, u32[]{:S(2)}, u32[]{:S(2)}) collective-permute-start(bf16[4,128,256]{2,1,0:T(8,128)(2,1)} %get-tuple-element.26), channel_id=1, source_target_pairs={{0,8},{4,12},{1,9},{5,13},{2,10},{6,14},{3,11},{7,15},{16,24},{20,... | collective-permute-start | bytes 786440 | tf_op jit(solution)/shard_map/ppermute | solution.py:430
  106.5 10.0 %collective-permute-start.3 = (bf16[4,128,128]{2,1,0:T(8,128)(2,1)}, bf16[4,128,128]{2,1,0:T(8,128)(2,1)S(1)}, u32[]{:S(2)}, u32[]{:S(2)}) collective-permute-start(bf16[4,128,128]{2,1,0:T(8,128)(2,1)} %slice.201), channel_id=1, source_target_pairs={{0,12},{1,13},{2,14},{3,15},{16,28},{17,29},{18,30},{19,31},{32,44... | collective-permute-start | bytes 393224 | tf_op jit(solution)/shard_map/ppermute | solution.py:430
  124.8 15.6 %collective-permute-start.4 = (bf16[128,2176]{1,0:T(8,128)(2,1)S(1)}, bf16[128,2176]{1,0:T(8,128)(2,1)S(1)}, u32[]{:S(2)}, u32[]{:S(2)}) collective-permute-start(bf16[128,2176]{1,0:T(8,128)(2,1)S(1)} %convolution_convert_fusion.8), channel_id=1, source_target_pairs={{0,1},{1,2},{2,3},{3,0},{4,5},{5,6},{6,7},{7,4},{8,9},{9,10},{10,1... | collective-permute-start | bytes 1671176 | tf_op jit(solution)/shard_map/ppermute | solution.py:430
  126.2 17.7 %collective-permute-start.5 = (bf16[128,2176]{1,0:T(8,128)(2,1)S(1)}, bf16[128,2176]{1,0:T(8,128)(2,1)S(1)}, u32[]{:S(2)}, u32[]{:S(2)}) collective-permute-start(bf16[128,2176]{1,0:T(8,128)(2,1)S(1)} %convolution_convert_fusion.7), channel_id=1, source_target_pairs={{0,2},{1,3},{2,0},{3,1},{4,6},{5,7},{6,4},{7,5},{8,10},{9,11},{10,... | collective-permute-start | bytes 1671176 | tf_op jit(solution)/shard_map/ppermute | solution.py:430
  130.0 22.5 %collective-permute-start.6 = (bf16[128,2176]{1,0:T(8,128)(2,1)S(1)}, bf16[128,2176]{1,0:T(8,128)(2,1)S(1)}, u32[]{:S(2)}, u32[]{:S(2)}) collective-permute-start(bf16[128,2176]{1,0:T(8,128)(2,1)S(1)} %convolution_convert_fusion.6), channel_id=1, source_target_pairs={{0,3},{1,0},{2,1},{3,2},{4,7},{5,4},{6,5},{7,6},{8,11},{9,8},{10,9... | collective-permute-start | bytes 1671176 | tf_op jit(solution)/shard_map/ppermute | solution.py:430
  131.5 161.9 %collective-permute-start.25 = (bf16[4,128,256]{2,1,0:T(8,128)(2,1)}, bf16[4,128,256]{2,1,0:T(8,128)(2,1)S(1)}, u32[]{:S(2)}, u32[]{:S(2)}) collective-permute-start(bf16[4,128,256]{2,1,0:T(8,128)(2,1)} %get-tuple-element.26), channel_id=1, source_target_pairs={{4,0},{8,4},{12,8},{5,1},{9,5},{13,9},{6,2},{10,6},{14,10},{7,3},{... | collective-permute-start | bytes 786440 | tf_op jit(solution)/shard_map/ppermute | solution.py:430
  133.0 162.0 %collective-permute-start.26 = (bf16[4,128,256]{2,1,0:T(8,128)(2,1)}, bf16[4,128,256]{2,1,0:T(8,128)(2,1)S(1)}, u32[]{:S(2)}, u32[]{:S(2)}) collective-permute-start(bf16[4,128,256]{2,1,0:T(8,128)(2,1)} %get-tuple-element.26), channel_id=1, source_target_pairs={{8,0},{12,4},{9,1},{13,5},{10,2},{14,6},{11,3},{15,7},{24,16},{28,... | collective-permute-start | bytes 786440 | tf_op jit(solution)/shard_map/ppermute | solution.py:430
  157.6 34.2 %collective-permute-start.7 = (bf16[128,2176]{1,0:T(8,128)(2,1)}, bf16[128,2176]{1,0:T(8,128)(2,1)}, u32[]{:S(2)}, u32[]{:S(2)}) collective-permute-start(bf16[128,2176]{1,0:T(8,128)(2,1)} %fusion.88), channel_id=1, source_target_pairs={{0,3},{1,0},{2,1},{3,2},{4,7},{5,4},{6,5},{7,6},{8,11},{9,8},{10,9... | collective-permute-start | bytes 1671176 | tf_op jit(solution)/shard_map/ppermute | solution.py:430
  158.4 40.6 %collective-permute-start.9 = (bf16[128,2176]{1,0:T(8,128)(2,1)}, bf16[128,2176]{1,0:T(8,128)(2,1)}, u32[]{:S(2)}, u32[]{:S(2)}) collective-permute-start(bf16[128,2176]{1,0:T(8,128)(2,1)} %fusion.88), channel_id=1, source_target_pairs={{0,2},{1,3},{2,0},{3,1},{4,6},{5,7},{6,4},{7,5},{8,10},{9,11},{10,... | collective-permute-start | bytes 1671176 | tf_op jit(solution)/shard_map/ppermute | solution.py:430
  159.9 35.2 %collective-permute-start.11 = (bf16[128,2176]{1,0:T(8,128)(2,1)}, bf16[128,2176]{1,0:T(8,128)(2,1)}, u32[]{:S(2)}, u32[]{:S(2)}) collective-permute-start(bf16[128,2176]{1,0:T(8,128)(2,1)} %fusion.88), channel_id=1, source_target_pairs={{0,1},{1,2},{2,3},{3,0},{4,5},{5,6},{6,7},{7,4},{8,9},{9,10},{10,1... | collective-permute-start | bytes 1671176 | tf_op jit(solution)/shard_map/ppermute | solution.py:430
  211.1 24.7 %collective-permute-start.16 = (bf16[128,2176]{1,0:T(8,128)(2,1)}, bf16[128,2176]{1,0:T(8,128)(2,1)}, u32[]{:S(2)}, u32[]{:S(2)}) collective-permute-start(bf16[128,2176]{1,0:T(8,128)(2,1)} %convolution_convert_fusion.2), channel_id=1, source_target_pairs={{0,1},{1,2},{2,3},{3,0},{4,5},{5,6},{6,7},{7,4},{8,9},{9,10},{10,1... | collective-permute-start | bytes 1671176 | tf_op jit(solution)/shard_map/ppermute | solution.py:430
  215.9 19.9 %collective-permute-start.17 = (bf16[128,2176]{1,0:T(8,128)(2,1)}, bf16[128,2176]{1,0:T(8,128)(2,1)}, u32[]{:S(2)}, u32[]{:S(2)}) collective-permute-start(bf16[128,2176]{1,0:T(8,128)(2,1)} %convolution_convert_fusion.1), channel_id=1, source_target_pairs={{0,2},{1,3},{2,0},{3,1},{4,6},{5,7},{6,4},{7,5},{8,10},{9,11},{10,... | collective-permute-start | bytes 1671176 | tf_op jit(solution)/shard_map/ppermute | solution.py:430
  223.3 20.0 %collective-permute-start.18 = (bf16[128,2176]{1,0:T(8,128)(2,1)}, bf16[128,2176]{1,0:T(8,128)(2,1)S(1)}, u32[]{:S(2)}, u32[]{:S(2)}) collective-permute-start(bf16[128,2176]{1,0:T(8,128)(2,1)} %convolution_convert_fusion), channel_id=1, source_target_pairs={{0,3},{1,0},{2,1},{3,2},{4,7},{5,4},{6,5},{7,6},{8,11},{9,8},{10,9... | collective-permute-start | bytes 1671176 | tf_op jit(solution)/shard_map/ppermute | solution.py:430
  257.0 29.0 %collective-permute-start.20 = (bf16[128,2176]{1,0:T(8,128)(2,1)S(1)}, bf16[128,2176]{1,0:T(8,128)(2,1)S(1)}, u32[]{:S(2)}, u32[]{:S(2)}) collective-permute-start(bf16[128,2176]{1,0:T(8,128)(2,1)S(1)} %fusion.89), channel_id=1, source_target_pairs={{0,2},{1,3},{2,0},{3,1},{4,6},{5,7},{6,4},{7,5},{8,10},{9,11},{10,... | collective-permute-start | bytes 1671176 | tf_op jit(solution)/shard_map/ppermute | solution.py:430
  258.6 26.5 %collective-permute-start.19 = (bf16[128,2176]{1,0:T(8,128)(2,1)S(1)}, bf16[128,2176]{1,0:T(8,128)(2,1)S(1)}, u32[]{:S(2)}, u32[]{:S(2)}) collective-permute-start(bf16[128,2176]{1,0:T(8,128)(2,1)S(1)} %fusion.89), channel_id=1, source_target_pairs={{0,3},{1,0},{2,1},{3,2},{4,7},{5,4},{6,5},{7,6},{8,11},{9,8},{10,9... | collective-permute-start | bytes 1671176 | tf_op jit(solution)/shard_map/ppermute | solution.py:430
  258.8 28.1 %collective-permute-start.21 = (bf16[128,2176]{1,0:T(8,128)(2,1)S(1)}, bf16[128,2176]{1,0:T(8,128)(2,1)S(1)}, u32[]{:S(2)}, u32[]{:S(2)}) collective-permute-start(bf16[128,2176]{1,0:T(8,128)(2,1)S(1)} %fusion.89), channel_id=1, source_target_pairs={{0,1},{1,2},{2,3},{3,0},{4,5},{5,6},{6,7},{7,4},{8,9},{9,10},{10,1... | collective-permute-start | bytes 1671176 | tf_op jit(solution)/shard_map/ppermute | solution.py:430
  289.3 7.3 %collective-permute-start.22 = (bf16[4,128,128]{2,1,0:T(8,128)(2,1)S(1)}, bf16[4,128,128]{2,1,0:T(8,128)(2,1)S(1)}, u32[]{:S(2)}, u32[]{:S(2)}) collective-permute-start(bf16[4,128,128]{2,1,0:T(8,128)(2,1)S(1)} %get-tuple-element.33), channel_id=1, source_target_pairs={{4,0},{8,4},{12,8},{5,1},{9,5},{13,9},{6,2},{10,6},{14,10},{7,3},{... | collective-permute-start | bytes 393224 | tf_op jit(solution)/shard_map/ppermute | solution.py:430
  290.6 9.6 %collective-permute-start.23 = (bf16[4,128,128]{2,1,0:T(8,128)(2,1)S(1)}, bf16[4,128,128]{2,1,0:T(8,128)(2,1)S(1)}, u32[]{:S(2)}, u32[]{:S(2)}) collective-permute-start(bf16[4,128,128]{2,1,0:T(8,128)(2,1)S(1)} %get-tuple-element.33), channel_id=1, source_target_pairs={{8,0},{12,4},{9,1},{13,5},{10,2},{14,6},{11,3},{15,7},{24,16},{28,... | collective-permute-start | bytes 393224 | tf_op jit(solution)/shard_map/ppermute | solution.py:430
  291.9 11.0 %collective-permute-start.24 = (bf16[4,128,128]{2,1,0:T(8,128)(2,1)S(1)}, bf16[4,128,128]{2,1,0:T(8,128)(2,1)S(1)}, u32[]{:S(2)}, u32[]{:S(2)}) collective-permute-start(bf16[4,128,128]{2,1,0:T(8,128)(2,1)S(1)} %get-tuple-element.33), channel_id=1, source_target_pairs={{12,0},{13,1},{14,2},{15,3},{28,16},{29,17},{30,18},{31,19},{44,32... | collective-permute-start | bytes 393224 | tf_op jit(solution)/shard_map/ppermute | solution.py:430
  294.2 79.5 %collective-permute-start.8 = (bf16[128,2176]{1,0:T(8,128)(2,1)}, bf16[128,2176]{1,0:T(8,128)(2,1)}, u32[]{:S(2)}, u32[]{:S(2)}) collective-permute-start(bf16[128,2176]{1,0:T(8,128)(2,1)} %convolution_convert_fusion.5), channel_id=1, source_target_pairs={{0,1},{1,2},{2,3},{3,0},{4,5},{5,6},{6,7},{7,4},{8,9},{9,10},{10,1... | collective-permute-start | bytes 1671176 | tf_op jit(solution)/shard_map/ppermute | solution.py:430
  330.7 7.2 %collective-permute-start.27 = (f32[8,1536]{1,0:T(8,128)S(1)}, f32[8,1536]{1,0:T(8,128)S(1)}, u32[]{:S(2)}, u32[]{:S(2)}) collective-permute-start(f32[8,1536]{1,0:T(8,128)S(1)} %get-tuple-element.36), channel_id=1, source_target_pairs={{4,0},{8,4},{12,8},{5,1},{9,5},{13,9},{6,2},{10,6},{14,10},{7,3},{... | collective-permute-start | bytes 147464 | tf_op jit(solution)/shard_map/ppermute | solution.py:430
  336.4 37.3 %collective-permute-start.10 = (bf16[128,2176]{1,0:T(8,128)(2,1)}, bf16[128,2176]{1,0:T(8,128)(2,1)}, u32[]{:S(2)}, u32[]{:S(2)}) collective-permute-start(bf16[128,2176]{1,0:T(8,128)(2,1)} %convolution_convert_fusion.4), channel_id=1, source_target_pairs={{0,2},{1,3},{2,0},{3,1},{4,6},{5,7},{6,4},{7,5},{8,10},{9,11},{10,... | collective-permute-start | bytes 1671176 | tf_op jit(solution)/shard_map/ppermute | solution.py:430
  338.6 15.8 %collective-permute-start.31 = (bf16[512,64]{0,1:T(8,128)(2,1)S(1)}, bf16[512,64]{0,1:T(8,128)(2,1)S(1)}, u32[]{:S(2)}, u32[]{:S(2)}) collective-permute-start(bf16[512,64]{0,1:T(8,128)(2,1)S(1)} %convolution_convert_fusion.11), channel_id=1, source_target_pairs={{0,2},{1,3},{2,0},{3,1},{4,6},{5,7},{6,4},{7,5},{8,10},{9,11},{10,... | collective-permute-start | bytes 196616 | tf_op jit(solution)/shard_map/ppermute | solution.py:430
  340.7 14.3 %collective-permute-start.32 = (bf16[512,64]{0,1:T(8,128)(2,1)S(1)}, bf16[512,64]{0,1:T(8,128)(2,1)S(1)}, u32[]{:S(2)}, u32[]{:S(2)}) collective-permute-start(bf16[512,64]{0,1:T(8,128)(2,1)S(1)} %convolution_convert_fusion.11), channel_id=1, source_target_pairs={{0,3},{1,0},{2,1},{3,2},{4,7},{5,4},{6,5},{7,6},{8,11},{9,8},{10,9... | collective-permute-start | bytes 196616 | tf_op jit(solution)/shard_map/ppermute | solution.py:430
  340.7 14.3 %collective-permute-start.33 = (bf16[512,64]{0,1:T(8,128)(2,1)S(1)}, bf16[512,64]{0,1:T(8,128)(2,1)S(1)}, u32[]{:S(2)}, u32[]{:S(2)}) collective-permute-start(bf16[512,64]{0,1:T(8,128)(2,1)S(1)} %convolution_convert_fusion.11), channel_id=1, source_target_pairs={{0,1},{1,2},{2,3},{3,0},{4,5},{5,6},{6,7},{7,4},{8,9},{9,10},{10,1... | collective-permute-start | bytes 196616 | tf_op jit(solution)/shard_map/ppermute | solution.py:430
  355.6 6.7 %collective-permute-start.37 = (bf16[16,3712]{1,0:T(8,128)(2,1)S(1)}, bf16[16,3712]{1,0:T(8,128)(2,1)S(1)}, u32[]{:S(2)}, u32[]{:S(2)}) collective-permute-start(bf16[16,3712]{1,0:T(8,128)(2,1)S(1)} %constant_dynamic-update-slice_fusion.4), channel_id=1, source_target_pairs={{0,8},{4,12},{8,0},{12,4},{1,9},{5,13},{9,1},{13,5},{2,10},{6,14},... | collective-permute-start | bytes 356360 | tf_op jit(solution)/shard_map/ppermute | solution.py:430
  357.6 6.5 %collective-permute-start.38 = (bf16[16,3712]{1,0:T(8,128)(2,1)S(1)}, bf16[16,3712]{1,0:T(8,128)(2,1)S(1)}, u32[]{:S(2)}, u32[]{:S(2)}) collective-permute-start(bf16[16,3712]{1,0:T(8,128)(2,1)S(1)} %constant_dynamic-update-slice_fusion.4), channel_id=1, source_target_pairs={{0,12},{4,0},{8,4},{12,8},{1,13},{5,1},{9,5},{13,9},{2,14},{6,2},{... | collective-permute-start | bytes 356360 | tf_op jit(solution)/shard_map/ppermute | solution.py:430
  360.8 6.0 %collective-permute-start.39 = (bf16[16,3712]{1,0:T(8,128)(2,1)S(1)}, bf16[16,3712]{1,0:T(8,128)(2,1)S(1)}, u32[]{:S(2)}, u32[]{:S(2)}) collective-permute-start(bf16[16,3712]{1,0:T(8,128)(2,1)S(1)} %constant_dynamic-update-slice_fusion.4), channel_id=1, source_target_pairs={{0,4},{4,8},{8,12},{12,0},{1,5},{5,9},{9,13},{13,1},{2,6},{6,10},{... | collective-permute-start | bytes 356360 | tf_op jit(solution)/shard_map/ppermute | solution.py:430
  362.4 15.2 %collective-permute-start.12 = (bf16[128,2176]{1,0:T(8,128)(2,1)}, bf16[128,2176]{1,0:T(8,128)(2,1)}, u32[]{:S(2)}, u32[]{:S(2)}) collective-permute-start(bf16[128,2176]{1,0:T(8,128)(2,1)} %convolution_convert_fusion.3), channel_id=1, source_target_pairs={{0,3},{1,0},{2,1},{3,2},{4,7},{5,4},{6,5},{7,6},{8,11},{9,8},{10,9... | collective-permute-start | bytes 1671176 | tf_op jit(solution)/shard_map/ppermute | solution.py:430
  367.5 167.9 %all-gather.13.cloned.1.call-start = ((), (), s32[]{:S(2)}) async-start(), calls=%async_computation.3 | async-start | bytes 7163904 | tf_op jit(solution)/shard_map/all_gather | solution.py:691
  387.9 5.8 %collective-permute-start.41 = (bf16[16,2048]{1,0:T(8,128)(2,1)S(1)}, bf16[16,2048]{1,0:T(8,128)(2,1)S(1)}, u32[]{:S(2)}, u32[]{:S(2)}) collective-permute-start(bf16[16,2048]{1,0:T(8,128)(2,1)S(1)} %get-tuple-element.92), channel_id=1, source_target_pairs={{0,2},{1,3},{2,0},{3,1},{4,6},{5,7},{6,4},{7,5},{8,10},{9,11},{10,... | collective-permute-start | bytes 196616 | tf_op jit(solution)/shard_map/ppermute | solution.py:430
  398.0 8.1 %collective-permute-start.43 = (bf16[16,6784]{1,0:T(8,128)(2,1)S(1)}, bf16[16,6784]{1,0:T(8,128)(2,1)S(1)}, u32[]{:S(2)}, u32[]{:S(2)}) collective-permute-start(bf16[16,6784]{1,0:T(8,128)(2,1)S(1)} %fusion.51), channel_id=1, source_target_pairs={{0,8},{4,12},{8,0},{12,4},{1,9},{5,13},{9,1},{13,5},{2,10},{6,14},... | collective-permute-start | bytes 651272 | tf_op jit(solution)/shard_map/ppermute | solution.py:430
  400.0 7.4 %collective-permute-start.44 = (bf16[16,6784]{1,0:T(8,128)(2,1)S(1)}, bf16[16,6784]{1,0:T(8,128)(2,1)S(1)}, u32[]{:S(2)}, u32[]{:S(2)}) collective-permute-start(bf16[16,6784]{1,0:T(8,128)(2,1)S(1)} %fusion.51), channel_id=1, source_target_pairs={{0,12},{4,0},{8,4},{12,8},{1,13},{5,1},{9,5},{13,9},{2,14},{6,2},{... | collective-permute-start | bytes 651272 | tf_op jit(solution)/shard_map/ppermute | solution.py:430
  403.1 7.1 %collective-permute-start.45 = (bf16[16,6784]{1,0:T(8,128)(2,1)S(1)}, bf16[16,6784]{1,0:T(8,128)(2,1)S(1)}, u32[]{:S(2)}, u32[]{:S(2)}) collective-permute-start(bf16[16,6784]{1,0:T(8,128)(2,1)S(1)} %fusion.51), channel_id=1, source_target_pairs={{0,4},{4,8},{8,12},{12,0},{1,5},{5,9},{9,13},{13,1},{2,6},{6,10},{... | collective-permute-start | bytes 651272 | tf_op jit(solution)/shard_map/ppermute | solution.py:430
  430.5 20.2 %collective-permute-start.28 = (bf16[128,2048]{1,0:T(8,128)(2,1)S(1)}, bf16[128,2048]{1,0:T(8,128)(2,1)S(1)}, u32[]{:S(2)}, u32[]{:S(2)}) collective-permute-start(bf16[128,2048]{1,0:T(8,128)(2,1)S(1)} %fusion.41), channel_id=1, source_target_pairs={{0,1},{1,2},{2,3},{3,0},{4,5},{5,6},{6,7},{7,4},{8,9},{9,10},{10,1... | collective-permute-start | bytes 1572872 | tf_op jit(solution)/shard_map/ppermute | solution.py:430
  437.6 16.5 %collective-permute-start.29 = (bf16[128,2048]{1,0:T(8,128)(2,1)S(1)}, bf16[128,2048]{1,0:T(8,128)(2,1)S(1)}, u32[]{:S(2)}, u32[]{:S(2)}) collective-permute-start(bf16[128,2048]{1,0:T(8,128)(2,1)S(1)} %fusion.44), channel_id=1, source_target_pairs={{0,2},{1,3},{2,0},{3,1},{4,6},{5,7},{6,4},{7,5},{8,10},{9,11},{10,... | collective-permute-start | bytes 1572872 | tf_op jit(solution)/shard_map/ppermute | solution.py:430
  441.2 30.2 %collective-permute-start.30 = (bf16[128,2048]{1,0:T(8,128)(2,1)S(1)}, bf16[128,2048]{1,0:T(8,128)(2,1)S(1)}, u32[]{:S(2)}, u32[]{:S(2)}) collective-permute-start(bf16[128,2048]{1,0:T(8,128)(2,1)S(1)} %fusion.47), channel_id=1, source_target_pairs={{0,3},{1,0},{2,1},{3,2},{4,7},{5,4},{6,5},{7,6},{8,11},{9,8},{10,9... | collective-permute-start | bytes 1572872 | tf_op jit(solution)/shard_map/ppermute | solution.py:430
  445.0 42.7 %collective-permute-start.13 = (bf16[128,2048]{1,0:T(8,128)(2,1)S(1)}, bf16[128,2048]{1,0:T(8,128)(2,1)S(1)}, u32[]{:S(2)}, u32[]{:S(2)}) collective-permute-start(bf16[128,2048]{1,0:T(8,128)(2,1)S(1)} %get-tuple-element.103), channel_id=1, source_target_pairs={{0,3},{1,0},{2,1},{3,2},{4,7},{5,4},{6,5},{7,6},{8,11},{9,8},{10,9... | collective-permute-start | bytes 1572872 | tf_op jit(solution)/shard_map/ppermute | solution.py:430
  447.3 54.5 %collective-permute-start.14 = (bf16[128,2048]{1,0:T(8,128)(2,1)S(1)}, bf16[128,2048]{1,0:T(8,128)(2,1)S(1)}, u32[]{:S(2)}, u32[]{:S(2)}) collective-permute-start(bf16[128,2048]{1,0:T(8,128)(2,1)S(1)} %get-tuple-element.103), channel_id=1, source_target_pairs={{0,2},{1,3},{2,0},{3,1},{4,6},{5,7},{6,4},{7,5},{8,10},{9,11},{10,... | collective-permute-start | bytes 1572872 | tf_op jit(solution)/shard_map/ppermute | solution.py:430
  450.7 53.1 %collective-permute-start.15 = (bf16[128,2048]{1,0:T(8,128)(2,1)S(1)}, bf16[128,2048]{1,0:T(8,128)(2,1)S(1)}, u32[]{:S(2)}, u32[]{:S(2)}) collective-permute-start(bf16[128,2048]{1,0:T(8,128)(2,1)S(1)} %get-tuple-element.103), channel_id=1, source_target_pairs={{0,1},{1,2},{2,3},{3,0},{4,5},{5,6},{6,7},{7,4},{8,9},{9,10},{10,1... | collective-permute-start | bytes 1572872 | tf_op jit(solution)/shard_map/ppermute | solution.py:430
  478.0 34.8 %collective-permute-start.34 = (bf16[128,2048]{1,0:T(8,128)(2,1)S(1)}, bf16[128,2048]{1,0:T(8,128)(2,1)S(1)}, u32[]{:S(2)}, u32[]{:S(2)}) collective-permute-start(bf16[128,2048]{1,0:T(8,128)(2,1)S(1)} %get-tuple-element.62), channel_id=1, source_target_pairs={{0,3},{1,0},{2,1},{3,2},{4,7},{5,4},{6,5},{7,6},{8,11},{9,8},{10,9... | collective-permute-start | bytes 1572872 | tf_op jit(solution)/shard_map/ppermute | solution.py:430
  502.6 18.8 %collective-permute-start.35 = (bf16[128,2048]{1,0:T(8,128)(2,1)S(1)}, bf16[128,2048]{1,0:T(8,128)(2,1)S(1)}, u32[]{:S(2)}, u32[]{:S(2)}) collective-permute-start(bf16[128,2048]{1,0:T(8,128)(2,1)S(1)} %get-tuple-element.62), channel_id=1, source_target_pairs={{0,2},{1,3},{2,0},{3,1},{4,6},{5,7},{6,4},{7,5},{8,10},{9,11},{10,... | collective-permute-start | bytes 1572872 | tf_op jit(solution)/shard_map/ppermute | solution.py:430
  504.7 17.8 %collective-permute-start.36 = (bf16[128,2048]{1,0:T(8,128)(2,1)S(1)}, bf16[128,2048]{1,0:T(8,128)(2,1)S(1)}, u32[]{:S(2)}, u32[]{:S(2)}) collective-permute-start(bf16[128,2048]{1,0:T(8,128)(2,1)S(1)} %get-tuple-element.62), channel_id=1, source_target_pairs={{0,1},{1,2},{2,3},{3,0},{4,5},{5,6},{6,7},{7,4},{8,9},{9,10},{10,1... | collective-permute-start | bytes 1572872 | tf_op jit(solution)/shard_map/ppermute | solution.py:430
  (91 other events, 1207.0 us)
Sparse Core Ops, SparseCore 0:
  12.4 54.8 all-gather.6
  70.2 81.4 all-gather.8
  367.7 43.9 all-gather.10
  414.3 90.6 all-gather.12

commit v2 on v1

v2 whole, which is shorter than its diff:
```python
import functools

import jax
import jax.numpy as jnp
from jax import lax
from jax.experimental import pallas as pl
from jax.experimental.pallas import tpu as pltpu
from jax.sharding import PartitionSpec as P

EPSILON = 1e-06
HALO = 8
CHUNK = 128
LANES = 128
F32 = jnp.float32
BF16 = jnp.bfloat16
MIB = 1024 * 1024


def dot_low(left, right, left_dim=1, right_dim=0):
    return lax.dot_general(
        left.astype(BF16),
        right.astype(BF16),
        (((left_dim,), (right_dim,)), ((), ())),
        preferred_element_type=F32,
    )


def conv_rows(x_ref, columns, taps_ref, seg_ref, span):
    here = seg_ref[HALO : HALO + span, :]
    total = taps_ref[0:1, columns] * x_ref[HALO : HALO + span, columns]
    for tap in range(1, taps_ref.shape[0]):
        same = seg_ref[HALO - tap : HALO - tap + span, :] == here
        total = total + taps_ref[tap : tap + 1, columns] * jnp.where(
            same, x_ref[HALO - tap : HALO - tap + span, columns], 0.0
        )
    return total


def inverse_norm(values):
    return lax.rsqrt(jnp.sum(values * values, axis=-1, keepdims=True) + EPSILON)


def head_column(array, head):
    lane = lax.broadcasted_iota(jnp.int32, array.shape, 1)
    return jnp.sum(jnp.where(lane == head, array, 0.0), axis=1, keepdims=True)


def chunk_masks(seg_ref, row_ref, chunk):
    start = HALO + chunk * CHUNK
    column = seg_ref[start : start + CHUNK, :]
    row = row_ref[chunk : chunk + 1, :]
    before = seg_ref[start - 1 : start, :]
    last = seg_ref[start + CHUNK - 1 : start + CHUNK, :]
    same = column == row
    row_ids = lax.broadcasted_iota(jnp.int32, (CHUNK, CHUNK), 0)
    col_ids = lax.broadcasted_iota(jnp.int32, (CHUNK, CHUNK), 1)
    strict = (same & (row_ids > col_ids)).astype(F32)
    causal = (same & (row_ids >= col_ids)).astype(F32)
    running = (column == before).astype(F32)
    closing = (column == last).astype(F32)
    carried = (before == last).astype(F32)
    return strict, causal, running, closing, carried


def unit_lower_inverses(lowers):
    size = lowers[0].shape[0]
    row_ids = lax.broadcasted_iota(jnp.int32, (size, size), 0)
    col_ids = lax.broadcasted_iota(jnp.int32, (size, size), 1)
    identity = (row_ids == col_ids).astype(F32)
    pair = (row_ids >> 1) == (col_ids >> 1)
    highs = [lower.astype(BF16) for lower in lowers]
    inverses = [identity - jnp.where(pair, lower, 0.0) for lower in lowers]
    bits = 2
    while (1 << bits) <= size:
        joined = ((row_ids >> bits) == (col_ids >> bits)) & (
            (row_ids >> (bits - 1)) != (col_ids >> (bits - 1))
        )
        rounded = [inverse.astype(BF16) for inverse in inverses]
        inner = [
            dot_low(jnp.where(joined, high, jnp.zeros_like(high)), inverse)
            for high, inverse in zip(highs, rounded)
        ]
        inverses = [
            inverse - dot_low(low, part) for inverse, low, part in zip(inverses, rounded, inner)
        ]
        bits += 1
    rounded = [inverse.astype(BF16) for inverse in inverses]
    rests = [(lower - high.astype(F32)).astype(BF16) for lower, high in zip(lowers, highs)]
    residuals = [
        identity - low.astype(F32) - (dot_low(high, low) + dot_low(rest, low))
        for low, high, rest in zip(rounded, highs, rests)
    ]
    return [low.astype(F32) + dot_low(low, part) for low, part in zip(rounded, residuals)]


def delta_local_kernel(
    q_ref, k_ref, v_ref, logit_ref, taps_q, taps_k, taps_v, seg_ref, row_ref,
    qp_ref, op_ref, offset_ref, linear_ref, inverse_ref, prefix_ref, solved_ref, score_ref, zq_ref, zk_ref, zv_ref,
    *, span, head_dim, group,
):
    chunks = span // CHUNK
    step = pl.program_id(0)
    masks = [chunk_masks(seg_ref, row_ref, chunk) for chunk in range(chunks)]
    rates_all = jax.nn.sigmoid(logit_ref[HALO : HALO + span, :])
    work = []
    for local in range(group):
        columns = slice(local * head_dim, (local + 1) * head_dim)
        zq_ref[:, columns] = conv_rows(q_ref, columns, taps_q, seg_ref, span)
        zk_ref[:, columns] = conv_rows(k_ref, columns, taps_k, seg_ref, span)
        zv_ref[:, columns] = conv_rows(v_ref, columns, taps_v, seg_ref, span)
        rates_head = head_column(rates_all, step * group + local)
        for chunk in range(chunks):
            rows = slice(chunk * CHUNK, (chunk + 1) * CHUNK)
            queries = jax.nn.silu(zq_ref[rows, columns])
            queries = (queries * (inverse_norm(queries) * head_dim**-0.5)).astype(BF16)
            keys = jax.nn.silu(zk_ref[rows, columns])
            keys = (keys * inverse_norm(keys)).astype(BF16)
            values = jax.nn.silu(zv_ref[rows, columns]).astype(BF16)
            work.append((local, chunk, queries, keys, values, rates_head[rows]))
    lowers = [
        dot_low(keys, keys, 1, 1) * (rates * masks[chunk][0])
        for _, chunk, _, keys, _, rates in work
    ]
    inverses = unit_lower_inverses(lowers)
    parts = []
    for (local, chunk, queries, keys, values, rates), inverse in zip(work, inverses):
        rows = slice(chunk * CHUNK, (chunk + 1) * CHUNK)
        strict, causal, running, closing, carried = masks[chunk]
        inverse = inverse.astype(BF16)
        inverse_ref[local, rows, :] = inverse
        right = jnp.concatenate([rates * values.astype(F32), rates * keys.astype(F32)], axis=1)
        solved = dot_low(inverse, right)
        solved_ref[local, rows, :] = solved.astype(BF16)
        updates = solved[:, :head_dim]
        weighted = running * solved[:, head_dim:]
        both = jnp.concatenate([updates, weighted], axis=1).astype(BF16)
        scores = (dot_low(queries, keys, 1, 1) * causal).astype(BF16)
        score_ref[local, rows, :] = scores
        near = dot_low(scores, both)
        ends = dot_low(closing * keys.astype(F32), both, 0, 0)
        reach = running * queries.astype(F32) - near[:, head_dim:]
        parts.append((near[:, :head_dim], reach.astype(BF16), ends))
    row_ids = lax.broadcasted_iota(jnp.int32, (head_dim, head_dim), 0)
    col_ids = lax.broadcasted_iota(jnp.int32, (head_dim, head_dim), 1)
    identity = (row_ids == col_ids).astype(F32)
    start = jnp.concatenate([jnp.zeros((head_dim, head_dim), F32), identity], axis=1)
    prefixes = [start] * group
    for chunk in range(chunks):
        rows = slice(chunk * CHUNK, (chunk + 1) * CHUNK)
        carried = masks[chunk][4]
        for local in range(group):
            columns = slice(local * head_dim, (local + 1) * head_dim)
            near, reach, ends = parts[local * chunks + chunk]
            prefix = prefixes[local]
            prefix_ref[local, chunk * head_dim : (chunk + 1) * head_dim, :] = prefix.astype(BF16)
            seen = dot_low(reach, prefix)
            op_ref[rows, columns] = near + seen[:, :head_dim]
            qp_ref[rows, columns] = seen[:, head_dim:].astype(BF16)
            moved = jnp.concatenate([carried, carried], axis=1) * prefix - dot_low(
                ends[:, head_dim:], prefix
            )
            prefixes[local] = jnp.concatenate(
                [moved[:, :head_dim] + ends[:, :head_dim], moved[:, head_dim:]], axis=1
            )
    for local in range(group):
        offset_ref[local] = prefixes[local][:, :head_dim].astype(BF16)
        linear_ref[local] = prefixes[local][:, head_dim:].astype(BF16)


def delta_local(projected, taps, seg_column, seg_rows, heads, head_dim, span, group):
    rows = projected.shape[0]
    width = group * head_dim
    steps = heads // group
    third = lambda part: pl.BlockSpec((rows, width), lambda i: (0, part * steps + i))
    tap_third = lambda part: pl.BlockSpec((taps.shape[0], width), lambda i: (0, part * steps + i))
    whole = lambda array: pl.BlockSpec(array.shape, lambda i: (0,) * array.ndim)
    by_head = lambda *shape: pl.BlockSpec((group,) + shape, lambda i: (i, 0, 0))
    columns = pl.BlockSpec((span, width), lambda i: (0, i))
    chunks = span // CHUNK
    kept = lambda *shape, kind=BF16: jax.ShapeDtypeStruct(shape, kind)
    return pl.pallas_call(
        functools.partial(delta_local_kernel, span=span, head_dim=head_dim, group=group),
        grid=(steps,),
        in_specs=[
            third(0), third(1), third(2),
            pl.BlockSpec((rows, LANES), lambda i: (0, 3 * heads * head_dim // LANES)),
            tap_third(0), tap_third(1), tap_third(2), whole(seg_column), whole(seg_rows),
        ],
        out_specs=[
            columns, columns, by_head(head_dim, head_dim), by_head(head_dim, head_dim),
            by_head(span, CHUNK),
            by_head(chunks * head_dim, 2 * head_dim), by_head(span, 2 * head_dim),
            by_head(span, CHUNK), columns, columns, columns,
        ],
        out_shape=[
            kept(span, heads * head_dim),
            kept(span, heads * head_dim, kind=F32),
            kept(heads, head_dim, head_dim),
            kept(heads, head_dim, head_dim),
            kept(heads, span, CHUNK),
            kept(heads, chunks * head_dim, 2 * head_dim),
            kept(heads, span, 2 * head_dim),
            kept(heads, span, CHUNK),
            kept(span, heads * head_dim, kind=F32),
            kept(span, heads * head_dim, kind=F32),
            kept(span, heads * head_dim, kind=F32),
        ],
        compiler_params=pltpu.CompilerParams(vmem_limit_bytes=22 * MIB),
        name="delta_local",
    )(projected, projected, projected, projected, taps, taps, taps, seg_column, seg_rows)


def attend_kernel(
    position_ref, place_ref, op_ref, qp_ref, one_ref, two_ref, map_ref, three_ref, gain_ref, weight_ref,
    out_ref, att_ref, state_ref, *part_refs,
):
    heads, head_dim = one_ref.shape[0], one_ref.shape[1]
    owners = len(part_refs)
    share = out_ref.shape[0] // owners
    for head in range(heads):
        columns = slice(head * head_dim, (head + 1) * head_dim)
        through = one_ref[head].astype(F32) + dot_low(map_ref[head], three_ref[head])
        state = jnp.where(position_ref[0] == 2, two_ref[head].astype(F32), through)
        state_ref[head] = state.astype(BF16)
        attended = op_ref[:, columns] + dot_low(qp_ref[:, columns], state)
        att_ref[:, columns] = attended
        scale = lax.rsqrt(jnp.mean(attended * attended, axis=-1, keepdims=True) + EPSILON)
        out_ref[:, columns] = (attended * scale * gain_ref[...]).astype(BF16)
    for k, part_ref in enumerate(part_refs):
        start = lax.rem(place_ref[0] + k, owners) * share
        rows = out_ref[pl.ds(pl.multiple_of(start, share), share), :]
        part_ref[...] = dot_low(rows, weight_ref[...], 1, 1).astype(BF16)


def attend(position, place, op, qp, one, two, mapped, three, gain, weight, owners):
    vmem = pl.BlockSpec(memory_space=pltpu.VMEM)
    smem = pl.BlockSpec(memory_space=pltpu.SMEM)
    part = jax.ShapeDtypeStruct((op.shape[0] // owners, weight.shape[0]), BF16)
    return pl.pallas_call(
        attend_kernel,
        in_specs=[smem] * 2 + [vmem] * 8,
        out_specs=[vmem] * (3 + owners),
        out_shape=[
            jax.ShapeDtypeStruct(op.shape, BF16),
            jax.ShapeDtypeStruct(op.shape, F32),
            jax.ShapeDtypeStruct(one.shape, BF16),
        ]
        + [part] * owners,
        compiler_params=pltpu.CompilerParams(vmem_limit_bytes=14 * MIB),
        name="attend",
    )(position, place, op, qp, one, two, mapped, three, gain, weight)


def attend_back_kernel(
    place_ref, att_ref, qp_ref, gain_ref, weight_ref, *refs
):
    *block_refs, out_ref, own_ref, grad_ref = refs
    heads, head_dim = own_ref.shape[0], own_ref.shape[1]
    owners = len(block_refs)
    share = out_ref.shape[0] // owners
    for k, block_ref in enumerate(block_refs):
        start = lax.rem(place_ref[0] + k, owners) * share
        grad_ref[pl.ds(pl.multiple_of(start, share), share), :] = dot_low(
            block_ref[...], weight_ref[...]
        )
    for head in range(heads):
        columns = slice(head * head_dim, (head + 1) * head_dim)
        attended = att_ref[:, columns]
        scale = lax.rsqrt(jnp.mean(attended * attended, axis=-1, keepdims=True) + EPSILON)
        gained = grad_ref[:, columns] * gain_ref[...]
        along = jnp.mean(attended * gained, axis=-1, keepdims=True)
        grad = (scale * gained - attended * (scale * scale * scale * along)).astype(BF16)
        out_ref[:, columns] = grad
        own_ref[head] = dot_low(qp_ref[:, columns], grad, 0, 0).astype(BF16)


def attend_back(place, attended, qp, gain, weight, blocks, heads, head_dim):
    vmem = pl.BlockSpec(memory_space=pltpu.VMEM)
    return pl.pallas_call(
        attend_back_kernel,
        in_specs=[pl.BlockSpec(memory_space=pltpu.SMEM)] + [vmem] * (4 + len(blocks)),
        out_specs=[vmem] * 2,
        out_shape=[
            jax.ShapeDtypeStruct(attended.shape, BF16),
            jax.ShapeDtypeStruct((heads, head_dim, head_dim), BF16),
        ],
        scratch_shapes=[pltpu.VMEM(attended.shape, F32)],
        compiler_params=pltpu.CompilerParams(vmem_limit_bytes=14 * MIB),
        name="attend_back",
    )(place, attended, qp, gain, weight, *blocks)


def delta_back_kernel(
    zq_ref, zk_ref, zv_ref, logit_ref, taps_q, taps_k, taps_v, seg_ref, row_ref,
    inverse_ref, prefix_ref, solved_ref, score_ref, state_ref, grad_ref,
    place_ref, one_ref, two_ref, map_ref, three_ref,
    out_ref, halo_ref, tail_ref, dz_ref, *, span, heads, head_dim, group,
):
    chunks = span // CHUNK
    step = pl.program_id(0)
    features = heads * head_dim
    masks = [chunk_masks(seg_ref, row_ref, chunk) for chunk in range(chunks)]
    rates_all = jax.nn.sigmoid(logit_ref[HALO : HALO + span, :])
    lane = lax.broadcasted_iota(jnp.int32, (CHUNK, LANES), 1)

    @pl.when(step == 0)
    def _():
        out_ref[:, 3 * features :] = jnp.zeros((span, LANES), BF16)
        for slot in range(3 * group):
            dz_ref[slot, 0:HALO, :] = jnp.zeros((HALO, head_dim), F32)
            dz_ref[slot, HALO + span :, :] = jnp.zeros((HALO, head_dim), F32)

    kept, leavings = [], []
    for local in range(group):
        columns = slice(local * head_dim, (local + 1) * head_dim)
        rates_head = head_column(rates_all, step * group + local)
        entry = state_ref[local]
        through = one_ref[local].astype(F32) + dot_low(map_ref[local], three_ref[local], 0, 0)
        leavings.append(jnp.where(place_ref[0] == 1, two_ref[local].astype(F32), through))
        for chunk in range(chunks):
            rows = slice(chunk * CHUNK, (chunk + 1) * CHUNK)
            strict, causal, running, closing, carried = masks[chunk]
            queries = jax.nn.silu(zq_ref[rows, columns])
            scale_q = inverse_norm(queries)
            queries = queries * scale_q
            keys = jax.nn.silu(zk_ref[rows, columns])
            scale_k = inverse_norm(keys)
            keys = keys * scale_k
            low_q = (queries * head_dim**-0.5).astype(BF16)
            low_k = keys.astype(BF16)
            values = jax.nn.silu(zv_ref[rows, columns])
            solved = solved_ref[local, rows, :].astype(F32)
            weighted = (running * solved[:, head_dim:]).astype(BF16)
            prefix = prefix_ref[local, chunk * head_dim : (chunk + 1) * head_dim, :]
            state = (
                prefix[:, :head_dim].astype(F32) + dot_low(prefix[:, head_dim:], entry)
            ).astype(BF16)
            errors = (solved[:, :head_dim] - dot_low(weighted, state)).astype(BF16)
            scores = score_ref[local, rows, :]
            grad = grad_ref[rows, columns]
            near = dot_low(scores, grad, 0, 0)
            far = dot_low(running * low_q.astype(F32), grad, 0, 0)
            grad_scores = (dot_low(grad, errors, 1, 1) * causal).astype(BF16)
            kept.append((queries, scale_q, keys, scale_k, low_q, low_k, values,
                         rates_head[rows], weighted, state, errors, near, far, grad_scores))
    grad_errors_all = [None] * (group * chunks)
    leaving_all = [None] * (group * chunks)
    for chunk in reversed(range(chunks)):
        strict, causal, running, closing, carried = masks[chunk]
        for local in range(group):
            item = local * chunks + chunk
            low_k, weighted, near, far = (kept[item][i] for i in (5, 8, 11, 12))
            leaving = leavings[local]
            low_leaving = leaving.astype(BF16)
            leaving_all[item] = low_leaving
            grad_errors = near + closing * dot_low(low_k, low_leaving)
            grad_errors_all[item] = grad_errors.astype(BF16)
            leavings[local] = (
                carried * leaving + far - dot_low(weighted, grad_errors_all[item], 0, 0)
            )
    for local in range(group):
        columns = slice(local * head_dim, (local + 1) * head_dim)
        head = step * group + local
        for chunk in range(chunks):
            rows = slice(chunk * CHUNK, (chunk + 1) * CHUNK)
            inner = slice(HALO + chunk * CHUNK, HALO + (chunk + 1) * CHUNK)
            strict, causal, running, closing, carried = masks[chunk]
            item = local * chunks + chunk
            (queries, scale_q, keys, scale_k, low_q, low_k, values, rates, weighted, state,
             errors, near, far, grad_scores) = kept[item]
            grad_errors, leaving = grad_errors_all[item], leaving_all[item]
            grad = grad_ref[rows, columns]
            grad_queries = running * dot_low(grad, state, 1, 1) + dot_low(grad_scores, low_k)
            grad_keys = dot_low(grad_scores, low_q, 0, 0) + closing * dot_low(
                errors, leaving, 1, 1
            )
            grad_weighted = -running * dot_low(grad_errors, state, 1, 1)
            grad_right = dot_low(
                inverse_ref[local, rows, :],
                jnp.concatenate([grad_errors, grad_weighted.astype(BF16)], axis=1), 0, 0,
            )
            right_v, right_k = grad_right[:, :head_dim], grad_right[:, head_dim:]
            grad_lower = -dot_low(grad_right, solved_ref[local, rows, :], 1, 1) * strict
            gram = dot_low(low_k, low_k, 1, 1)
            grad_rates = jnp.sum(
                right_v * values + right_k * keys + grad_lower * gram, axis=1, keepdims=True
            )
            grad_gram = (rates * grad_lower).astype(BF16)
            grad_keys = (
                grad_keys
                + rates * right_k
                + dot_low(grad_gram, low_k)
                + dot_low(grad_gram, low_k, 0, 0)
            )
            grad_logit = grad_rates * rates * (1.0 - rates)
            previous = out_ref[rows, 3 * features :].astype(F32)
            out_ref[rows, 3 * features :] = jnp.where(lane == head, grad_logit, previous).astype(BF16)
            grad_queries = grad_queries * head_dim**-0.5
            grad_queries = scale_q * (
                grad_queries - queries * jnp.sum(queries * grad_queries, axis=-1, keepdims=True)
            )
            grad_keys = scale_k * (
                grad_keys - keys * jnp.sum(keys * grad_keys, axis=-1, keepdims=True)
            )
            for part, (z_ref, grad_part) in enumerate(
                ((zq_ref, grad_queries), (zk_ref, grad_keys), (zv_ref, rates * right_v))
            ):
                conv = z_ref[rows, columns]
                sig = jax.nn.sigmoid(conv)
                dz_ref[local * 3 + part, inner, :] = grad_part * (
                    sig * (1.0 + conv * (1.0 - sig))
                )
        here = seg_ref[0 : HALO + span, :]
        for part, taps in enumerate((taps_q, taps_k, taps_v)):
            slot = local * 3 + part
            total = taps[0:1, columns] * dz_ref[slot, 0 : HALO + span, :]
            for tap in range(1, taps.shape[0]):
                same = seg_ref[tap : tap + HALO + span, :] == here
                total = total + taps[tap : tap + 1, columns] * jnp.where(
                    same, dz_ref[slot, tap : tap + HALO + span, :], 0.0
                )
            place = pl.ds(pl.multiple_of(part * features + head * head_dim, LANES), head_dim)
            halo_ref[:, place] = total[:HALO]
            tail_ref[:, place] = total[span:]
            out_ref[:, place] = total[HALO:].astype(BF16)


def delta_back(
    projected, taps, seg_column, seg_rows, kept, state, grad, position, arrived, heads, head_dim, span,
    group,
):
    inverse, prefix, solved, scores, conv_q, conv_k, conv_v = kept
    rows = projected.shape[0]
    width = group * head_dim
    steps = heads // group
    columns = pl.BlockSpec((span, width), lambda i: (0, i))
    tap_third = lambda part: pl.BlockSpec((taps.shape[0], width), lambda i: (0, part * steps + i))
    whole = lambda array: pl.BlockSpec(array.shape, lambda i: (0,) * array.ndim)
    by_head = lambda array: pl.BlockSpec((group,) + array.shape[1:], lambda i: (i, 0, 0))
    total = 3 * heads * head_dim
    return pl.pallas_call(
        functools.partial(
            delta_back_kernel, span=span, heads=heads, head_dim=head_dim, group=group
        ),
        grid=(steps,),
        in_specs=[
            columns, columns, columns,
            pl.BlockSpec((rows, LANES), lambda i: (0, total // LANES)),
            tap_third(0), tap_third(1), tap_third(2), whole(seg_column), whole(seg_rows),
            by_head(inverse), by_head(prefix), by_head(solved), by_head(scores), by_head(state),
            columns, pl.BlockSpec(memory_space=pltpu.SMEM), *[by_head(array) for array in arrived],
        ],
        out_specs=[
            pl.BlockSpec((span, total + LANES), lambda i: (0, 0)),
            pl.BlockSpec((HALO, total), lambda i: (0, 0)),
            pl.BlockSpec((HALO, total), lambda i: (0, 0)),
        ],
        out_shape=[
            jax.ShapeDtypeStruct((span, total + LANES), BF16),
            jax.ShapeDtypeStruct((HALO, total), F32),
            jax.ShapeDtypeStruct((HALO, total), F32),
        ],
        scratch_shapes=[pltpu.VMEM((3 * group, span + 2 * HALO, head_dim), F32)],
        compiler_params=pltpu.CompilerParams(vmem_limit_bytes=24 * MIB),
        name="delta_back",
    )(
        conv_q, conv_k, conv_v, projected, taps, taps, taps, seg_column, seg_rows,
        inverse, prefix, solved, scores, state, grad, position, *arrived,
    )


def normed_grad(values, gain, grad):
    scale = lax.rsqrt(jnp.mean(values * values, axis=-1, keepdims=True) + EPSILON)
    gained = gain * grad
    along = jnp.mean(values * gained, axis=-1, keepdims=True)
    return scale * gained - values * (scale * scale * scale * along)


def added(refs, columns):
    total = refs[0][:, columns].astype(F32)
    for ref in refs[1:]:
        total = total + ref[:, columns].astype(F32)
    return total


def middle_kernel(
    place_ref, own_ref, one_ref, two_ref, three_ref, tokens_ref, out_map_ref, gain_ref, in_map_ref,
    middle_ref, packed_ref, low_ref,
):
    model = tokens_ref.shape[1]
    refs = (own_ref, one_ref, two_ref, three_ref)
    low = added(refs, slice(model, model + LANES)).astype(BF16)
    low_ref[...] = low
    middle = (
        tokens_ref[...].astype(F32)
        + added(refs, slice(0, model))
        + dot_low(low, out_map_ref[...])
    )
    middle_ref[...] = middle
    scale = lax.rsqrt(jnp.mean(middle * middle, axis=-1, keepdims=True) + EPSILON)
    normed = (middle * scale * gain_ref[...]).astype(BF16)
    packed_ref[:, :model] = normed
    packed_ref[:, model:] = dot_low(normed, in_map_ref[...], 1, 1).astype(BF16)


def back_kernel(
    place_ref, own_ref, one_ref, two_ref, three_ref, cot_ref, middle_in, gain_ref, in_map_ref,
    out_map_ref, low_ref, grad_ref, packed_ref, *, rank,
):
    model = cot_ref.shape[1]
    refs = (own_ref, one_ref, two_ref, three_ref)
    low_ffn = added(refs, slice(model, model + LANES)).astype(BF16)
    grad = added(refs, slice(0, model)) + dot_low(low_ffn, in_map_ref[...])
    grad = cot_ref[...].astype(F32) + normed_grad(middle_in[...], gain_ref[...], grad)
    grad_ref[...] = grad
    rounded = grad.astype(BF16)
    packed_ref[:, :model] = rounded
    low_out = dot_low(rounded, out_map_ref[...], 1, 1).astype(BF16).astype(F32)
    packed_ref[:, model:] = (
        low_out
        + pltpu.roll(low_ref[...].astype(F32), rank, 1)
        + pltpu.roll(low_ffn.astype(F32), 2 * rank, 1)
    ).astype(BF16)


def tokens_kernel(
    place_ref, own_ref, one_ref, two_ref, three_ref, low_ref, in_map_ref, tokens_ref, gain_ref,
    grad_ref, out_ref,
):
    refs = (own_ref, one_ref, two_ref, three_ref)
    grad = added(refs, slice(None)) + dot_low(low_ref[...], in_map_ref[...])
    out_ref[...] = (
        grad_ref[...] + normed_grad(tokens_ref[...].astype(F32), gain_ref[...], grad)
    ).astype(BF16)


def owner_call(kernel, name, place, share, arrays, outs, strips=2):
    strip = share // strips

    def spec(array, mark):
        if mark == "rows":
            return pl.BlockSpec((strip, array.shape[1]), lambda i, c: (i, 0))
        if mark == "span":
            return pl.BlockSpec((strip, array.shape[1]), lambda i, c: (c[0] * strips + i, 0))
        return pl.BlockSpec(array.shape, lambda i, c: (0, 0))

    return pl.pallas_call(
        kernel,
        grid_spec=pltpu.PrefetchScalarGridSpec(
            num_scalar_prefetch=1,
            grid=(strips,),
            in_specs=[spec(array, mark) for array, mark in arrays],
            out_specs=[pl.BlockSpec((strip, shape[1]), lambda i, c: (i, 0)) for shape, _ in outs],
        ),
        out_shape=[jax.ShapeDtypeStruct(shape, kind) for shape, kind in outs],
        compiler_params=pltpu.CompilerParams(vmem_limit_bytes=56 * MIB),
        name=name,
    )(place, *[array for array, _ in arrays])


def early_kernel(
    place_ref, g0, g1, g2, g3, x0, x1, x2, x3, head_ref, low_down_ref, cot_ref,
    out_one, out_two, down_one, down_two, *refs, rank,
):
    (pack_ref,) = refs
    model = cot_ref.shape[1]
    hidden_units = down_one.shape[1]
    owners, share = 4, g0.shape[0]
    through_g, through_x, through_h = 0.0, 0.0, 0.0
    for k, (g_ref, x_ref) in enumerate(zip((g0, g1, g2, g3), (x0, x1, x2, x3))):
        low = g_ref[:, model:]
        start = lax.rem(place_ref[0] + k, owners) * share
        heads = head_ref[pl.ds(pl.multiple_of(start, share), share), :]
        through_g = through_g + dot_low(low, g_ref[:, :model], 0, 0)
        through_x = through_x + dot_low(low, x_ref[:, :model], 0, 0)
        through_h = through_h + dot_low(low, heads, 0, 0)
    out_terms = out_one[...] + out_two[...]
    pack_ref[0, :, :model] = through_x[2 * rank : 3 * rank].astype(BF16)
    pack_ref[0, :, model:] = out_terms[:rank, :hidden_units].astype(BF16)
    pack_ref[1, :, :model] = through_x[3 * rank : 4 * rank].astype(BF16)
    pack_ref[1, :, model:] = out_terms[rank:, hidden_units:].astype(BF16)
    pack_ref[2, :, :model] = dot_low(low_down_ref[...], cot_ref[...]).astype(BF16)
    pack_ref[2, :, model:] = (down_one[...] + down_two[...]).astype(BF16)
    pack_ref[3, :, :model] = through_g[rank : 2 * rank].astype(BF16)
    pack_ref[3, :, model:] = jnp.zeros((rank, hidden_units), BF16)
    pack_ref[3, :, model : model + through_h.shape[1]] = through_h[:rank].astype(BF16)


def late_kernel(
    position_ref, p0, p1, p2, p3, normed_ref, low_ref, grad_ref, early_ref, low_out_ref, *refs, rank
):
    *out_refs, pack_ref = refs
    model = normed_ref.shape[1]
    features = (grad_ref.shape[1] - LANES) // 3
    total = (p0[...].astype(F32) + p2[...].astype(F32)) + (
        p1[...].astype(F32) + p3[...].astype(F32)
    )
    low_grad = total.astype(BF16)
    low_out_ref[...] = low_grad
    items = dot_low(low_grad, normed_ref[...], 0, 0)
    blocks = dot_low(low_ref[...], grad_ref[...], 0, 0)
    for part in range(4):
        rows = slice(part * rank, (part + 1) * rank)
        pack_ref[part, :, :model] = items[rows].astype(BF16)
        if part < 3:
            pack_ref[part, :, model:] = blocks[rows, part * features : (part + 1) * features].astype(BF16)
        else:
            pack_ref[part, :, model:] = jnp.zeros((rank, features), BF16)
            pack_ref[part, :, model : model + LANES] = blocks[rows, 3 * features :].astype(BF16)
    early_width = early_ref.shape[2]
    for k, out_ref in enumerate(out_refs):
        quarter = lax.rem(position_ref[0] + k, 4)
        out_ref[:, :early_width] = early_ref[quarter]
        out_ref[:, early_width:] = pack_ref[quarter]


def span_call(kernel, name, scalars, arrays, outs, scratch, limit):
    vmem = pl.BlockSpec(memory_space=pltpu.VMEM)
    return pl.pallas_call(
        kernel,
        in_specs=[pl.BlockSpec(memory_space=pltpu.SMEM)] * len(scalars) + [vmem] * len(arrays),
        out_specs=[vmem] * len(outs),
        out_shape=[jax.ShapeDtypeStruct(shape, kind) for shape, kind in outs],
        scratch_shapes=scratch,
        compiler_params=pltpu.CompilerParams(vmem_limit_bytes=limit * MIB),
        name=name,
    )(*scalars, *arrays)


def ffn_kernel(
    place_ref, x_first, x_second, weight_ref, low_ref, grad_ref, down_ref,
    hidden_ref, back_first, back_second, out_low_ref, down_low_ref, *, strip,
):
    share = x_first.shape[0]
    model, hidden_units = weight_ref.shape[0], weight_ref.shape[1] // 2
    rows = jnp.concatenate([x_first[...], x_second[...]], axis=0)

    def theirs(ref):
        parts = [
            ref[pl.ds(pl.multiple_of(place_ref[i] * share, share), share), :] for i in range(2)
        ]
        return jnp.concatenate(parts, axis=0)

    both = dot_low(rows[:, model:], low_ref[...]) + dot_low(rows[:, :model], weight_ref[...])
    gate, up = both[:, :hidden_units], both[:, hidden_units:]
    sig = jax.nn.sigmoid(gate)
    silu = gate * sig
    hidden = (silu * up).astype(BF16)
    hidden_ref[...] = hidden
    grad = theirs(grad_ref)
    grads = jnp.concatenate(
        [
            (grad * up * (sig * (1.0 + gate * (1.0 - sig)))).astype(BF16),
            (grad * silu).astype(BF16),
        ],
        axis=1,
    )
    for start in range(0, model, strip):
        back = dot_low(grads, weight_ref[start : start + strip, :], 1, 1)
        back_first[:, start : start + strip] = back[:share].astype(back_first.dtype)
        back_second[:, start : start + strip] = back[share:].astype(back_second.dtype)
    back = dot_low(grads, low_ref[...], 1, 1)
    back_first[:, model:] = back[:share].astype(back_first.dtype)
    back_second[:, model:] = back[share:].astype(back_second.dtype)
    out_low_ref[...] = dot_low(rows[:, model:], grads, 0, 0)[: out_low_ref.shape[0]]
    down_low_ref[...] = dot_low(theirs(down_ref), hidden, 0, 0)[: down_low_ref.shape[0]]


def ffn_rows(chunks, first, second, weights, low, grad_hidden, low_grad_down, rank, kinds):
    share, wide = first.shape
    hidden_units = grad_hidden.shape[1]
    vmem = pl.BlockSpec(memory_space=pltpu.VMEM)
    return pl.pallas_call(
        functools.partial(ffn_kernel, strip=512),
        in_specs=[pl.BlockSpec(memory_space=pltpu.SMEM)] + [vmem] * 6,
        out_specs=[vmem] * 5,
        out_shape=[
            jax.ShapeDtypeStruct((2 * share, hidden_units), BF16),
            jax.ShapeDtypeStruct((share, wide), kinds[0]),
            jax.ShapeDtypeStruct((share, wide), kinds[1]),
            jax.ShapeDtypeStruct((2 * rank, 2 * hidden_units), F32),
            jax.ShapeDtypeStruct((rank, hidden_units), F32),
        ],
        cost_estimate=pl.CostEstimate(
            flops=16 * share * wide * hidden_units,
            bytes_accessed=4 * wide * hidden_units,
            transcendentals=2 * share * hidden_units,
        ),
        compiler_params=pltpu.CompilerParams(vmem_limit_bytes=14 * MIB),
        name="ffn_rows",
    )(chunks, first, second, weights, low, grad_hidden, low_grad_down)


def in_place_kernel(place_ref, *refs):
    out_ref = refs[-1]
    for k, block_ref in enumerate(refs[:-1]):

        @pl.when(pl.program_id(0) == k)
        def _():
            out_ref[...] = block_ref[...].astype(out_ref.dtype)


def in_place(place, blocks, width, kind):
    owners, share = len(blocks), blocks[0].shape[0]
    return pl.pallas_call(
        in_place_kernel,
        grid_spec=pltpu.PrefetchScalarGridSpec(
            num_scalar_prefetch=1,
            grid=(owners,),
            in_specs=[pl.BlockSpec((share, width), lambda k, c: (0, 0))] * owners,
            out_specs=pl.BlockSpec((share, width), lambda k, c: (lax.rem(c[0] + k, owners), 0)),
        ),
        out_shape=jax.ShapeDtypeStruct((owners * share, width), kind),
        compiler_params=pltpu.CompilerParams(vmem_limit_bytes=8 * MIB),
        name="in_place",
    )(place, *blocks)


def totals_kernel(
    pick_ref, terms_ref, attn_ref, triple_ref, strength_ref, projection_in_ref,
    projection_out_ref, ffn_in_ref, ffn_out_ref, down_in_ref, down_out_ref, *, cuts,
):
    step = pl.program_id(0)
    sequences, _, rank, width = terms_ref.shape
    adapters = projection_out_ref.shape[0]
    shape = (adapters * rank, sequences * rank)
    to = lax.broadcasted_iota(jnp.int32, shape, 0)
    source = lax.broadcasted_iota(jnp.int32, shape, 1)
    wanted = jnp.full(shape, -1, jnp.int32)
    for sequence in range(sequences):
        wanted = jnp.where(
            (source >= sequence * rank) & (source < (sequence + 1) * rank),
            pick_ref[sequence] * rank + source - sequence * rank,
            wanted,
        )
    select = (to == wanted).astype(BF16)
    terms = terms_ref[:, 0].reshape(sequences * rank, width)

    def add_up(out_ref, start, wide):
        total = dot_low(select, terms[:, start : start + wide])
        out_ref[...] = total[:, : out_ref.shape[-1]].reshape(out_ref.shape)

    model = ffn_in_ref.shape[-1]
    add_up(attn_ref, cuts[2], model)

    @pl.when(step < 3)
    def _():
        add_up(triple_ref, cuts[3], triple_ref.shape[-1])

    @pl.when(step < 2)
    def _():
        add_up(ffn_in_ref, cuts[0], model)
        add_up(ffn_out_ref, cuts[1], ffn_out_ref.shape[-1])

    @pl.when(step == 2)
    def _():
        add_up(down_out_ref, cuts[0], model)
        add_up(down_in_ref, cuts[1], down_in_ref.shape[-1])

    @pl.when(step == 3)
    def _():
        add_up(projection_out_ref, cuts[0], model)
        add_up(projection_in_ref, cuts[1], projection_in_ref.shape[-1])
        add_up(strength_ref, cuts[3], LANES)


def totals(picks, terms, cuts, adapters, rank, model, features, hidden_units, heads):
    sequences, quarters, _, width = terms.shape
    part = lambda last, wide: pl.BlockSpec(
        (1, adapters, rank, wide), lambda q, c: (jnp.minimum(q, last), 0, 0, 0)
    )
    one = lambda wide: pl.BlockSpec((adapters, rank, wide), lambda q, c: (0, 0, 0))
    shape = lambda *dims: jax.ShapeDtypeStruct(dims, F32)
    return pl.pallas_call(
        functools.partial(totals_kernel, cuts=cuts),
        grid_spec=pltpu.PrefetchScalarGridSpec(
            num_scalar_prefetch=1,
            grid=(quarters,),
            in_specs=[pl.BlockSpec((sequences, 1, rank, width), lambda q, c: (0, q, 0, 0))],
            out_specs=[
                part(3, model), part(2, features), one(heads), one(features), one(model),
                part(1, model), part(1, hidden_units), one(hidden_units), one(model),
            ],
        ),
        out_shape=[
            shape(4, adapters, rank, model),
            shape(3, adapters, rank, features),
            shape(adapters, rank, heads),
            shape(adapters, rank, features),
            shape(adapters, rank, model),
            shape(2, adapters, rank, model),
            shape(2, adapters, rank, hidden_units),
            shape(adapters, rank, hidden_units),
            shape(adapters, rank, model),
        ],
        compiler_params=pltpu.CompilerParams(vmem_limit_bytes=56 * MIB),
        name="totals",
    )(picks, terms)


def shifted(block, axis, distance, wrap=True):
    size = lax.axis_size(axis)
    if wrap:
        route = [(i, (i + distance) % size) for i in range(size)]
    else:
        route = [(i, i + distance) for i in range(size) if 0 <= i + distance < size]
    return lax.ppermute(block, axis, route)


def sent_to_owners(parts, axis, order=(2, 1, 3)):
    received = {k: shifted(parts[k], axis, k) for k in order}
    return [parts[0]] + [received[k] for k in sorted(order)]


def blocks_of_others(block, axis):
    return [block] + [shifted(block, axis, -k) for k in (1, 2, 3)]


def blocks_by_ring(block, axis, ahead=None):
    half = block.shape[0] // 2
    before = shifted(block, axis, 1)
    after = shifted(block, axis, -1)
    if ahead is not None:
        before, after, ahead = lax.optimization_barrier((before, after, ahead))
    far = jnp.concatenate(
        [shifted(after[:half], axis, -1), shifted(before[half:], axis, 1)], axis=0
    )
    blocks = [block, after, far, before]
    return blocks if ahead is None else (blocks, ahead)


def paired_sum(block, axis):
    blocks = [part.astype(F32) for part in blocks_of_others(block, axis)]
    half = len(blocks) // 2
    while half:
        blocks = [blocks[i] + blocks[i + half] for i in range(half)]
        half //= 2
    return blocks[0]


def dot(left, right):
    return jnp.dot(left, right, preferred_element_type=F32)


def dot_nt(left, right):
    return lax.dot_general(left, right, (((1,), (1,)), ((), ())), preferred_element_type=F32)


def dot_tn(left, right):
    return lax.dot_general(left, right, (((0,), (0,)), ((), ())), preferred_element_type=F32)


def rms_scale(values, gain):
    return values * lax.rsqrt(jnp.mean(values * values, axis=-1, keepdims=True) + EPSILON) * gain


def rms_back(values, gain, grad):
    scale = lax.rsqrt(jnp.mean(values * values, axis=-1, keepdims=True) + EPSILON)
    gained = gain * grad
    return scale * gained - values * (scale**3) * jnp.mean(values * gained, axis=-1, keepdims=True)


def pad_columns(array, width):
    return jnp.pad(array, ((0, 0), (0, width - array.shape[1])))


def pad_rows(array, height):
    return jnp.pad(array, ((0, height - array.shape[0]), (0, 0)))


def on_device(
    tokens,
    cotangent,
    token_document_ids,
    sequence_adapter_index,
    mixer_norm_gain,
    head_norm_gain,
    feedforward_norm_gain,
    short_filter_kernels,
    query_weight,
    key_weight,
    value_weight,
    strength_weight,
    mixer_output_weight,
    gate_weight,
    up_weight,
    down_weight,
    adapter_attention_input,
    adapter_triple_output,
    adapter_strength_output,
    adapter_projection_input,
    adapter_projection_output,
    adapter_feedforward_input,
    adapter_feedforward_output,
    adapter_down_input,
    adapter_down_output,
):
    span, model = tokens.shape
    head_dim = head_norm_gain.shape[0]
    taps = short_filter_kernels.shape[1]
    heads = strength_weight.shape[1]
    features = heads * head_dim
    hidden_units = gate_weight.shape[1]
    adapters = adapter_attention_input.shape[1]
    rank = adapter_attention_input.shape[3]
    owners = lax.axis_size("tensor")
    place = lax.axis_index("tensor")
    position = lax.axis_index("context")
    share = span // owners
    everyone = ("weights", "context")

    def chunk_at(array, k):
        start = lax.rem(place + k, owners) * share
        return lax.dynamic_slice_in_dim(array, start, share, axis=0)

    mixer_pack = jnp.concatenate(
        [
            query_weight, key_weight, value_weight, strength_weight,
            jnp.full(
                (strength_weight.shape[0], LANES - heads),
                sequence_adapter_index[0].astype(BF16),
            ),
            mixer_output_weight.T,
        ],
        axis=1,
    )
    ffn_pack = jnp.concatenate([gate_weight, up_weight, down_weight.T], axis=1)
    mixer_all = lax.all_gather(mixer_pack, everyone, axis=0, tiled=True)
    ffn_all = lax.all_gather(ffn_pack, everyone, axis=0, tiled=True)
    triple = 3 * features + LANES
    weight_in = mixer_all[:, :triple]
    weight_out = mixer_all[:, triple:]
    weight_gate_up = ffn_all[:, : 2 * hidden_units]
    weight_down = ffn_all[:, 2 * hidden_units :]
    picks = mixer_all[:: mixer_all.shape[0] // lax.axis_size("weights"), 3 * features + heads]
    picks = picks.astype(jnp.int32)

    chosen = sequence_adapter_index[0]
    take = lambda table, axis: lax.dynamic_index_in_dim(table, chosen, axis, keepdims=False)
    attention_in = jnp.swapaxes(take(adapter_attention_input, 1), 1, 2).reshape(4 * rank, model)
    triple_out = take(adapter_triple_output, 1)
    strength_out = take(adapter_strength_output, 0)
    projection_in = jnp.swapaxes(take(adapter_projection_input, 0), 0, 1)
    projection_out = take(adapter_projection_output, 0)
    feedforward_in = jnp.swapaxes(take(adapter_feedforward_input, 1), 1, 2).reshape(2 * rank, model)
    feedforward_out = take(adapter_feedforward_output, 1)
    down_in_ext = pad_rows(jnp.swapaxes(take(adapter_down_input, 0), 0, 1), LANES)
    ffn_low = pad_rows(
        jnp.concatenate(
            [
                pad_columns(feedforward_out[0], 2 * hidden_units),
                jnp.pad(feedforward_out[1], ((0, 0), (hidden_units, 0))),
            ],
            axis=0,
        ),
        LANES,
    )
    down_out = take(adapter_down_output, 0)
    low_in = jnp.concatenate(
        [
            jnp.pad(triple_out[part], ((0, 0), (part * features, (2 - part) * features + LANES)))
            for part in range(3)
        ]
        + [jnp.pad(strength_out, ((0, 0), (3 * features, LANES - heads)))],
        axis=0,
    )

    padded_ids = jnp.concatenate(
        [jnp.full((HALO,), -1, jnp.int32), token_document_ids[0], jnp.full((HALO,), -2, jnp.int32)]
    )
    window = lax.dynamic_slice_in_dim(padded_ids, position * span, span + 2 * HALO)
    window = jnp.where(
        jnp.arange(span + 2 * HALO) < span + HALO, window, jnp.full_like(window, -2)
    )
    seg_column = jnp.broadcast_to(window[:, None], (span + 2 * HALO, LANES))
    seg_rows = window[HALO : HALO + span].reshape(span // CHUNK, CHUNK)
    kernels = jnp.transpose(short_filter_kernels, (1, 0, 2)).reshape(taps, -1)

    edge = shifted(tokens[span - HALO :], "context", 1, wrap=False)
    inputs_ext = jnp.concatenate([edge, tokens], axis=0).astype(F32)
    normed_ext = rms_scale(inputs_ext, mixer_norm_gain).astype(BF16)
    low_ext = dot_nt(normed_ext, attention_in).astype(BF16)
    projected = dot(normed_ext, weight_in) + dot(low_ext, low_in)
    normed = normed_ext[HALO:]
    low_attn = low_ext[HALO:]

    where = position[None]
    here = place[None]
    qp, op, offset, linear, *kept = delta_local(
        projected, kernels, seg_column, seg_rows, heads, head_dim, span, heads
    )
    one = shifted(offset, "context", 1, wrap=False)
    linear_two = lax.ppermute(linear, "context", [(2, 3)])
    second = (
        offset.astype(F32)
        + jnp.einsum("hij,hjk->hik", linear, one, preferred_element_type=F32)
    ).astype(BF16)
    out_ext = jnp.concatenate([weight_out, pad_rows(projection_in, LANES)], axis=0)
    second, out_ext = lax.optimization_barrier((second, out_ext))
    two = lax.ppermute(second, "context", [(1, 2)])
    three = lax.ppermute(second, "context", [(1, 3)])
    gain_row = head_norm_gain[None, :]
    head_low, attended, state, *branch_parts = attend(
        where, here, op, qp, one, two, linear_two, three, gain_row, out_ext, owners
    )
    linear_one = lax.ppermute(linear, "context", [(1, 0)])

    wide = model + LANES
    branch = sent_to_owners(branch_parts, "tensor")
    ffn_gain = feedforward_norm_gain[None, :]
    out_map = pad_rows(projection_out, LANES)
    in_map = pad_rows(feedforward_in, LANES)
    middle, packed, low_o = owner_call(
        middle_kernel, "middle_rows", here, share,
        [(part, "rows") for part in branch]
        + [(tokens, "span"), (out_map, "whole"), (ffn_gain, "whole"), (in_map, "whole")],
        [((share, model), F32), ((share, wide), BF16), ((share, LANES), BF16)],
    )
    low_grad_down = pad_columns(dot_nt(cotangent, down_out).astype(BF16), LANES)
    grad_hidden = dot(cotangent, weight_down) + dot(low_grad_down, down_in_ext)
    ffn_in, grad_hidden = blocks_by_ring(packed, "tensor", grad_hidden)

    back_parts, hidden_parts = [None] * owners, [None] * owners
    ffn_out_terms, down_in_terms = [], []
    for pair in ((1, 3), (2, 0)):
        chunks = jnp.stack([lax.rem(place + k, owners) for k in pair])
        hidden_pair, back_parts[pair[0]], back_parts[pair[1]], out_term, down_term = ffn_rows(
            chunks, ffn_in[pair[0]], ffn_in[pair[1]], weight_gate_up, ffn_low, grad_hidden,
            low_grad_down, rank, [F32 if k == 0 else BF16 for k in pair],
        )
        for i, k in enumerate(pair):
            hidden_parts[k] = hidden_pair[i * share : (i + 1) * share]
        ffn_out_terms.append(out_term)
        down_in_terms.append(down_term)
    back = sent_to_owners(back_parts, "tensor", (1, 3, 2))
    hidden = in_place(here, hidden_parts, hidden_units, BF16)
    down_all = dot_nt(hidden, weight_down).astype(BF16)
    back, down_all = lax.optimization_barrier((back, down_all))
    grad_middle, grad_packed = owner_call(
        functools.partial(back_kernel, rank=rank), "back_rows", here, share,
        [(part, "rows") for part in back]
        + [(cotangent, "span"), (middle, "rows"), (ffn_gain, "whole"), (in_map, "whole"),
           (out_map, "whole"), (low_o, "rows")],
        [((share, model), F32), ((share, wide), BF16)],
    )

    grad_blocks = blocks_by_ring(grad_packed, "tensor")

    grad_attended, own = attend_back(
        here, attended, qp, gain_row, out_ext, grad_blocks, heads, head_dim
    )
    hidden, down_all, own = lax.optimization_barrier((hidden, down_all, own))
    down_sum = lax.psum_scatter(down_all, "tensor", scatter_dimension=0, tiled=True).astype(F32)
    down_low = dot_nt(down_in_ext[:rank], hidden).astype(BF16)
    own_one = shifted(own, "context", -1, wrap=False)
    own_one, down_low = lax.optimization_barrier((own_one, down_low))
    own_second = (
        own.astype(F32) + jnp.einsum("hji,hjk->hik", linear, own_one, preferred_element_type=F32)
    ).astype(BF16)
    own_two = lax.ppermute(own_second, "context", [(2, 1)])
    own_three = lax.ppermute(own_second, "context", [(2, 0)])

    low_down = paired_sum(down_low, "tensor").astype(BF16)

    grad_projected, halo, tail = delta_back(
        projected, kernels, seg_column, seg_rows, kept, state, grad_attended, where,
        (own_one, own_two, linear_one, own_three), heads, head_dim, span, heads,
    )
    returned = shifted(halo, "context", -1, wrap=False)
    low_down_own = lax.dynamic_slice_in_dim(low_down, place * share, share, axis=1)
    block_own = (middle + down_sum + dot_tn(low_down_own, down_out)).astype(BF16)
    returned, block_own = lax.optimization_barrier((returned, block_own))
    block_half = share // 2
    block_before = shifted(block_own, "tensor", 1)
    block_after = shifted(block_own, "tensor", -1)
    grad_projected = lax.dynamic_update_slice(
        grad_projected, (tail + returned).astype(BF16), (span - HALO, 0)
    )

    low_part = dot_nt(grad_projected, low_in).astype(BF16)
    low_parts = blocks_of_others(low_part, "tensor")
    early_width = model + hidden_units
    (early,) = span_call(
        functools.partial(early_kernel, rank=rank), "early_terms", (here,),
        [*grad_blocks, *ffn_in, head_low, low_down, cotangent, *ffn_out_terms, *down_in_terms],
        [((4, rank, early_width), BF16)], [], 56,
    )
    *low_parts, block_before, block_after, early = lax.optimization_barrier(
        (*low_parts, block_before, block_after, early)
    )
    late_width = model + features
    low_grad_attn, *quarters = span_call(
        functools.partial(late_kernel, rank=rank), "late_terms", (where,),
        [*low_parts, normed, low_attn, grad_projected, early],
        [((span, 4 * rank), BF16)] + [((rank, early_width + late_width), BF16)] * 4,
        [pltpu.VMEM((4, rank, late_width), BF16)], 24,
    )
    quarters = sent_to_owners(quarters, "context")
    grad_rows, _ = lax.optimization_barrier((grad_projected, low_grad_attn))
    normed_parts = dot_nt(grad_rows, weight_in).astype(BF16)
    *quarters, normed_parts = lax.optimization_barrier((*quarters, normed_parts))
    normed_sent = sent_to_owners([chunk_at(normed_parts, k) for k in range(owners)], "tensor")
    block_far = jnp.concatenate(
        [
            shifted(block_after[:block_half], "tensor", -1),
            shifted(block_before[block_half:], "tensor", 1),
        ],
        axis=0,
    )
    block_out = in_place(here, [block_own, block_after, block_far, block_before], model, BF16)
    (grad_tokens,) = owner_call(
        tokens_kernel, "token_rows", here, share,
        [(part, "rows") for part in normed_sent]
        + [(low_grad_attn, "span"), (attention_in, "whole"), (tokens, "span"),
           (mixer_norm_gain[None, :], "whole"), (grad_middle, "rows")],
        [((share, model), BF16)],
    )
    tokens_grad = in_place(here, blocks_by_ring(grad_tokens, "tensor"), model, F32)

    quarter = sum(part.astype(F32) for part in quarters).astype(BF16)
    terms = lax.all_gather(quarter, everyone, axis=0, tiled=False)
    sequences = lax.axis_size("weights")
    terms = terms.reshape(sequences, 4, rank, -1)
    cuts = (0, model, model + hidden_units, 2 * model + hidden_units)
    sums = totals(
        picks, terms, cuts, adapters, rank, model, features, hidden_units, heads
    )
    flip = lambda array: jnp.swapaxes(array, -1, -2)
    return (
        block_out,
        tokens_grad,
        flip(sums[0]),
        sums[1],
        sums[2],
        flip(sums[3]),
        sums[4],
        flip(sums[5]),
        sums[6],
        flip(sums[7]),
        sums[8],
    )


def solution(mesh):
    rows = P(("weights", "context"), None)
    return jax.shard_map(
        on_device,
        mesh=mesh,
        in_specs=(
            rows,
            rows,
            P("weights", None),
            P("weights"),
            P(),
            P(),
            P(),
            P(None, None, "tensor"),
            P(("weights", "context"), "tensor"),
            P(("weights", "context"), "tensor"),
            P(("weights", "context"), "tensor"),
            P(("weights", "context"), "tensor"),
            P("tensor", ("weights", "context")),
            P(("weights", "context"), "tensor"),
            P(("weights", "context"), "tensor"),
            P("tensor", ("weights", "context")),
            P(),
            P(None, None, None, "tensor"),
            P(None, None, "tensor"),
            P(None, "tensor", None),
            P(),
            P(),
            P(None, None, None, "tensor"),
            P(None, "tensor", None),
            P(),
        ),
        out_specs=(
            rows,
            rows,
            P(),
            P(None, None, None, "tensor"),
            P(None, None, "tensor"),
            P(None, "tensor", None),
            P(),
            P(),
            P(None, None, None, "tensor"),
            P(None, "tensor", None),
            P(),
        ),
        check_vma=False,
    )
```

time: 568 us -> 393 us (0.69)
  the two profiles are of different devices: /device:TPU:120 before, /device:TPU:28 now
where the time goes in v2:
time: 393 us; the launch traced here: 386 us
  waiting for transfers between devices  117 us (30%)
  Pallas kernels  84.4 us (21%)
  starting transfers between devices  67.8 us (17%)
  local copies, waits for them, and re-layouts  49.4 us (13%)
  matrix products  44.1 us (11%)
  between operations  15.9 us (4%)
  other arithmetic  7.12 us (2%)
    ppermute x38, waiting for transfers between devices, shifted(): return lax.ppermute(block, axis, route)  72.9 us
    ppermute x38, starting transfers between devices, shifted(): return lax.ppermute(block, axis, route)  58.6 us
    all_gather x1, waiting for transfers between devices, on_device(): mixer_all = lax.all_gather(mixer_pack, everyone, axis=0, tiled=True)  38.4 us
    unnamed x155, local copies, waits for them, and re-layouts  24.4 us
    dot_general x6, matrix products, dot_nt(): lax.dot_general(left, right, (((1,), (1,)), ((), ())), preferred_element_...  21.4 us
    dot_general x4, matrix products, dot(): return jnp.dot(left, right, preferred_element_type=F32)  19.6 us
    pallas_call x2, Pallas kernels, ffn_rows(): pl.pallas_call(functools.partial(ffn_kernel, strip=512), in_specs=[pl.Blo...  19.3 us
    pallas_call x1, Pallas kernels, delta_back(): pl.pallas_call(functools.partial(delta_back_kernel, span=span, heads=head...  14 us
  transfers between devices with their start and end apart: 48, of which 21 were waited for; matrix products, arithmetic and copies ran while one was open for 19% of the time, Pallas kernels for 17%

profile of v2, /device:TPU:28, one launch (start us, length us, event | category | flops | bytes accessed | tf_op | source)
XLA Modules:
  0.0 385.6 jit_solution(10317670943514133972)
XLA Ops:
  13.4 3.1 collective-permute-start
  19.2 2.4 convolution_convert_fusion.3
  26.4 2.5 fusion.56
  28.9 38.4 %all-gather.5.cloned.1.call-done = bf16[2048,2176]{1,0:T(8,128)(2,1)} async-done(((bf16[64,2176]{1,0:T(8,128)(2,1)}), bf16[2048,2176]{1,0:T(8,128)(2,1)}) %all-gather.5.cloned.1.call-update) | async-done | bytes 8912912 | tf_op jit(solution)/shard_map/all_gather | solution.py:928
  67.3 8.5 %fusion.15.q_ref.k_ref.v_ref.logit_ref = f32[520,1664]{1,0:T(8,128)S(1)} fusion(f32[520,1664]{1,0:T(8,128)} %fusion.56, bf16[520,2048]{1,0:T(8,128)(2,1)} %copy-done.53, bf16[2048,2176]{1,0:T(8,128)(2,1)} %all-gather.5.cloned.1.call-done), kind=kOutput, calls=%fused_computation.17 | convolution fusion | flops 3545052160 | bytes 15867904 | tf_op jit(solution)/shard_map/dot_general | solution.py:842
  76.0 9.9 %delta_local.1 = (bf16[512,512]{1,0:T(8,128)(2,1)S(1)}, f32[512,512]{1,0:T(8,128)S(1)}, bf16[4,128,128]{2,1,0:T(8,128)(2,1)S(1)}, bf16[4,128,128]{2,1,0:T(8,128)...) custom-call(f32[520,1664]{1,0:T(8,128)S(1)} %fusion.15.q_ref.k_ref.v, ...), custom_call_target="tpu_custom_call" | custom-call | tf_op jit(solution)/shard_map/delta_local/pallas_call | solution.py:181
  87.7 3.3 collective-permute-start.1
  92.7 3.1 collective-permute-done.1.one_ref
  99.6 3.5 collective-permute-done.2.two_ref
  103.1 4.4 %attend.1 = (bf16[512,512]{1,0:T(8,128)(2,1)S(1)}, f32[512,512]{1,0:T(8,128)S(1)}, bf16[4,128,128]{2,1,0:T(8,128)(2,1)S(1)}, bf16[128,2176]{1,0:T(8,128)(2,1)S(1...) custom-call(s32[1]{0:T(128)} %bitcast.14.position_ref.place_ref, ...), custom_call_target="tpu_custom_call" | custom-call | tf_op jit(solution)/shard_map/attend/pallas_call | solution.py:239
  111.2 2.4 collective-permute-start.6
  124.3 2.3 collective-permute-done.5.one_ref
  128.7 9.5 %collective-permute-done.7.three_ref = bf16[128,2176]{1,0:T(8,128)(2,1)} collective-permute-done((bf16[128,2176]{1,0:T(8,128)(2,1)}, bf16[128,2176]{1,0:T(8,128)(2,1)}, u32[]{:S(2)}, u32[]{:S(2)}) %collective-permute-start.7) | collective-permute-done | bytes 557088 | tf_op jit(solution)/shard_map/ppermute | solution.py:807
  138.2 4.2 %middle_rows.1 = (f32[128,2048]{1,0:T(8,128)}, bf16[128,2176]{1,0:T(8,128)(2,1)}, bf16[128,128]{1,0:T(8,128)(2,1)}) custom-call(s32[1]{0:T(128)} %bitcast.place_ref, bf16[128,2176]{1,0:T(8,128)(2,1)} %copy-done.33, bf16[128,2176]{1,0:T(8,128)(2,1)} %collective-permute-done.5.one_ref, bf16[128,2176]{1,0:T(8,128)(2,1)} %collective-permute-done.6.two_ref, ...), custom_call_target="tpu_custom_call" | custom-call | tf_op jit(solution)/shard_map/middle_rows/pallas_call | solution.py:547
  144.4 6.5 %fusion.12 = f32[512,1408]{1,0:T(8,128)S(1)} fusion(bf16[512,2048]{1,0:T(8,128)(2,1)} %cot_ref.3, bf16[2048,4224]{1,0:T(8,128)(2,1)} %all-gather.7.cloned.1.call-done), kind=kOutput, calls=%fused_computation.16 | convolution fusion | flops 2952790016 | bytes 10747904 | tf_op jit(solution)/shard_map/dot_general | solution.py:842
  153.0 4.3 %collective-permute-done.8.x_second.x3 = bf16[128,2176]{1,0:T(8,128)(2,1)} collective-permute-done((bf16[128,2176]{1,0:T(8,128)(2,1)}, bf16[128,2176]{1,0:T(8,128)(2,1)}, u32[]{:S(2)}, u32[]{:S(2)}) %collective-permute-start.8) | collective-permute-done | bytes 557088 | tf_op jit(solution)/shard_map/ppermute | solution.py:807
  161.2 2.8 collective-permute-start.11
  164.9 10.1 %ffn_rows.3 = (bf16[256,1408]{1,0:T(8,128)(2,1)S(1)}, bf16[128,2176]{1,0:T(8,128)(2,1)}, bf16[128,2176]{1,0:T(8,128)(2,1)}, f32[32,2816]{1,0:T(8,128)S(1)}, f32[16,1408]{1,0:T(8,128)S(1)}) custom-call(s32[2]{0:T(128)S(1)} %pad_add_fusion.1.place_ref, bf16[128,2176]{1,0:T(8,128)(2,1)} %collective-permute-done.9.x_first.x1, ...), custom_call_target="tpu_custom_call" | custom-call | flops 6274678784 | bytes 12255232 | tf_op jit(solution)/shard_map/ffn_rows/pallas_call | solution.py:673
  175.2 2.1 collective-permute-start.14
  177.4 9.2 %ffn_rows.2 = (bf16[256,1408]{1,0:T(8,128)(2,1)S(1)}, bf16[128,2176]{1,0:T(8,128)(2,1)}, f32[128,2176]{1,0:T(8,128)S(1)}, f32[32,2816]{1,0:T(8,128)S(1)}, f32[16,1408]{1,0:T(8,128)S(1)}) custom-call(s32[2]{0:T(128)S(1)} %pad_add_fusion.place_ref, bf16[128,2176]{1,0:T(8,128)(2,1)S(1)} %constant_dynamic-update-slice_fusion.x_first.x2, ...), custom_call_target="tpu_custom_call" | custom-call | flops 6274678784 | bytes 12255232 | tf_op jit(solution)/shard_map/ffn_rows/pallas_call | solution.py:673
  190.1 6.0 %fusion.21 = bf16[512,2048]{1,0:T(8,128)(2,1)} fusion(bf16[512,1408]{1,0:T(8,128)(2,1)} %in_place.3, bf16[2048,4224]{1,0:T(8,128)(2,1)S(1)} %copy-done.55), kind=kOutput, calls=%fused_computation.19 | convolution fusion | flops 2953838592 | bytes 9306112 | tf_op jit(solution)/shard_map/dot_general | solution.py:846
  196.1 4.9 %collective-permute-done.13.two_ref = bf16[128,2176]{1,0:T(8,128)(2,1)} collective-permute-done((bf16[128,2176]{1,0:T(8,128)(2,1)}, bf16[128,2176]{1,0:T(8,128)(2,1)}, u32[]{:S(2)}, u32[]{:S(2)}) %collective-permute-start.13) | collective-permute-done | bytes 557088 | tf_op jit(solution)/shard_map/ppermute | solution.py:807
  201.0 4.4 %back_rows.1 = (f32[128,2048]{1,0:T(8,128)}, bf16[128,2176]{1,0:T(8,128)(2,1)}) custom-call(s32[1]{0:T(128)} %bitcast.place_ref, f32[128,2176]{1,0:T(8,128)} %copy-done.17, bf16[128,2176]{1,0:T(8,128)(2,1)} %collective-permute-done.12.one_ref, bf16[128,2176]{1,0:T(8,128)(2,1)} %collective-permute-done.13.two_ref, ...), custom_call_target="tpu_custom_call" | custom-call | tf_op jit(solution)/shard_map/back_rows/pallas_call | solution.py:547
  205.8 2.9 collective-permute-start.17
  208.7 9.7 %collective-permute-done.15.refs_1_.g1 = bf16[128,2176]{1,0:T(8,128)(2,1)S(1)} collective-permute-done((bf16[128,2176]{1,0:T(8,128)(2,1)}, bf16[128,2176]{1,0:T(8,128)(2,1)S(1)}, u32[]{:S(2)}, u32[]{:S(2)}) %collective-permute-start.15) | collective-permute-done | bytes 557088 | tf_op jit(solution)/shard_map/ppermute | solution.py:807
  218.6 3.3 collective-permute-start.18
  221.9 4.4 %collective-permute-done.16 = bf16[64,2176]{1,0:T(8,128)(2,1)S(1)} collective-permute-done((bf16[64,2176]{1,0:T(8,128)(2,1)S(1)}, bf16[64,2176]{1,0:T(8,128)(2,1)S(1)}, u32[]{:S(2)}, u32[]{:S(2)}) %collective-permute-start.16) | collective-permute-done | bytes 278560 | tf_op jit(solution)/shard_map/ppermute | solution.py:807
  227.6 2.2 attend_back.1
  232.2 3.3 collective-permute-start.19
  237.3 2.1 collective-permute-done.19.one_ref
  239.4 3.3 collective-permute-start.26
  245.4 3.1 collective-permute-start.20
  260.3 14.0 %delta_back.1 = (bf16[512,1664]{1,0:T(8,128)(2,1)S(1)}, f32[8,1536]{1,0:T(8,128)}, f32[8,1536]{1,0:T(8,128)S(1)}) custom-call(f32[512,512]{1,0:T(8,128)S(1)} %copy-done.23, f32[512,512]{1,0:T(8,128)S(1)} %copy-done.25, f32[512,512]{1,0:T(8,128)S(1)} %copy-done.27, f32[520,1664]{1,0:T(8,128)S(1)} %fusion.15.q_ref.k_ref.v_ref.logit_ref, ...), custom_call_target="tpu_custom_call" | custom-call | tf_op jit(solution)/shard_map/delta_back/pallas_call | solution.py:441
  275.5 3.2 collective-permute-start.23
  285.1 2.3 convolution_convert_fusion.1.p0
  287.4 2.1 collective-permute-start.27
  292.7 5.8 %early_terms.1.early_ref = bf16[4,16,3456]{2,1,0:T(8,128)(2,1)} custom-call(s32[1]{0:T(128)} %bitcast.place_ref, bf16[128,2176]{1,0:T(8,128)(2,1)} %get-tuple-element.128.refs_0_.g0, bf16[128,2176]{1,0:T(8,128)(2,1)} %copy-done.4, bf16[128,2176]{1,0:T(8,128)(2,1)} %copy-done.6, bf16[128,2176]{1,0:T(8,128)(2,1)} %copy-done.5, ...), custom_call_target="tpu_custom_call" | custom-call | tf_op jit(solution)/shard_map/early_terms/pallas_call | solution.py:619
  300.5 4.0 %collective-permute-start.35 = (bf16[16,6016]{1,0:T(8,128)(2,1)S(1)}, bf16[16,6016]{1,0:T(8,128)(2,1)S(1)}, u32[]{:S(2)}, u32[]{:S(2)}) collective-permute-start(bf16[16,6016]{1,0:T(8,128)(2,1)S(1)} %get-tuple-element.156), channel_id=1, source_target_pairs={{0,8},{4,12},{8,0},{12,4},{1,9},{5,13},{9,1},{13,5},{2,10},{6,14},... | collective-permute-start | bytes 577544 | tf_op jit(solution)/shard_map/ppermute | solution.py:807
  304.5 2.5 collective-permute-start.36
  307.0 8.1 %fusion.18 = bf16[512,2048]{1,0:T(8,128)(2,1)} fusion(bf16[512,1664]{1,0:T(8,128)(2,1)S(1)} %copy-done.15, bf16[2048,2176]{1,0:T(8,128)(2,1)} %all-gather.5.cloned.1.call-done), kind=kOutput, calls=%fused_computation.18 | convolution fusion | flops 3490709504 | bytes 10616832 | tf_op jit(solution)/shard_map/dot_general | solution.py:846
  316.0 2.6 constant_dynamic-slice_fusion.2
  321.7 6.0 %collective-permute-done.37.one_ref = bf16[128,2048]{1,0:T(8,128)(2,1)S(1)} collective-permute-done((bf16[128,2048]{1,0:T(8,128)(2,1)S(1)}, bf16[128,2048]{1,0:T(8,128)(2,1)S(1)}, u32[]{:S(2)}, u32[]{:S(2)}) %collective-permute-start.37) | collective-permute-done | bytes 524320 | tf_op jit(solution)/shard_map/ppermute | solution.py:807
  327.7 2.9 collective-permute-done.38.two_ref
  330.6 11.0 %collective-permute-done.39.three_ref = bf16[128,2048]{1,0:T(8,128)(2,1)S(1)} collective-permute-done((bf16[128,2048]{1,0:T(8,128)(2,1)S(1)}, bf16[128,2048]{1,0:T(8,128)(2,1)S(1)}, u32[]{:S(2)}, u32[]{:S(2)}) %collective-permute-start.39) | collective-permute-done | bytes 524320 | tf_op jit(solution)/shard_map/ppermute | solution.py:807
  342.5 3.4 token_rows.1.refs_0_
  351.2 4.0 %collective-permute-done.42.refs_3_ = bf16[128,2048]{1,0:T(8,128)(2,1)S(1)} collective-permute-done((bf16[128,2048]{1,0:T(8,128)(2,1)}, bf16[128,2048]{1,0:T(8,128)(2,1)S(1)}, u32[]{:S(2)}, u32[]{:S(2)}) %collective-permute-start.42) | collective-permute-done | bytes 524320 | tf_op jit(solution)/shard_map/ppermute | solution.py:807
  364.8 2.5 in_place.5
  367.3 10.0 %totals.1 = (f32[4,8,16,2048]{3,2,1,0:T(8,128)}, f32[3,8,16,512]{3,2,1,0:T(8,128)}, f32[8,16,4]{2,1,0:T(8,128)}, f32[8,16,512]{2,1,0:T(8,128)}, f32[8,16,2048]{2...) custom-call(s32[8]{0:T(128)} %convert_reduce_fusion.pick_ref, ...), custom_call_target="tpu_custom_call" | custom-call | tf_op jit(solution)/shard_map/totals/pallas_call | solution.py:774
  (290 shorter events, 103.1 us)
Async XLA Ops:
  7.2 60.1 %all-gather.5.cloned.1.call-start = ((), (), s32[]{:S(2)}) async-start(), calls=%async_computation.1 | async-start | bytes 9191424 | tf_op jit(solution)/shard_map/all_gather | solution.py:928
  10.6 133.8 %all-gather.7.cloned.1.call-start = ((), (), s32[]{:S(2)}) async-start(), calls=%async_computation.2 | async-start | bytes 17842176 | tf_op jit(solution)/shard_map/all_gather | solution.py:929
  12.6 266.1 %reduce-scatter.2.cloned.1.call-start = ((), (), s32[]{:S(2)}) async-start(), calls=%async_computation.3 | async-start | bytes 2621440 | tf_op jit(solution)/shard_map/reduce_scatter | solution.py:1053
  13.4 10.0 %collective-permute-start = (bf16[8,2048]{1,0:T(8,128)(2,1)S(1)}, bf16[8,2048]{1,0:T(8,128)(2,1)S(1)}, u32[]{:S(2)}, u32[]{:S(2)}) collective-permute-start(bf16[8,2048]{1,0:T(8,128)(2,1)S(1)} %slice.84), channel_id=1, source_target_pairs={{0,4},{4,8},{8,12},{1,5},{5,9},{9,13},{2,6},{6,10},{10,14},{3,7},{... | collective-permute-start | bytes 98312 | tf_op jit(solution)/shard_map/ppermute | solution.py:807
  87.7 8.2 %collective-permute-start.1 = (bf16[4,128,128]{2,1,0:T(8,128)(2,1)S(1)}, bf16[4,128,128]{2,1,0:T(8,128)(2,1)S(1)}, u32[]{:S(2)}, u32[]{:S(2)}) collective-permute-start(bf16[4,128,128]{2,1,0:T(8,128)(2,1)S(1)} %get-tuple-element.102), channel_id=1, source_target_pairs={{0,4},{4,8},{8,12},{1,5},{5,9},{9,13},{2,6},{6,10},{10,14},{3,7},{... | collective-permute-start | bytes 393224 | tf_op jit(solution)/shard_map/ppermute | solution.py:807
  91.1 8.5 %collective-permute-start.3 = (bf16[4,128,128]{2,1,0:T(8,128)(2,1)S(1)}, bf16[4,128,128]{2,1,0:T(8,128)(2,1)S(1)}, u32[]{:S(2)}, u32[]{:S(2)}) collective-permute-start(bf16[4,128,128]{2,1,0:T(8,128)(2,1)S(1)} %get-tuple-element.103), channel_id=1, source_target_pairs={{8,12},{9,13},{10,14},{11,15},{24,28},{25,29},{26,30},{27,31},{40,... | collective-permute-start | bytes 393224 | tf_op jit(solution)/shard_map/ppermute | solution.py:993
  96.0 7.1 %collective-permute-start.2 = (bf16[4,128,128]{2,1,0:T(8,128)(2,1)S(1)}, bf16[4,128,128]{2,1,0:T(8,128)(2,1)S(1)}, u32[]{:S(2)}, u32[]{:S(2)}) collective-permute-start(bf16[4,128,128]{2,1,0:T(8,128)(2,1)S(1)} %add_convert_fusion.2), channel_id=1, source_target_pairs={{4,8},{5,9},{6,10},{7,11},{20,24},{21,25},{22,26},{23,27},{36,40},... | collective-permute-start | bytes 393224 | tf_op jit(solution)/shard_map/ppermute | solution.py:1000
  97.3 5.8 %collective-permute-start.4 = (bf16[4,128,128]{2,1,0:T(8,128)(2,1)S(1)}, bf16[4,128,128]{2,1,0:T(8,128)(2,1)S(1)}, u32[]{:S(2)}, u32[]{:S(2)}) collective-permute-start(bf16[4,128,128]{2,1,0:T(8,128)(2,1)S(1)} %add_convert_fusion.2), channel_id=1, source_target_pairs={{4,12},{5,13},{6,14},{7,15},{20,28},{21,29},{22,30},{23,31},{36,44... | collective-permute-start | bytes 393224 | tf_op jit(solution)/shard_map/ppermute | solution.py:1001
  110.7 15.9 %collective-permute-start.5 = (bf16[128,2176]{1,0:T(8,128)(2,1)}, bf16[128,2176]{1,0:T(8,128)(2,1)}, u32[]{:S(2)}, u32[]{:S(2)}) collective-permute-start(bf16[128,2176]{1,0:T(8,128)(2,1)} %get-tuple-element.109), channel_id=1, source_target_pairs={{0,1},{1,2},{2,3},{3,0},{4,5},{5,6},{6,7},{7,4},{8,9},{9,10},{10,1... | collective-permute-start | bytes 1671176 | tf_op jit(solution)/shard_map/ppermute | solution.py:807
  111.2 17.4 %collective-permute-start.6 = (bf16[128,2176]{1,0:T(8,128)(2,1)}, bf16[128,2176]{1,0:T(8,128)(2,1)}, u32[]{:S(2)}, u32[]{:S(2)}) collective-permute-start(bf16[128,2176]{1,0:T(8,128)(2,1)} %get-tuple-element.110), channel_id=1, source_target_pairs={{0,2},{1,3},{2,0},{3,1},{4,6},{5,7},{6,4},{7,5},{8,10},{9,11},{10,... | collective-permute-start | bytes 1671176 | tf_op jit(solution)/shard_map/ppermute | solution.py:807
  113.7 24.5 %collective-permute-start.7 = (bf16[128,2176]{1,0:T(8,128)(2,1)}, bf16[128,2176]{1,0:T(8,128)(2,1)}, u32[]{:S(2)}, u32[]{:S(2)}) collective-permute-start(bf16[128,2176]{1,0:T(8,128)(2,1)} %get-tuple-element.111), channel_id=1, source_target_pairs={{0,3},{1,0},{2,1},{3,2},{4,7},{5,4},{6,5},{7,6},{8,11},{9,8},{10,9... | collective-permute-start | bytes 1671176 | tf_op jit(solution)/shard_map/ppermute | solution.py:807
  142.4 15.0 %collective-permute-start.8 = (bf16[128,2176]{1,0:T(8,128)(2,1)}, bf16[128,2176]{1,0:T(8,128)(2,1)}, u32[]{:S(2)}, u32[]{:S(2)}) collective-permute-start(bf16[128,2176]{1,0:T(8,128)(2,1)} %get-tuple-element.112.x_second.x0), channel_id=1, source_target_pairs={{0,1},{1,2},{2,3},{3,0},{4,5},{5,6},{6,7},{7,4},{8,9},{9,10},{10,1... | collective-permute-start | bytes 1671176 | tf_op jit(solution)/shard_map/ppermute | solution.py:807
  143.5 15.1 %collective-permute-start.9 = (bf16[128,2176]{1,0:T(8,128)(2,1)}, bf16[128,2176]{1,0:T(8,128)(2,1)}, u32[]{:S(2)}, u32[]{:S(2)}) collective-permute-start(bf16[128,2176]{1,0:T(8,128)(2,1)} %get-tuple-element.112.x_second.x0), channel_id=1, source_target_pairs={{0,3},{1,0},{2,1},{3,2},{4,7},{5,4},{6,5},{7,6},{8,11},{9,8},{10,9... | collective-permute-start | bytes 1671176 | tf_op jit(solution)/shard_map/ppermute | solution.py:807
  159.6 17.7 %collective-permute-start.10 = (bf16[64,2176]{1,0:T(8,128)(2,1)S(1)}, bf16[64,2176]{1,0:T(8,128)(2,1)S(1)}, u32[]{:S(2)}, u32[]{:S(2)}) collective-permute-start(bf16[64,2176]{1,0:T(8,128)(2,1)S(1)} %slice.92), channel_id=1, source_target_pairs={{0,3},{1,0},{2,1},{3,2},{4,7},{5,4},{6,5},{7,6},{8,11},{9,8},{10,9... | collective-permute-start | bytes 835592 | tf_op jit(solution)/shard_map/ppermute | solution.py:807
  161.2 16.2 %collective-permute-start.11 = (bf16[64,2176]{1,0:T(8,128)(2,1)S(1)}, bf16[64,2176]{1,0:T(8,128)(2,1)S(1)}, u32[]{:S(2)}, u32[]{:S(2)}) collective-permute-start(bf16[64,2176]{1,0:T(8,128)(2,1)S(1)} %slice.93), channel_id=1, source_target_pairs={{0,1},{1,2},{2,3},{3,0},{4,5},{5,6},{6,7},{7,4},{8,9},{9,10},{10,1... | collective-permute-start | bytes 835592 | tf_op jit(solution)/shard_map/ppermute | solution.py:807
  175.0 21.1 %collective-permute-start.12 = (bf16[128,2176]{1,0:T(8,128)(2,1)}, bf16[128,2176]{1,0:T(8,128)(2,1)}, u32[]{:S(2)}, u32[]{:S(2)}) collective-permute-start(bf16[128,2176]{1,0:T(8,128)(2,1)} %get-tuple-element.117), channel_id=1, source_target_pairs={{0,1},{1,2},{2,3},{3,0},{4,5},{5,6},{6,7},{7,4},{8,9},{9,10},{10,1... | collective-permute-start | bytes 1671176 | tf_op jit(solution)/shard_map/ppermute | solution.py:807
  175.2 20.9 %collective-permute-start.14 = (bf16[128,2176]{1,0:T(8,128)(2,1)}, bf16[128,2176]{1,0:T(8,128)(2,1)}, u32[]{:S(2)}, u32[]{:S(2)}) collective-permute-start(bf16[128,2176]{1,0:T(8,128)(2,1)} %get-tuple-element.119), channel_id=1, source_target_pairs={{0,3},{1,0},{2,1},{3,2},{4,7},{5,4},{6,5},{7,6},{8,11},{9,8},{10,9... | collective-permute-start | bytes 1671176 | tf_op jit(solution)/shard_map/ppermute | solution.py:807
  187.7 13.4 %collective-permute-start.13 = (bf16[128,2176]{1,0:T(8,128)(2,1)}, bf16[128,2176]{1,0:T(8,128)(2,1)}, u32[]{:S(2)}, u32[]{:S(2)}) collective-permute-start(bf16[128,2176]{1,0:T(8,128)(2,1)} %get-tuple-element.118), channel_id=1, source_target_pairs={{0,2},{1,3},{2,0},{3,1},{4,6},{5,7},{6,4},{7,5},{8,10},{9,11},{10,... | collective-permute-start | bytes 1671176 | tf_op jit(solution)/shard_map/ppermute | solution.py:807
  205.4 13.0 %collective-permute-start.15 = (bf16[128,2176]{1,0:T(8,128)(2,1)}, bf16[128,2176]{1,0:T(8,128)(2,1)S(1)}, u32[]{:S(2)}, u32[]{:S(2)}) collective-permute-start(bf16[128,2176]{1,0:T(8,128)(2,1)} %get-tuple-element.128.refs_0_.g0), channel_id=1, source_target_pairs={{0,3},{1,0},{2,1},{3,2},{4,7},{5,4},{6,5},{7,6},{8,11},{9,8},{10,9... | collective-permute-start | bytes 1671176 | tf_op jit(solution)/shard_map/ppermute | solution.py:807
  205.8 12.7 %collective-permute-start.17 = (bf16[128,2176]{1,0:T(8,128)(2,1)}, bf16[128,2176]{1,0:T(8,128)(2,1)S(1)}, u32[]{:S(2)}, u32[]{:S(2)}) collective-permute-start(bf16[128,2176]{1,0:T(8,128)(2,1)} %get-tuple-element.128.refs_0_.g0), channel_id=1, source_target_pairs={{0,1},{1,2},{2,3},{3,0},{4,5},{5,6},{6,7},{7,4},{8,9},{9,10},{10,1... | collective-permute-start | bytes 1671176 | tf_op jit(solution)/shard_map/ppermute | solution.py:807
  218.4 7.8 %collective-permute-start.16 = (bf16[64,2176]{1,0:T(8,128)(2,1)S(1)}, bf16[64,2176]{1,0:T(8,128)(2,1)S(1)}, u32[]{:S(2)}, u32[]{:S(2)}) collective-permute-start(bf16[64,2176]{1,0:T(8,128)(2,1)S(1)} %slice.114), channel_id=1, source_target_pairs={{0,3},{1,0},{2,1},{3,2},{4,7},{5,4},{6,5},{7,6},{8,11},{9,8},{10,9... | collective-permute-start | bytes 835592 | tf_op jit(solution)/shard_map/ppermute | solution.py:807
  218.6 7.7 %collective-permute-start.18 = (bf16[64,2176]{1,0:T(8,128)(2,1)S(1)}, bf16[64,2176]{1,0:T(8,128)(2,1)S(1)}, u32[]{:S(2)}, u32[]{:S(2)}) collective-permute-start(bf16[64,2176]{1,0:T(8,128)(2,1)S(1)} %slice.115), channel_id=1, source_target_pairs={{0,1},{1,2},{2,3},{3,0},{4,5},{5,6},{6,7},{7,4},{8,9},{9,10},{10,1... | collective-permute-start | bytes 835592 | tf_op jit(solution)/shard_map/ppermute | solution.py:807
  231.3 135.9 %all-gather.9.cloned.1.call-start = ((), (), s32[]{:S(2)}) async-start(), calls=%async_computation.4 | async-start | bytes 6352896 | tf_op jit(solution)/shard_map/all_gather | solution.py:1121
  231.4 18.9 %collective-permute-start.21 = (bf16[4,128,128]{2,1,0:T(8,128)(2,1)}, bf16[4,128,128]{2,1,0:T(8,128)(2,1)S(1)}, u32[]{:S(2)}, u32[]{:S(2)}) collective-permute-start(bf16[4,128,128]{2,1,0:T(8,128)(2,1)} %copy-done.41), channel_id=1, source_target_pairs={{4,0},{5,1},{6,2},{7,3},{20,16},{21,17},{22,18},{23,19},{36,32},{3... | collective-permute-start | bytes 393224 | tf_op jit(solution)/shard_map/ppermute | solution.py:1006
  232.2 7.2 %collective-permute-start.19 = (bf16[4,128,128]{2,1,0:T(8,128)(2,1)}, bf16[4,128,128]{2,1,0:T(8,128)(2,1)S(1)}, u32[]{:S(2)}, u32[]{:S(2)}) collective-permute-start(bf16[4,128,128]{2,1,0:T(8,128)(2,1)} %copy-done.48), channel_id=1, source_target_pairs={{4,0},{8,4},{12,8},{5,1},{9,5},{13,9},{6,2},{10,6},{14,10},{7,3},{... | collective-permute-start | bytes 393224 | tf_op jit(solution)/shard_map/ppermute | solution.py:807
  239.4 9.1 %collective-permute-start.26 = (bf16[16,512]{1,0:T(8,128)(2,1)S(1)}, bf16[16,512]{1,0:T(8,128)(2,1)S(1)}, u32[]{:S(2)}, u32[]{:S(2)}) collective-permute-start(bf16[16,512]{1,0:T(8,128)(2,1)S(1)} %convolution_convert_fusion.2), channel_id=1, source_target_pairs={{0,1},{1,2},{2,3},{3,0},{4,5},{5,6},{6,7},{7,4},{8,9},{9,10},{10,1... | collective-permute-start | bytes 49160 | tf_op jit(solution)/shard_map/ppermute | solution.py:807
  242.7 7.5 %collective-permute-start.25 = (bf16[16,512]{1,0:T(8,128)(2,1)S(1)}, bf16[16,512]{1,0:T(8,128)(2,1)S(1)}, u32[]{:S(2)}, u32[]{:S(2)}) collective-permute-start(bf16[16,512]{1,0:T(8,128)(2,1)S(1)} %convolution_convert_fusion.2), channel_id=1, source_target_pairs={{0,3},{1,0},{2,1},{3,2},{4,7},{5,4},{6,5},{7,6},{8,11},{9,8},{10,9... | collective-permute-start | bytes 49160 | tf_op jit(solution)/shard_map/ppermute | solution.py:807
  242.7 7.5 %collective-permute-start.24 = (bf16[16,512]{1,0:T(8,128)(2,1)S(1)}, bf16[16,512]{1,0:T(8,128)(2,1)S(1)}, u32[]{:S(2)}, u32[]{:S(2)}) collective-permute-start(bf16[16,512]{1,0:T(8,128)(2,1)S(1)} %convolution_convert_fusion.2), channel_id=1, source_target_pairs={{0,2},{1,3},{2,0},{3,1},{4,6},{5,7},{6,4},{7,5},{8,10},{9,11},{10,... | collective-permute-start | bytes 49160 | tf_op jit(solution)/shard_map/ppermute | solution.py:807
  245.4 5.6 %collective-permute-start.20 = (bf16[4,128,128]{2,1,0:T(8,128)(2,1)S(1)}, bf16[4,128,128]{2,1,0:T(8,128)(2,1)S(1)}, u32[]{:S(2)}, u32[]{:S(2)}) collective-permute-start(bf16[4,128,128]{2,1,0:T(8,128)(2,1)S(1)} %fusion.25), channel_id=1, source_target_pairs={{8,4},{9,5},{10,6},{11,7},{24,20},{25,21},{26,22},{27,23},{40,36},... | collective-permute-start | bytes 393224 | tf_op jit(solution)/shard_map/ppermute | solution.py:1060
  248.6 3.8 collective-permute-start.22
  275.5 6.3 %collective-permute-start.23 = (f32[8,1536]{1,0:T(8,128)}, f32[8,1536]{1,0:T(8,128)S(1)}, u32[]{:S(2)}, u32[]{:S(2)}) collective-permute-start(f32[8,1536]{1,0:T(8,128)} %get-tuple-element.135), channel_id=1, source_target_pairs={{4,0},{8,4},{12,8},{5,1},{9,5},{13,9},{6,2},{10,6},{14,10},{7,3},{... | collective-permute-start | bytes 147464 | tf_op jit(solution)/shard_map/ppermute | solution.py:807
  281.8 16.7 %collective-permute-start.30 = (bf16[128,2048]{1,0:T(8,128)(2,1)S(1)}, bf16[128,2048]{1,0:T(8,128)(2,1)S(1)}, u32[]{:S(2)}, u32[]{:S(2)}) collective-permute-start(bf16[128,2048]{1,0:T(8,128)(2,1)S(1)} %add_convert_fusion.refs_0_), channel_id=1, source_target_pairs={{0,1},{1,2},{2,3},{3,0},{4,5},{5,6},{6,7},{7,4},{8,9},{9,10},{10,1... | collective-permute-start | bytes 1572872 | tf_op jit(solution)/shard_map/ppermute | solution.py:807
  283.5 15.0 %collective-permute-start.31 = (bf16[128,2048]{1,0:T(8,128)(2,1)S(1)}, bf16[128,2048]{1,0:T(8,128)(2,1)S(1)}, u32[]{:S(2)}, u32[]{:S(2)}) collective-permute-start(bf16[128,2048]{1,0:T(8,128)(2,1)S(1)} %add_convert_fusion.refs_0_), channel_id=1, source_target_pairs={{0,3},{1,0},{2,1},{3,2},{4,7},{5,4},{6,5},{7,6},{8,11},{9,8},{10,9... | collective-permute-start | bytes 1572872 | tf_op jit(solution)/shard_map/ppermute | solution.py:807
  287.4 11.1 %collective-permute-start.27 = (bf16[512,64]{1,0:T(8,128)(2,1)S(1)}, bf16[512,64]{1,0:T(8,128)(2,1)S(1)}, u32[]{:S(2)}, u32[]{:S(2)}) collective-permute-start(bf16[512,64]{1,0:T(8,128)(2,1)S(1)} %convolution_convert_fusion.1.p0), channel_id=1, source_target_pairs={{0,3},{1,0},{2,1},{3,2},{4,7},{5,4},{6,5},{7,6},{8,11},{9,8},{10,9... | collective-permute-start | bytes 196616 | tf_op jit(solution)/shard_map/ppermute | solution.py:807
  289.5 9.0 %collective-permute-start.28 = (bf16[512,64]{1,0:T(8,128)(2,1)S(1)}, bf16[512,64]{1,0:T(8,128)(2,1)S(1)}, u32[]{:S(2)}, u32[]{:S(2)}) collective-permute-start(bf16[512,64]{1,0:T(8,128)(2,1)S(1)} %convolution_convert_fusion.1.p0), channel_id=1, source_target_pairs={{0,2},{1,3},{2,0},{3,1},{4,6},{5,7},{6,4},{7,5},{8,10},{9,11},{10,... | collective-permute-start | bytes 196616 | tf_op jit(solution)/shard_map/ppermute | solution.py:807
  291.4 7.1 %collective-permute-start.29 = (bf16[512,64]{1,0:T(8,128)(2,1)S(1)}, bf16[512,64]{1,0:T(8,128)(2,1)S(1)}, u32[]{:S(2)}, u32[]{:S(2)}) collective-permute-start(bf16[512,64]{1,0:T(8,128)(2,1)S(1)} %convolution_convert_fusion.1.p0), channel_id=1, source_target_pairs={{0,1},{1,2},{2,3},{3,0},{4,5},{5,6},{6,7},{7,4},{8,9},{9,10},{10,1... | collective-permute-start | bytes 196616 | tf_op jit(solution)/shard_map/ppermute | solution.py:807
  300.4 14.7 %collective-permute-start.34 = (bf16[16,6016]{1,0:T(8,128)(2,1)S(1)}, bf16[16,6016]{1,0:T(8,128)(2,1)S(1)}, u32[]{:S(2)}, u32[]{:S(2)}) collective-permute-start(bf16[16,6016]{1,0:T(8,128)(2,1)S(1)} %get-tuple-element.155), channel_id=1, source_target_pairs={{0,4},{4,8},{8,12},{12,0},{1,5},{5,9},{9,13},{13,1},{2,6},{6,10},{... | collective-permute-start | bytes 577544 | tf_op jit(solution)/shard_map/ppermute | solution.py:807
  300.5 14.6 %collective-permute-start.35 = (bf16[16,6016]{1,0:T(8,128)(2,1)S(1)}, bf16[16,6016]{1,0:T(8,128)(2,1)S(1)}, u32[]{:S(2)}, u32[]{:S(2)}) collective-permute-start(bf16[16,6016]{1,0:T(8,128)(2,1)S(1)} %get-tuple-element.156), channel_id=1, source_target_pairs={{0,8},{4,12},{8,0},{12,4},{1,9},{5,13},{9,1},{13,5},{2,10},{6,14},... | collective-permute-start | bytes 577544 | tf_op jit(solution)/shard_map/ppermute | solution.py:807
  304.5 10.6 %collective-permute-start.36 = (bf16[16,6016]{1,0:T(8,128)(2,1)S(1)}, bf16[16,6016]{1,0:T(8,128)(2,1)S(1)}, u32[]{:S(2)}, u32[]{:S(2)}) collective-permute-start(bf16[16,6016]{1,0:T(8,128)(2,1)S(1)} %get-tuple-element.157), channel_id=1, source_target_pairs={{0,12},{4,0},{8,4},{12,8},{1,13},{5,1},{9,5},{13,9},{2,14},{6,2},{... | collective-permute-start | bytes 577544 | tf_op jit(solution)/shard_map/ppermute | solution.py:807
  318.5 9.2 %collective-permute-start.37 = (bf16[128,2048]{1,0:T(8,128)(2,1)S(1)}, bf16[128,2048]{1,0:T(8,128)(2,1)S(1)}, u32[]{:S(2)}, u32[]{:S(2)}) collective-permute-start(bf16[128,2048]{1,0:T(8,128)(2,1)S(1)} %get-tuple-element.210), channel_id=1, source_target_pairs={{0,1},{1,2},{2,3},{3,0},{4,5},{5,6},{6,7},{7,4},{8,9},{9,10},{10,1... | collective-permute-start | bytes 1572872 | tf_op jit(solution)/shard_map/ppermute | solution.py:807
  319.9 10.8 %collective-permute-start.38 = (bf16[128,2048]{1,0:T(8,128)(2,1)S(1)}, bf16[128,2048]{1,0:T(8,128)(2,1)S(1)}, u32[]{:S(2)}, u32[]{:S(2)}) collective-permute-start(bf16[128,2048]{1,0:T(8,128)(2,1)S(1)} %get-tuple-element.209), channel_id=1, source_target_pairs={{0,2},{1,3},{2,0},{3,1},{4,6},{5,7},{6,4},{7,5},{8,10},{9,11},{10,... | collective-permute-start | bytes 1572872 | tf_op jit(solution)/shard_map/ppermute | solution.py:807
  321.7 20.0 %collective-permute-start.39 = (bf16[128,2048]{1,0:T(8,128)(2,1)S(1)}, bf16[128,2048]{1,0:T(8,128)(2,1)S(1)}, u32[]{:S(2)}, u32[]{:S(2)}) collective-permute-start(bf16[128,2048]{1,0:T(8,128)(2,1)S(1)} %get-tuple-element.208), channel_id=1, source_target_pairs={{0,3},{1,0},{2,1},{3,2},{4,7},{5,4},{6,5},{7,6},{8,11},{9,8},{10,9... | collective-permute-start | bytes 1572872 | tf_op jit(solution)/shard_map/ppermute | solution.py:807
  345.8 9.4 %collective-permute-start.42 = (bf16[128,2048]{1,0:T(8,128)(2,1)}, bf16[128,2048]{1,0:T(8,128)(2,1)S(1)}, u32[]{:S(2)}, u32[]{:S(2)}) collective-permute-start(bf16[128,2048]{1,0:T(8,128)(2,1)} %token_rows.1.refs_0_), channel_id=1, source_target_pairs={{0,1},{1,2},{2,3},{3,0},{4,5},{5,6},{6,7},{7,4},{8,9},{9,10},{10,1... | collective-permute-start | bytes 1572872 | tf_op jit(solution)/shard_map/ppermute | solution.py:807
  346.3 10.7 %collective-permute-start.40 = (bf16[128,2048]{1,0:T(8,128)(2,1)}, bf16[128,2048]{1,0:T(8,128)(2,1)S(1)}, u32[]{:S(2)}, u32[]{:S(2)}) collective-permute-start(bf16[128,2048]{1,0:T(8,128)(2,1)} %token_rows.1.refs_0_), channel_id=1, source_target_pairs={{0,3},{1,0},{2,1},{3,2},{4,7},{5,4},{6,5},{7,6},{8,11},{9,8},{10,9... | collective-permute-start | bytes 1572872 | tf_op jit(solution)/shard_map/ppermute | solution.py:807
  347.9 10.2 %collective-permute-start.33 = (bf16[64,2048]{1,0:T(8,128)(2,1)S(1)}, bf16[64,2048]{1,0:T(8,128)(2,1)S(1)}, u32[]{:S(2)}, u32[]{:S(2)}) collective-permute-start(bf16[64,2048]{1,0:T(8,128)(2,1)S(1)} %slice.104), channel_id=1, source_target_pairs={{0,1},{1,2},{2,3},{3,0},{4,5},{5,6},{6,7},{7,4},{8,9},{9,10},{10,1... | collective-permute-start | bytes 786440 | tf_op jit(solution)/shard_map/ppermute | solution.py:807
  349.7 10.2 %collective-permute-start.32 = (bf16[64,2048]{1,0:T(8,128)(2,1)S(1)}, bf16[64,2048]{1,0:T(8,128)(2,1)}, u32[]{:S(2)}, u32[]{:S(2)}) collective-permute-start(bf16[64,2048]{1,0:T(8,128)(2,1)S(1)} %slice.103), channel_id=1, source_target_pairs={{0,3},{1,0},{2,1},{3,2},{4,7},{5,4},{6,5},{7,6},{8,11},{9,8},{10,9... | collective-permute-start | bytes 786440 | tf_op jit(solution)/shard_map/ppermute | solution.py:807
  355.2 7.5 %collective-permute-start.43 = (bf16[64,2048]{1,0:T(8,128)(2,1)S(1)}, bf16[64,2048]{1,0:T(8,128)(2,1)S(1)}, u32[]{:S(2)}, u32[]{:S(2)}) collective-permute-start(bf16[64,2048]{1,0:T(8,128)(2,1)S(1)} %slice.119), channel_id=1, source_target_pairs={{0,1},{1,2},{2,3},{3,0},{4,5},{5,6},{6,7},{7,4},{8,9},{9,10},{10,1... | collective-permute-start | bytes 786440 | tf_op jit(solution)/shard_map/ppermute | solution.py:807
  357.1 7.7 %collective-permute-start.41 = (bf16[64,2048]{1,0:T(8,128)(2,1)S(1)}, bf16[64,2048]{1,0:T(8,128)(2,1)S(1)}, u32[]{:S(2)}, u32[]{:S(2)}) collective-permute-start(bf16[64,2048]{1,0:T(8,128)(2,1)S(1)} %slice.118), channel_id=1, source_target_pairs={{0,3},{1,0},{2,1},{3,2},{4,7},{5,4},{6,5},{7,6},{8,11},{9,8},{10,9... | collective-permute-start | bytes 786440 | tf_op jit(solution)/shard_map/ppermute | solution.py:807
  (75 other events, 568.2 us)
Sparse Core Ops, SparseCore 0:
  10.9 56.3 all-gather.4
  70.1 74.1 all-gather.6
  231.4 30.7 reduce-scatter.1
  316.1 48.7 all-gather.8

commit v3 on v2

--- a/solution.py
+++ b/solution.py
@@ -293,7 +293,7 @@
 def delta_back_kernel(
     zq_ref, zk_ref, zv_ref, logit_ref, taps_q, taps_k, taps_v, seg_ref, row_ref,
     inverse_ref, prefix_ref, solved_ref, score_ref, state_ref, grad_ref,
-    place_ref, one_ref, two_ref, map_ref, three_ref,
+    one_ref, two_ref, three_ref, map_one_ref, map_two_ref,
     out_ref, halo_ref, tail_ref, dz_ref, *, span, heads, head_dim, group,
 ):
     chunks = span // CHUNK
@@ -315,8 +315,10 @@
         columns = slice(local * head_dim, (local + 1) * head_dim)
         rates_head = head_column(rates_all, step * group + local)
         entry = state_ref[local]
-        through = one_ref[local].astype(F32) + dot_low(map_ref[local], three_ref[local], 0, 0)
-        leavings.append(jnp.where(place_ref[0] == 1, two_ref[local].astype(F32), through))
+        through = two_ref[local].astype(F32) + dot_low(
+            map_two_ref[local], three_ref[local], 0, 0
+        )
+        leavings.append(one_ref[local].astype(F32) + dot_low(map_one_ref[local], through, 0, 0))
         for chunk in range(chunks):
             rows = slice(chunk * CHUNK, (chunk + 1) * CHUNK)
             strict, causal, running, closing, carried = masks[chunk]
@@ -426,8 +428,7 @@
 
 
 def delta_back(
-    projected, taps, seg_column, seg_rows, kept, state, grad, position, arrived, heads, head_dim, span,
-    group,
+    projected, taps, seg_column, seg_rows, kept, state, grad, arrived, heads, head_dim, span, group,
 ):
     inverse, prefix, solved, scores, conv_q, conv_k, conv_v = kept
     rows = projected.shape[0]
@@ -448,7 +449,7 @@
             pl.BlockSpec((rows, LANES), lambda i: (0, total // LANES)),
             tap_third(0), tap_third(1), tap_third(2), whole(seg_column), whole(seg_rows),
             by_head(inverse), by_head(prefix), by_head(solved), by_head(scores), by_head(state),
-            columns, pl.BlockSpec(memory_space=pltpu.SMEM), *[by_head(array) for array in arrived],
+            columns, *[by_head(array) for array in arrived],
         ],
         out_specs=[
             pl.BlockSpec((span, total + LANES), lambda i: (0, 0)),
@@ -461,11 +462,11 @@
             jax.ShapeDtypeStruct((HALO, total), F32),
         ],
         scratch_shapes=[pltpu.VMEM((3 * group, span + 2 * HALO, head_dim), F32)],
-        compiler_params=pltpu.CompilerParams(vmem_limit_bytes=24 * MIB),
+        compiler_params=pltpu.CompilerParams(vmem_limit_bytes=56 * MIB),
         name="delta_back",
     )(
         conv_q, conv_k, conv_v, projected, taps, taps, taps, seg_column, seg_rows,
-        inverse, prefix, solved, scores, state, grad, position, *arrived,
+        inverse, prefix, solved, scores, state, grad, *arrived,
     )
 
 
@@ -560,9 +561,8 @@
 
 def early_kernel(
     place_ref, g0, g1, g2, g3, x0, x1, x2, x3, head_ref, low_down_ref, cot_ref,
-    out_one, out_two, down_one, down_two, *refs, rank,
+    out_one, out_two, down_one, down_two, pack_ref, *, rank,
 ):
-    (pack_ref,) = refs
     model = cot_ref.shape[1]
     hidden_units = down_one.shape[1]
     owners, share = 4, g0.shape[0]
@@ -628,18 +628,23 @@
 
 
 def ffn_kernel(
-    place_ref, x_first, x_second, weight_ref, low_ref, grad_ref, down_ref,
-    hidden_ref, back_first, back_second, out_low_ref, down_low_ref, *, strip,
+    place_ref, weight_ref, low_ref, grad_ref, down_ref, *refs, count, strip,
 ):
-    share = x_first.shape[0]
+    x_refs, hidden_ref, back_refs = refs[:count], refs[count], refs[count + 1 : -2]
+    out_low_ref, down_low_ref = refs[-2:]
+    share = x_refs[0].shape[0]
     model, hidden_units = weight_ref.shape[0], weight_ref.shape[1] // 2
-    rows = jnp.concatenate([x_first[...], x_second[...]], axis=0)
+    rows = jnp.concatenate([ref[...] for ref in x_refs], axis=0)
 
     def theirs(ref):
         parts = [
-            ref[pl.ds(pl.multiple_of(place_ref[i] * share, share), share), :] for i in range(2)
+            ref[pl.ds(pl.multiple_of(place_ref[i] * share, share), share), :] for i in range(count)
         ]
         return jnp.concatenate(parts, axis=0)
+
+    def send(back, start, width):
+        for i, ref in enumerate(back_refs):
+            ref[:, start : start + width] = back[i * share : (i + 1) * share].astype(ref.dtype)
 
     both = dot_low(rows[:, model:], low_ref[...]) + dot_low(rows[:, :model], weight_ref[...])
     gate, up = both[:, :hidden_units], both[:, hidden_units:]
@@ -656,39 +661,35 @@
         axis=1,
     )
     for start in range(0, model, strip):
-        back = dot_low(grads, weight_ref[start : start + strip, :], 1, 1)
-        back_first[:, start : start + strip] = back[:share].astype(back_first.dtype)
-        back_second[:, start : start + strip] = back[share:].astype(back_second.dtype)
-    back = dot_low(grads, low_ref[...], 1, 1)
-    back_first[:, model:] = back[:share].astype(back_first.dtype)
-    back_second[:, model:] = back[share:].astype(back_second.dtype)
+        send(dot_low(grads, weight_ref[start : start + strip, :], 1, 1), start, strip)
+    send(dot_low(grads, low_ref[...], 1, 1), model, low_ref.shape[0])
     out_low_ref[...] = dot_low(rows[:, model:], grads, 0, 0)[: out_low_ref.shape[0]]
     down_low_ref[...] = dot_low(theirs(down_ref), hidden, 0, 0)[: down_low_ref.shape[0]]
 
 
-def ffn_rows(chunks, first, second, weights, low, grad_hidden, low_grad_down, rank, kinds):
-    share, wide = first.shape
+def ffn_rows(chunks, blocks, weights, low, grad_hidden, low_grad_down, rank, kind):
+    share, wide = blocks[0].shape
+    count = len(blocks)
     hidden_units = grad_hidden.shape[1]
     vmem = pl.BlockSpec(memory_space=pltpu.VMEM)
     return pl.pallas_call(
-        functools.partial(ffn_kernel, strip=512),
-        in_specs=[pl.BlockSpec(memory_space=pltpu.SMEM)] + [vmem] * 6,
-        out_specs=[vmem] * 5,
-        out_shape=[
-            jax.ShapeDtypeStruct((2 * share, hidden_units), BF16),
-            jax.ShapeDtypeStruct((share, wide), kinds[0]),
-            jax.ShapeDtypeStruct((share, wide), kinds[1]),
+        functools.partial(ffn_kernel, count=count, strip=512),
+        in_specs=[pl.BlockSpec(memory_space=pltpu.SMEM)] + [vmem] * (4 + count),
+        out_specs=[vmem] * (3 + count),
+        out_shape=[jax.ShapeDtypeStruct((count * share, hidden_units), BF16)]
+        + [jax.ShapeDtypeStruct((share, wide), kind)] * count
+        + [
             jax.ShapeDtypeStruct((2 * rank, 2 * hidden_units), F32),
             jax.ShapeDtypeStruct((rank, hidden_units), F32),
         ],
         cost_estimate=pl.CostEstimate(
-            flops=16 * share * wide * hidden_units,
+            flops=8 * count * share * wide * hidden_units,
             bytes_accessed=4 * wide * hidden_units,
-            transcendentals=2 * share * hidden_units,
+            transcendentals=count * share * hidden_units,
         ),
         compiler_params=pltpu.CompilerParams(vmem_limit_bytes=14 * MIB),
         name="ffn_rows",
-    )(chunks, first, second, weights, low, grad_hidden, low_grad_down)
+    )(chunks, weights, low, grad_hidden, low_grad_down, *blocks)
 
 
 def in_place_kernel(place_ref, *refs):
@@ -761,7 +762,11 @@
     def _():
         add_up(projection_out_ref, cuts[0], model)
         add_up(projection_in_ref, cuts[1], projection_in_ref.shape[-1])
-        add_up(strength_ref, cuts[3], LANES)
+        strengths = dot_low(terms[:, cuts[3] : cuts[3] + LANES], select, 0, 1)
+        for adapter in range(adapters):
+            strength_ref[adapter] = strengths[
+                : strength_ref.shape[1], adapter * rank : (adapter + 1) * rank
+            ]
 
 
 def totals(picks, terms, cuts, adapters, rank, model, features, hidden_units, heads):
@@ -778,14 +783,15 @@
             grid=(quarters,),
             in_specs=[pl.BlockSpec((sequences, 1, rank, width), lambda q, c: (0, q, 0, 0))],
             out_specs=[
-                part(3, model), part(2, features), one(heads), one(features), one(model),
+                part(3, model), part(2, features),
+                pl.BlockSpec((adapters, heads, rank), lambda q, c: (0, 0, 0)), one(features), one(model),
                 part(1, model), part(1, hidden_units), one(hidden_units), one(model),
             ],
         ),
         out_shape=[
             shape(4, adapters, rank, model),
             shape(3, adapters, rank, features),
-            shape(adapters, rank, heads),
+            shape(adapters, heads, rank),
             shape(adapters, rank, features),
             shape(adapters, rank, model),
             shape(2, adapters, rank, model),
@@ -927,14 +933,6 @@
     ffn_pack = jnp.concatenate([gate_weight, up_weight, down_weight.T], axis=1)
     mixer_all = lax.all_gather(mixer_pack, everyone, axis=0, tiled=True)
     ffn_all = lax.all_gather(ffn_pack, everyone, axis=0, tiled=True)
-    triple = 3 * features + LANES
-    weight_in = mixer_all[:, :triple]
-    weight_out = mixer_all[:, triple:]
-    weight_gate_up = ffn_all[:, : 2 * hidden_units]
-    weight_down = ffn_all[:, 2 * hidden_units :]
-    picks = mixer_all[:: mixer_all.shape[0] // lax.axis_size("weights"), 3 * features + heads]
-    picks = picks.astype(jnp.int32)
-
     chosen = sequence_adapter_index[0]
     take = lambda table, axis: lax.dynamic_index_in_dim(table, chosen, axis, keepdims=False)
     attention_in = jnp.swapaxes(take(adapter_attention_input, 1), 1, 2).reshape(4 * rank, model)
@@ -980,6 +978,19 @@
     inputs_ext = jnp.concatenate([edge, tokens], axis=0).astype(F32)
     normed_ext = rms_scale(inputs_ext, mixer_norm_gain).astype(BF16)
     low_ext = dot_nt(normed_ext, attention_in).astype(BF16)
+    out_map = pad_rows(projection_out, LANES)
+    in_map = pad_rows(feedforward_in, LANES)
+    low_grad_down = pad_columns(dot_nt(cotangent, down_out).astype(BF16), LANES)
+    ffn_gain = feedforward_norm_gain[None, :]
+    projection_in = pad_rows(projection_in, LANES)
+    triple = 3 * features + LANES
+    weight_in = mixer_all[:, :triple]
+    weight_out = mixer_all[:, triple:]
+    weight_gate_up = ffn_all[:, : 2 * hidden_units]
+    weight_down = ffn_all[:, 2 * hidden_units :]
+    picks = mixer_all[:: mixer_all.shape[0] // lax.axis_size("weights"), 3 * features + heads]
+    picks = picks.astype(jnp.int32)
+
     projected = dot(normed_ext, weight_in) + dot(low_ext, low_in)
     normed = normed_ext[HALO:]
     low_attn = low_ext[HALO:]
@@ -995,7 +1006,7 @@
         offset.astype(F32)
         + jnp.einsum("hij,hjk->hik", linear, one, preferred_element_type=F32)
     ).astype(BF16)
-    out_ext = jnp.concatenate([weight_out, pad_rows(projection_in, LANES)], axis=0)
+    out_ext = jnp.concatenate([weight_out, projection_in], axis=0)
     second, out_ext = lax.optimization_barrier((second, out_ext))
     two = lax.ppermute(second, "context", [(1, 2)])
     three = lax.ppermute(second, "context", [(1, 3)])
@@ -1003,39 +1014,39 @@
     head_low, attended, state, *branch_parts = attend(
         where, here, op, qp, one, two, linear_two, three, gain_row, out_ext, owners
     )
-    linear_one = lax.ppermute(linear, "context", [(1, 0)])
-
     wide = model + LANES
     branch = sent_to_owners(branch_parts, "tensor")
-    ffn_gain = feedforward_norm_gain[None, :]
-    out_map = pad_rows(projection_out, LANES)
-    in_map = pad_rows(feedforward_in, LANES)
+    linear_one = shifted(linear, "context", -1, wrap=False)
+    linear_after = lax.ppermute(linear, "context", [(2, 0)])
+    *branch, linear_one, linear_after = lax.optimization_barrier(
+        (*branch, linear_one, linear_after)
+    )
     middle, packed, low_o = owner_call(
         middle_kernel, "middle_rows", here, share,
         [(part, "rows") for part in branch]
         + [(tokens, "span"), (out_map, "whole"), (ffn_gain, "whole"), (in_map, "whole")],
         [((share, model), F32), ((share, wide), BF16), ((share, LANES), BF16)],
     )
-    low_grad_down = pad_columns(dot_nt(cotangent, down_out).astype(BF16), LANES)
     grad_hidden = dot(cotangent, weight_down) + dot(low_grad_down, down_in_ext)
     ffn_in, grad_hidden = blocks_by_ring(packed, "tensor", grad_hidden)
 
     back_parts, hidden_parts = [None] * owners, [None] * owners
     ffn_out_terms, down_in_terms = [], []
-    for pair in ((1, 3), (2, 0)):
-        chunks = jnp.stack([lax.rem(place + k, owners) for k in pair])
-        hidden_pair, back_parts[pair[0]], back_parts[pair[1]], out_term, down_term = ffn_rows(
-            chunks, ffn_in[pair[0]], ffn_in[pair[1]], weight_gate_up, ffn_low, grad_hidden,
-            low_grad_down, rank, [F32 if k == 0 else BF16 for k in pair],
+    for which in ((1, 3), (2, 0)):
+        hidden_rows, *backs, out_term, down_term = ffn_rows(
+            jnp.stack([lax.rem(place + k, owners) for k in which]), [ffn_in[k] for k in which],
+            weight_gate_up, ffn_low, grad_hidden, low_grad_down, rank, BF16,
         )
-        for i, k in enumerate(pair):
-            hidden_parts[k] = hidden_pair[i * share : (i + 1) * share]
+        for i, k in enumerate(which):
+            hidden_parts[k] = hidden_rows[i * share : (i + 1) * share]
+            back_parts[k] = backs[i]
         ffn_out_terms.append(out_term)
         down_in_terms.append(down_term)
     back = sent_to_owners(back_parts, "tensor", (1, 3, 2))
     hidden = in_place(here, hidden_parts, hidden_units, BF16)
     down_all = dot_nt(hidden, weight_down).astype(BF16)
-    back, down_all = lax.optimization_barrier((back, down_all))
+    down_low = dot_nt(down_in_ext[:rank], hidden).astype(BF16)
+    back, down_all, down_low = lax.optimization_barrier((back, down_all, down_low))
     grad_middle, grad_packed = owner_call(
         functools.partial(back_kernel, rank=rank), "back_rows", here, share,
         [(part, "rows") for part in back]
@@ -1045,26 +1056,30 @@
     )
 
     grad_blocks = blocks_by_ring(grad_packed, "tensor")
+    low_down = paired_sum(down_low, "tensor").astype(BF16)
+    grad_blocks, low_down = lax.optimization_barrier((grad_blocks, low_down))
 
     grad_attended, own = attend_back(
         here, attended, qp, gain_row, out_ext, grad_blocks, heads, head_dim
     )
-    hidden, down_all, own = lax.optimization_barrier((hidden, down_all, own))
+    down_all, own = lax.optimization_barrier((down_all, own))
     down_sum = lax.psum_scatter(down_all, "tensor", scatter_dimension=0, tiled=True).astype(F32)
-    down_low = dot_nt(down_in_ext[:rank], hidden).astype(BF16)
+    own_three = shifted(own, "context", -3, wrap=False)
+    own_two = shifted(own, "context", -2, wrap=False)
     own_one = shifted(own, "context", -1, wrap=False)
-    own_one, down_low = lax.optimization_barrier((own_one, down_low))
-    own_second = (
-        own.astype(F32) + jnp.einsum("hji,hjk->hik", linear, own_one, preferred_element_type=F32)
-    ).astype(BF16)
-    own_two = lax.ppermute(own_second, "context", [(2, 1)])
-    own_three = lax.ppermute(own_second, "context", [(2, 0)])
-
-    low_down = paired_sum(down_low, "tensor").astype(BF16)
+    early_width = model + hidden_units
+    (early,) = span_call(
+        functools.partial(early_kernel, rank=rank), "early_terms", (here,),
+        [*grad_blocks, *ffn_in, head_low, low_down, cotangent, *ffn_out_terms, *down_in_terms],
+        [((4, rank, early_width), BF16)], [], 56,
+    )
+    own_one, own_two, own_three, early = lax.optimization_barrier(
+        (own_one, own_two, own_three, early)
+    )
 
     grad_projected, halo, tail = delta_back(
-        projected, kernels, seg_column, seg_rows, kept, state, grad_attended, where,
-        (own_one, own_two, linear_one, own_three), heads, head_dim, span, heads,
+        projected, kernels, seg_column, seg_rows, kept, state, grad_attended,
+        (own_one, own_two, own_three, linear_one, linear_after), heads, head_dim, span, heads // 2,
     )
     returned = shifted(halo, "context", -1, wrap=False)
     low_down_own = lax.dynamic_slice_in_dim(low_down, place * share, share, axis=1)
@@ -1079,14 +1094,10 @@
 
     low_part = dot_nt(grad_projected, low_in).astype(BF16)
     low_parts = blocks_of_others(low_part, "tensor")
-    early_width = model + hidden_units
-    (early,) = span_call(
-        functools.partial(early_kernel, rank=rank), "early_terms", (here,),
-        [*grad_blocks, *ffn_in, head_low, low_down, cotangent, *ffn_out_terms, *down_in_terms],
-        [((4, rank, early_width), BF16)], [], 56,
-    )
-    *low_parts, block_before, block_after, early = lax.optimization_barrier(
-        (*low_parts, block_before, block_after, early)
+    grad_rows, _ = lax.optimization_barrier((grad_projected, low_part))
+    normed_parts = dot_nt(grad_rows, weight_in).astype(BF16)
+    low_parts, normed_parts = lax.optimization_barrier(
+        (low_parts, [chunk_at(normed_parts, k) for k in range(owners)])
     )
     late_width = model + features
     low_grad_attn, *quarters = span_call(
@@ -1096,10 +1107,10 @@
         [pltpu.VMEM((4, rank, late_width), BF16)], 24,
     )
     quarters = sent_to_owners(quarters, "context")
-    grad_rows, _ = lax.optimization_barrier((grad_projected, low_grad_attn))
-    normed_parts = dot_nt(grad_rows, weight_in).astype(BF16)
-    *quarters, normed_parts = lax.optimization_barrier((*quarters, normed_parts))
-    normed_sent = sent_to_owners([chunk_at(normed_parts, k) for k in range(owners)], "tensor")
+    *quarters, block_before, block_after = lax.optimization_barrier(
+        (*quarters, block_before, block_after)
+    )
+    normed_sent = sent_to_owners(normed_parts, "tensor")
     block_far = jnp.concatenate(
         [
             shifted(block_after[:block_half], "tensor", -1),
@@ -1108,6 +1119,7 @@
         axis=0,
     )
     block_out = in_place(here, [block_own, block_after, block_far, block_before], model, BF16)
+    *normed_sent, block_out, picks = lax.optimization_barrier((*normed_sent, block_out, picks))
     (grad_tokens,) = owner_call(
         tokens_kernel, "token_rows", here, share,
         [(part, "rows") for part in normed_sent]
@@ -1131,7 +1143,7 @@
         tokens_grad,
         flip(sums[0]),
         sums[1],
-        sums[2],
+        flip(sums[2]),
         flip(sums[3]),
         sums[4],
         flip(sums[5]),

time: 393 us -> 379 us (0.964)
  local copies, waits for them, and re-layouts: 49.4 us -> 31.8 us
  waiting for transfers between devices: 117 us -> 130 us
  matrix products: 44.1 us -> 38.7 us
  starting transfers between devices: 67.8 us -> 63.2 us
    unnamed x155 -> x143, local copies, waits for them, and re-layouts: 24.4 us -> 9.09 us
    ppermute x38 -> x41, waiting for transfers between devices: 72.9 us -> 88.2 us  [shifted(): return lax.ppermute(block, axis, route)]
    ppermute x38 -> x41, starting transfers between devices: 58.6 us -> 57.7 us  [shifted(): return lax.ppermute(block, axis, route)]
  transfers between devices with their start and end apart: 48 -> 49, of which waited for: 21 -> 21; matrix products, arithmetic and copies ran while one was open for 19% -> 18% of each run, Pallas kernels for 17% -> 18%
where the time goes in v3:
time: 379 us; the launch traced here: 373 us
  waiting for transfers between devices  130 us (34%)
  Pallas kernels  85.5 us (23%)
  starting transfers between devices  63.2 us (17%)
  matrix products  38.7 us (10%)
  local copies, waits for them, and re-layouts  31.8 us (8%)
  between operations  16.2 us (4%)
  other arithmetic  7.24 us (2%)
    ppermute x41, waiting for transfers between devices, shifted(): return lax.ppermute(block, axis, route)  88.2 us
    ppermute x41, starting transfers between devices, shifted(): return lax.ppermute(block, axis, route)  57.7 us
    all_gather x1, waiting for transfers between devices, on_device(): mixer_all = lax.all_gather(mixer_pack, everyone, axis=0, tiled=True)  34.8 us
    dot_general x4, matrix products, dot(): return jnp.dot(left, right, preferred_element_type=F32)  18 us
    pallas_call x2, Pallas kernels, ffn_rows(): pl.pallas_call(functools.partial(ffn_kernel, count=count, strip=512), in_...  18 us
    dot_general x6, matrix products, dot_nt(): lax.dot_general(left, right, (((1,), (1,)), ((), ())), preferred_element_...  17.7 us
    pallas_call x1, Pallas kernels, delta_back(): pl.pallas_call(functools.partial(delta_back_kernel, span=span, heads=head...  17 us
    pallas_call x3, Pallas kernels, owner_call(): pl.pallas_call(kernel, grid_spec=pltpu.PrefetchScalarGridSpec(num_scalar_...  11.8 us
  transfers between devices with their start and end apart: 49, of which 21 were waited for; matrix products, arithmetic and copies ran while one was open for 18% of the time, Pallas kernels for 18%

profile of v3, /device:TPU:28, one launch (start us, length us, event | category | flops | bytes accessed | tf_op | source)
XLA Modules:
  0.0 372.5 jit_solution(14510406552365338361)
XLA Ops:
  13.4 3.1 collective-permute-start
  22.7 3.1 convolution_convert_fusion.3
  30.0 2.5 fusion.53
  32.5 34.8 %all-gather.5.cloned.1.call-done = bf16[2048,2176]{1,0:T(8,128)(2,1)} async-done(((bf16[64,2176]{1,0:T(8,128)(2,1)}), bf16[2048,2176]{1,0:T(8,128)(2,1)}) %all-gather.5.cloned.1.call-update) | async-done | bytes 8912912 | tf_op jit(solution)/shard_map/all_gather | solution.py:934
  67.3 8.5 %fusion.15.q_ref.k_ref.v_ref.logit_ref = f32[520,1664]{1,0:T(8,128)S(1)} fusion(f32[520,1664]{1,0:T(8,128)} %fusion.53, bf16[520,2048]{1,0:T(8,128)(2,1)} %copy-done.41, bf16[2048,2176]{1,0:T(8,128)(2,1)} %all-gather.5.cloned.1.call-done), kind=kOutput, calls=%fused_computation.17 | convolution fusion | flops 3545052160 | bytes 15867904 | tf_op jit(solution)/shard_map/dot_general | solution.py:848
  76.0 10.5 %delta_local.1 = (bf16[512,512]{1,0:T(8,128)(2,1)S(1)}, f32[512,512]{1,0:T(8,128)S(1)}, bf16[4,128,128]{2,1,0:T(8,128)(2,1)S(1)}, bf16[4,128,128]{2,1,0:T(8,128)...) custom-call(f32[520,1664]{1,0:T(8,128)S(1)} %fusion.15.q_ref.k_ref.v, ...), custom_call_target="tpu_custom_call" | custom-call | tf_op jit(solution)/shard_map/delta_local/pallas_call | solution.py:181
  86.6 3.3 collective-permute-start.1
  91.7 3.2 collective-permute-done.1.one_ref
  98.8 6.9 %collective-permute-done.2.two_ref = bf16[4,128,128]{2,1,0:T(8,128)(2,1)S(1)} collective-permute-done((bf16[4,128,128]{2,1,0:T(8,128)(2,1)S(1)}, bf16[4,128,128]{2,1,0:T(8,128)(2,1)S(1)}, u32[]{:S(2)}, u32[]{:S(2)}) %collective-permute-start.2) | collective-permute-done | bytes 131104 | tf_op jit(solution)/shard_map/ppermute | solution.py:1011
  105.8 3.6 attend.1
  113.1 2.4 collective-permute-start.6
  118.1 2.3 collective-permute-start.8
  130.3 8.4 %collective-permute-done.7.three_ref = bf16[128,2176]{1,0:T(8,128)(2,1)} collective-permute-done((bf16[128,2176]{1,0:T(8,128)(2,1)S(1)}, bf16[128,2176]{1,0:T(8,128)(2,1)}, u32[]{:S(2)}, u32[]{:S(2)}) %collective-permute-start.7) | collective-permute-done | bytes 557088 | tf_op jit(solution)/shard_map/ppermute | solution.py:813
  138.6 3.8 %middle_rows.1 = (f32[128,2048]{1,0:T(8,128)}, bf16[128,2176]{1,0:T(8,128)(2,1)}, bf16[128,128]{1,0:T(8,128)(2,1)}) custom-call(s32[1]{0:T(128)} %bitcast.14.place_ref, bf16[128,2176]{1,0:T(8,128)(2,1)} %copy-done.27, bf16[128,2176]{1,0:T(8,128)(2,1)} %collective-permute-done.5.one_ref, bf16[128,2176]{1,0:T(8,128)(2,1)} %collective-permute-done.6.two_ref, ...), custom_call_target="tpu_custom_call" | custom-call | tf_op jit(solution)/shard_map/middle_rows/pallas_call | solution.py:548
  143.5 2.2 collective-permute-start.10
  145.7 6.5 %fusion.12 = f32[512,1408]{1,0:T(8,128)S(1)} fusion(bf16[512,2048]{1,0:T(8,128)(2,1)} %cot_ref.3, bf16[2048,4224]{1,0:T(8,128)(2,1)} %all-gather.7.cloned.1.call-done), kind=kOutput, calls=%fused_computation.16 | convolution fusion | flops 2952790016 | bytes 10747904 | tf_op jit(solution)/shard_map/dot_general | solution.py:848
  152.8 5.8 %collective-permute-done.11.refs_0_.x1 = bf16[128,2176]{1,0:T(8,128)(2,1)S(1)} collective-permute-done((bf16[128,2176]{1,0:T(8,128)(2,1)}, bf16[128,2176]{1,0:T(8,128)(2,1)S(1)}, u32[]{:S(2)}, u32[]{:S(2)}) %collective-permute-start.11) | collective-permute-done | bytes 557088 | tf_op jit(solution)/shard_map/ppermute | solution.py:813
  158.7 3.0 collective-permute-start.13
  162.6 9.4 %ffn_rows.3 = (bf16[256,1408]{1,0:T(8,128)(2,1)S(1)}, bf16[128,2176]{1,0:T(8,128)(2,1)}, bf16[128,2176]{1,0:T(8,128)(2,1)}, f32[32,2816]{1,0:T(8,128)S(1)}, f32[16,1408]{1,0:T(8,128)S(1)}) custom-call(s32[2]{0:T(128)S(1)} %pad_add_fusion.1.place_ref, bf16[2048,2816]{1,0:T(8,128)(2,1)S(1)} %slice.112.weight_ref, bf16[128,2816]{1,0:T(8,128)(2,1)S(1)} %copy-done.24, ...), custom_call_target="tpu_custom_call" | custom-call | flops 6274678784 | bytes 12255232 | tf_op jit(solution)/shard_map/ffn_rows/pallas_call | solution.py:675
  172.0 3.3 collective-permute-start.14
  175.6 8.6 %ffn_rows.2 = (bf16[256,1408]{1,0:T(8,128)(2,1)S(1)}, bf16[128,2176]{1,0:T(8,128)(2,1)S(1)}, bf16[128,2176]{1,0:T(8,128)(2,1)S(1)}, f32[32,2816]{1,0:T(8,128)S(1)}, f32[16,1408]{1,0:T(8,128)S(1)}) custom-call(s32[2]{0:T(128)S(1)} %pad_add_fusion.place_ref, bf16[2048,2816]{1,0:T(8,128)(2,1)S(1)} %slice.112.weight_ref, bf16[128,2816]{1,0:T(8,128)(2,1)S(1)} %copy-done.24, ...), custom_call_target="tpu_custom_call" | custom-call | flops 6274678784 | bytes 12255232 | tf_op jit(solution)/shard_map/ffn_rows/pallas_call | solution.py:675
  187.5 4.7 %fusion.21 = bf16[512,2048]{1,0:T(8,128)(2,1)} fusion(bf16[512,1408]{1,0:T(8,128)(2,1)S(1)} %in_place.3, bf16[2048,4224]{1,0:T(8,128)(2,1)S(1)} %copy-done.42), kind=kOutput, calls=%fused_computation.19 | convolution fusion | flops 2953838592 | bytes 9306112 | tf_op jit(solution)/shard_map/dot_general | solution.py:852
  192.2 9.4 %collective-permute-done.16.three_ref = bf16[128,2176]{1,0:T(8,128)(2,1)} collective-permute-done((bf16[128,2176]{1,0:T(8,128)(2,1)}, bf16[128,2176]{1,0:T(8,128)(2,1)}, u32[]{:S(2)}, u32[]{:S(2)}) %collective-permute-start.16) | collective-permute-done | bytes 557088 | tf_op jit(solution)/shard_map/ppermute | solution.py:813
  201.6 4.3 %back_rows.1 = (f32[128,2048]{1,0:T(8,128)}, bf16[128,2176]{1,0:T(8,128)(2,1)}) custom-call(s32[1]{0:T(128)} %bitcast.14.place_ref, bf16[128,2176]{1,0:T(8,128)(2,1)} %copy-done.26, bf16[128,2176]{1,0:T(8,128)(2,1)} %copy-done.47, bf16[128,2176]{1,0:T(8,128)(2,1)} %collective-permute-done.15.two_ref, bf16[128,2176]{1,0:T(8,128)(2,1)} %collective-permute-done.16.three_ref, ...), custom_call_target="tpu_custom_call" | custom-call | tf_op jit(solution)/shard_map/back_rows/pallas_call | solution.py:548
  208.0 10.9 %collective-permute-done.19.refs_3_.g3 = bf16[128,2176]{1,0:T(8,128)(2,1)S(1)} collective-permute-done((bf16[128,2176]{1,0:T(8,128)(2,1)}, bf16[128,2176]{1,0:T(8,128)(2,1)S(1)}, u32[]{:S(2)}, u32[]{:S(2)}) %collective-permute-start.19) | collective-permute-done | bytes 557088 | tf_op jit(solution)/shard_map/ppermute | solution.py:813
  225.9 2.0 collective-permute-done.22
  229.3 2.3 attend_back.1
  238.2 5.7 %early_terms.1.early_ref = bf16[4,16,3456]{2,1,0:T(8,128)(2,1)} custom-call(s32[1]{0:T(128)} %bitcast.14.place_ref, bf16[128,2176]{1,0:T(8,128)(2,1)} %get-tuple-element.155.refs_0_.g0, bf16[128,2176]{1,0:T(8,128)(2,1)} %copy-done.5, bf16[128,2176]{1,0:T(8,128)(2,1)} %copy-done.3, bf16[128,2176]{1,0:T(8,128)(2,1)} %copy-done.4, ...), custom_call_target="tpu_custom_call" | custom-call | tf_op jit(solution)/shard_map/early_terms/pallas_call | solution.py:619
  244.6 17.0 %delta_back.1 = (bf16[512,1664]{1,0:T(8,128)(2,1)}, f32[8,1536]{1,0:T(8,128)}, f32[8,1536]{1,0:T(8,128)}) custom-call(f32[512,512]{1,0:T(8,128)} %copy-done.18, f32[512,512]{1,0:T(8,128)} %copy-done.19, f32[512,512]{1,0:T(8,128)} %copy-done.20, f32[520,1664]{1,0:T(8,128)} %copy-done.2, f32[4,1536]{1,0:T(4,128)} %bitcast.79, f32[4,1536]{1,0:T(4,128)} %bitcast.80, ...), custom_call_target="tpu_custom_call" | custom-call | tf_op jit(solution)/shard_map/delta_back/pallas_call | solution.py:442
  261.7 2.1 collective-permute-start.27
  265.7 2.4 collective-permute-done.27
  268.8 3.5 collective-permute-start.30
  273.3 2.5 collective-permute-start.38
  276.7 7.1 %fusion.18 = bf16[512,2048]{1,0:T(8,128)(2,1)S(1)} fusion(bf16[512,1664]{1,0:T(8,128)(2,1)S(1)} %fusion.45.grad_ref, bf16[2048,2176]{1,0:T(8,128)(2,1)} %all-gather.5.cloned.1.call-done), kind=kOutput, calls=%fused_computation.18 | convolution fusion | flops 3490709504 | bytes 10616832 | tf_op jit(solution)/shard_map/dot_general | solution.py:852
  288.8 5.7 %collective-permute-done.34 = bf16[16,6016]{1,0:T(8,128)(2,1)S(1)} collective-permute-done((bf16[16,6016]{1,0:T(8,128)(2,1)S(1)}, bf16[16,6016]{1,0:T(8,128)(2,1)S(1)}, u32[]{:S(2)}, u32[]{:S(2)}) %collective-permute-start.34) | collective-permute-done | bytes 192544 | tf_op jit(solution)/shard_map/ppermute | solution.py:813
  294.5 2.1 collective-permute-done.36
  298.6 2.3 collective-permute-start.32
  301.9 3.3 collective-permute-start.40
  307.0 12.3 %collective-permute-done.40 = bf16[64,2048]{1,0:T(8,128)(2,1)S(1)} collective-permute-done((bf16[64,2048]{1,0:T(8,128)(2,1)S(1)}, bf16[64,2048]{1,0:T(8,128)(2,1)S(1)}, u32[]{:S(2)}, u32[]{:S(2)}) %collective-permute-start.40) | collective-permute-done | bytes 262176 | tf_op jit(solution)/shard_map/ppermute | solution.py:813
  319.3 2.9 collective-permute-done.39
  323.2 2.9 in_place.4
  327.3 3.6 token_rows.1.refs_0_
  333.0 10.2 %collective-permute-done.43.refs_3_ = bf16[128,2048]{1,0:T(8,128)(2,1)S(1)} collective-permute-done((bf16[128,2048]{1,0:T(8,128)(2,1)}, bf16[128,2048]{1,0:T(8,128)(2,1)S(1)}, u32[]{:S(2)}, u32[]{:S(2)}) %collective-permute-start.43) | collective-permute-done | bytes 524320 | tf_op jit(solution)/shard_map/ppermute | solution.py:813
  343.2 2.0 collective-permute-start.44
  345.4 4.3 %collective-permute-done.44 = bf16[64,2048]{1,0:T(8,128)(2,1)S(1)} collective-permute-done((bf16[64,2048]{1,0:T(8,128)(2,1)S(1)}, bf16[64,2048]{1,0:T(8,128)(2,1)S(1)}, u32[]{:S(2)}, u32[]{:S(2)}) %collective-permute-start.44) | collective-permute-done | bytes 262176 | tf_op jit(solution)/shard_map/ppermute | solution.py:813
  349.6 3.3 collective-permute-done.42
  352.9 2.5 in_place.5
  355.4 10.1 %totals.1 = (f32[4,8,16,2048]{3,2,1,0:T(8,128)}, f32[3,8,16,512]{3,2,1,0:T(8,128)}, f32[8,4,16]{2,1,0:T(4,128)}, f32[8,16,512]{2,1,0:T(8,128)}, f32[8,16,2048]{2...) custom-call(s32[8]{0:T(128)} %convert_reduce_fusion.pick_ref, ...), custom_call_target="tpu_custom_call" | custom-call | tf_op jit(solution)/shard_map/totals/pallas_call | solution.py:779
  (279 shorter events, 79.7 us)
Async XLA Ops:
  7.2 60.1 %all-gather.5.cloned.1.call-start = ((), (), s32[]{:S(2)}) async-start(), calls=%async_computation.1 | async-start | bytes 9191424 | tf_op jit(solution)/shard_map/all_gather | solution.py:934
  10.6 135.2 %all-gather.7.cloned.1.call-start = ((), (), s32[]{:S(2)}) async-start(), calls=%async_computation.2 | async-start | bytes 17842176 | tf_op jit(solution)/shard_map/all_gather | solution.py:935
  12.6 251.2 %reduce-scatter.2.cloned.1.call-start = ((), (), s32[]{:S(2)}) async-start(), calls=%async_computation.3 | async-start | bytes 2621440 | tf_op jit(solution)/shard_map/reduce_scatter | solution.py:1066
  13.4 13.5 %collective-permute-start = (bf16[8,2048]{1,0:T(8,128)(2,1)S(1)}, bf16[8,2048]{1,0:T(8,128)(2,1)S(1)}, u32[]{:S(2)}, u32[]{:S(2)}) collective-permute-start(bf16[8,2048]{1,0:T(8,128)(2,1)S(1)} %slice.84), channel_id=1, source_target_pairs={{0,4},{4,8},{8,12},{1,5},{5,9},{9,13},{2,6},{6,10},{10,14},{3,7},{... | collective-permute-start | bytes 98312 | tf_op jit(solution)/shard_map/ppermute | solution.py:813
  86.6 8.3 %collective-permute-start.1 = (bf16[4,128,128]{2,1,0:T(8,128)(2,1)S(1)}, bf16[4,128,128]{2,1,0:T(8,128)(2,1)S(1)}, u32[]{:S(2)}, u32[]{:S(2)}) collective-permute-start(bf16[4,128,128]{2,1,0:T(8,128)(2,1)S(1)} %get-tuple-element.123), channel_id=1, source_target_pairs={{0,4},{4,8},{8,12},{1,5},{5,9},{9,13},{2,6},{6,10},{10,14},{3,7},{... | collective-permute-start | bytes 393224 | tf_op jit(solution)/shard_map/ppermute | solution.py:813
  90.0 8.8 %collective-permute-start.3 = (bf16[4,128,128]{2,1,0:T(8,128)(2,1)}, bf16[4,128,128]{2,1,0:T(8,128)(2,1)S(1)}, u32[]{:S(2)}, u32[]{:S(2)}) collective-permute-start(bf16[4,128,128]{2,1,0:T(8,128)(2,1)} %get-tuple-element.124), channel_id=1, source_target_pairs={{8,12},{9,13},{10,14},{11,15},{24,28},{25,29},{26,30},{27,31},{40,... | collective-permute-start | bytes 393224 | tf_op jit(solution)/shard_map/ppermute | solution.py:1004
  96.6 9.1 %collective-permute-start.2 = (bf16[4,128,128]{2,1,0:T(8,128)(2,1)S(1)}, bf16[4,128,128]{2,1,0:T(8,128)(2,1)S(1)}, u32[]{:S(2)}, u32[]{:S(2)}) collective-permute-start(bf16[4,128,128]{2,1,0:T(8,128)(2,1)S(1)} %add_convert_fusion.1), channel_id=1, source_target_pairs={{4,8},{5,9},{6,10},{7,11},{20,24},{21,25},{22,26},{23,27},{36,40},... | collective-permute-start | bytes 393224 | tf_op jit(solution)/shard_map/ppermute | solution.py:1011
  112.6 15.9 %collective-permute-start.5 = (bf16[128,2176]{1,0:T(8,128)(2,1)}, bf16[128,2176]{1,0:T(8,128)(2,1)}, u32[]{:S(2)}, u32[]{:S(2)}) collective-permute-start(bf16[128,2176]{1,0:T(8,128)(2,1)} %get-tuple-element.130), channel_id=1, source_target_pairs={{0,1},{1,2},{2,3},{3,0},{4,5},{5,6},{6,7},{7,4},{8,9},{9,10},{10,1... | collective-permute-start | bytes 1671176 | tf_op jit(solution)/shard_map/ppermute | solution.py:813
  113.1 17.2 %collective-permute-start.6 = (bf16[128,2176]{1,0:T(8,128)(2,1)S(1)}, bf16[128,2176]{1,0:T(8,128)(2,1)}, u32[]{:S(2)}, u32[]{:S(2)}) collective-permute-start(bf16[128,2176]{1,0:T(8,128)(2,1)S(1)} %get-tuple-element.131), channel_id=1, source_target_pairs={{0,2},{1,3},{2,0},{3,1},{4,6},{5,7},{6,4},{7,5},{8,10},{9,11},{10,... | collective-permute-start | bytes 1671176 | tf_op jit(solution)/shard_map/ppermute | solution.py:813
  115.5 23.2 %collective-permute-start.7 = (bf16[128,2176]{1,0:T(8,128)(2,1)S(1)}, bf16[128,2176]{1,0:T(8,128)(2,1)}, u32[]{:S(2)}, u32[]{:S(2)}) collective-permute-start(bf16[128,2176]{1,0:T(8,128)(2,1)S(1)} %get-tuple-element.132), channel_id=1, source_target_pairs={{0,3},{1,0},{2,1},{3,2},{4,7},{5,4},{6,5},{7,6},{8,11},{9,8},{10,9... | collective-permute-start | bytes 1671176 | tf_op jit(solution)/shard_map/ppermute | solution.py:813
  116.2 10.5 %collective-permute-start.9 = (bf16[4,128,128]{2,1,0:T(8,128)(2,1)}, bf16[4,128,128]{2,1,0:T(8,128)(2,1)}, u32[]{:S(2)}, u32[]{:S(2)}) collective-permute-start(bf16[4,128,128]{2,1,0:T(8,128)(2,1)} %get-tuple-element.124), channel_id=1, source_target_pairs={{8,0},{9,1},{10,2},{11,3},{24,16},{25,17},{26,18},{27,19},{40,32},... | collective-permute-start | bytes 393224 | tf_op jit(solution)/shard_map/ppermute | solution.py:1020
  118.1 10.1 %collective-permute-start.8 = (bf16[4,128,128]{2,1,0:T(8,128)(2,1)}, bf16[4,128,128]{2,1,0:T(8,128)(2,1)}, u32[]{:S(2)}, u32[]{:S(2)}) collective-permute-start(bf16[4,128,128]{2,1,0:T(8,128)(2,1)} %get-tuple-element.124), channel_id=1, source_target_pairs={{4,0},{8,4},{12,8},{5,1},{9,5},{13,9},{6,2},{10,6},{14,10},{7,3},{... | collective-permute-start | bytes 393224 | tf_op jit(solution)/shard_map/ppermute | solution.py:813
  142.4 16.2 %collective-permute-start.11 = (bf16[128,2176]{1,0:T(8,128)(2,1)}, bf16[128,2176]{1,0:T(8,128)(2,1)S(1)}, u32[]{:S(2)}, u32[]{:S(2)}) collective-permute-start(bf16[128,2176]{1,0:T(8,128)(2,1)} %get-tuple-element.137.refs_1_.x0), channel_id=1, source_target_pairs={{0,3},{1,0},{2,1},{3,2},{4,7},{5,4},{6,5},{7,6},{8,11},{9,8},{10,9... | collective-permute-start | bytes 1671176 | tf_op jit(solution)/shard_map/ppermute | solution.py:813
  143.5 15.1 %collective-permute-start.10 = (bf16[128,2176]{1,0:T(8,128)(2,1)}, bf16[128,2176]{1,0:T(8,128)(2,1)S(1)}, u32[]{:S(2)}, u32[]{:S(2)}) collective-permute-start(bf16[128,2176]{1,0:T(8,128)(2,1)} %get-tuple-element.137.refs_1_.x0), channel_id=1, source_target_pairs={{0,1},{1,2},{2,3},{3,0},{4,5},{5,6},{6,7},{7,4},{8,9},{9,10},{10,1... | collective-permute-start | bytes 1671176 | tf_op jit(solution)/shard_map/ppermute | solution.py:813
  158.7 16.9 %collective-permute-start.13 = (bf16[64,2176]{1,0:T(8,128)(2,1)S(1)}, bf16[64,2176]{1,0:T(8,128)(2,1)S(1)}, u32[]{:S(2)}, u32[]{:S(2)}) collective-permute-start(bf16[64,2176]{1,0:T(8,128)(2,1)S(1)} %slice.96), channel_id=1, source_target_pairs={{0,1},{1,2},{2,3},{3,0},{4,5},{5,6},{6,7},{7,4},{8,9},{9,10},{10,1... | collective-permute-start | bytes 835592 | tf_op jit(solution)/shard_map/ppermute | solution.py:813
  161.7 13.8 %collective-permute-start.12 = (bf16[64,2176]{1,0:T(8,128)(2,1)S(1)}, bf16[64,2176]{1,0:T(8,128)(2,1)S(1)}, u32[]{:S(2)}, u32[]{:S(2)}) collective-permute-start(bf16[64,2176]{1,0:T(8,128)(2,1)S(1)} %slice.95), channel_id=1, source_target_pairs={{0,3},{1,0},{2,1},{3,2},{4,7},{5,4},{6,5},{7,6},{8,11},{9,8},{10,9... | collective-permute-start | bytes 835592 | tf_op jit(solution)/shard_map/ppermute | solution.py:813
  172.0 20.2 %collective-permute-start.14 = (bf16[128,2176]{1,0:T(8,128)(2,1)}, bf16[128,2176]{1,0:T(8,128)(2,1)S(1)}, u32[]{:S(2)}, u32[]{:S(2)}) collective-permute-start(bf16[128,2176]{1,0:T(8,128)(2,1)} %get-tuple-element.142), channel_id=1, source_target_pairs={{0,1},{1,2},{2,3},{3,0},{4,5},{5,6},{6,7},{7,4},{8,9},{9,10},{10,1... | collective-permute-start | bytes 1671176 | tf_op jit(solution)/shard_map/ppermute | solution.py:813
  175.3 26.3 %collective-permute-start.16 = (bf16[128,2176]{1,0:T(8,128)(2,1)}, bf16[128,2176]{1,0:T(8,128)(2,1)}, u32[]{:S(2)}, u32[]{:S(2)}) collective-permute-start(bf16[128,2176]{1,0:T(8,128)(2,1)} %get-tuple-element.144), channel_id=1, source_target_pairs={{0,3},{1,0},{2,1},{3,2},{4,7},{5,4},{6,5},{7,6},{8,11},{9,8},{10,9... | collective-permute-start | bytes 1671176 | tf_op jit(solution)/shard_map/ppermute | solution.py:813
  184.3 17.3 %collective-permute-start.15 = (bf16[128,2176]{1,0:T(8,128)(2,1)S(1)}, bf16[128,2176]{1,0:T(8,128)(2,1)}, u32[]{:S(2)}, u32[]{:S(2)}) collective-permute-start(bf16[128,2176]{1,0:T(8,128)(2,1)S(1)} %get-tuple-element.143), channel_id=1, source_target_pairs={{0,2},{1,3},{2,0},{3,1},{4,6},{5,7},{6,4},{7,5},{8,10},{9,11},{10,... | collective-permute-start | bytes 1671176 | tf_op jit(solution)/shard_map/ppermute | solution.py:813
  205.9 13.0 %collective-permute-start.19 = (bf16[128,2176]{1,0:T(8,128)(2,1)}, bf16[128,2176]{1,0:T(8,128)(2,1)S(1)}, u32[]{:S(2)}, u32[]{:S(2)}) collective-permute-start(bf16[128,2176]{1,0:T(8,128)(2,1)} %get-tuple-element.155.refs_0_.g0), channel_id=1, source_target_pairs={{0,1},{1,2},{2,3},{3,0},{4,5},{5,6},{6,7},{7,4},{8,9},{9,10},{10,1... | collective-permute-start | bytes 1671176 | tf_op jit(solution)/shard_map/ppermute | solution.py:813
  206.1 13.5 %collective-permute-start.17 = (bf16[128,2176]{1,0:T(8,128)(2,1)}, bf16[128,2176]{1,0:T(8,128)(2,1)S(1)}, u32[]{:S(2)}, u32[]{:S(2)}) collective-permute-start(bf16[128,2176]{1,0:T(8,128)(2,1)} %get-tuple-element.155.refs_0_.g0), channel_id=1, source_target_pairs={{0,3},{1,0},{2,1},{3,2},{4,7},{5,4},{6,5},{7,6},{8,11},{9,8},{10,9... | collective-permute-start | bytes 1671176 | tf_op jit(solution)/shard_map/ppermute | solution.py:813
  218.9 10.3 %collective-permute-start.20 = (bf16[64,2176]{1,0:T(8,128)(2,1)S(1)}, bf16[64,2176]{1,0:T(8,128)(2,1)S(1)}, u32[]{:S(2)}, u32[]{:S(2)}) collective-permute-start(bf16[64,2176]{1,0:T(8,128)(2,1)S(1)} %slice.115), channel_id=1, source_target_pairs={{0,1},{1,2},{2,3},{3,0},{4,5},{5,6},{6,7},{7,4},{8,9},{9,10},{10,1... | collective-permute-start | bytes 835592 | tf_op jit(solution)/shard_map/ppermute | solution.py:813
  219.7 9.5 %collective-permute-start.18 = (bf16[64,2176]{1,0:T(8,128)(2,1)S(1)}, bf16[64,2176]{1,0:T(8,128)(2,1)S(1)}, u32[]{:S(2)}, u32[]{:S(2)}) collective-permute-start(bf16[64,2176]{1,0:T(8,128)(2,1)S(1)} %slice.114), channel_id=1, source_target_pairs={{0,3},{1,0},{2,1},{3,2},{4,7},{5,4},{6,5},{7,6},{8,11},{9,8},{10,9... | collective-permute-start | bytes 835592 | tf_op jit(solution)/shard_map/ppermute | solution.py:813
  221.1 4.8 %collective-permute-start.23 = (bf16[16,512]{1,0:T(8,128)(2,1)S(1)}, bf16[16,512]{1,0:T(8,128)(2,1)S(1)}, u32[]{:S(2)}, u32[]{:S(2)}) collective-permute-start(bf16[16,512]{1,0:T(8,128)(2,1)S(1)} %convolution_convert_fusion.2), channel_id=1, source_target_pairs={{0,1},{1,2},{2,3},{3,0},{4,5},{5,6},{6,7},{7,4},{8,9},{9,10},{10,1... | collective-permute-start | bytes 49160 | tf_op jit(solution)/shard_map/ppermute | solution.py:813
  223.0 4.9 %collective-permute-start.22 = (bf16[16,512]{1,0:T(8,128)(2,1)S(1)}, bf16[16,512]{1,0:T(8,128)(2,1)S(1)}, u32[]{:S(2)}, u32[]{:S(2)}) collective-permute-start(bf16[16,512]{1,0:T(8,128)(2,1)S(1)} %convolution_convert_fusion.2), channel_id=1, source_target_pairs={{0,3},{1,0},{2,1},{3,2},{4,7},{5,4},{6,5},{7,6},{8,11},{9,8},{10,9... | collective-permute-start | bytes 49160 | tf_op jit(solution)/shard_map/ppermute | solution.py:813
  223.2 5.4 %collective-permute-start.21 = (bf16[16,512]{1,0:T(8,128)(2,1)S(1)}, bf16[16,512]{1,0:T(8,128)(2,1)S(1)}, u32[]{:S(2)}, u32[]{:S(2)}) collective-permute-start(bf16[16,512]{1,0:T(8,128)(2,1)S(1)} %convolution_convert_fusion.2), channel_id=1, source_target_pairs={{0,2},{1,3},{2,0},{3,1},{4,6},{5,7},{6,4},{7,5},{8,10},{9,11},{10,... | collective-permute-start | bytes 49160 | tf_op jit(solution)/shard_map/ppermute | solution.py:813
  232.4 123.0 %all-gather.9.cloned.1.call-start = ((), (), s32[]{:S(2)}) async-start(), calls=%async_computation.4 | async-start | bytes 6352896 | tf_op jit(solution)/shard_map/all_gather | solution.py:1133
  232.5 11.4 %collective-permute-start.26 = (bf16[4,128,128]{2,1,0:T(8,128)(2,1)S(1)}, bf16[4,128,128]{2,1,0:T(8,128)(2,1)S(1)}, u32[]{:S(2)}, u32[]{:S(2)}) collective-permute-start(bf16[4,128,128]{2,1,0:T(8,128)(2,1)S(1)} %get-tuple-element.162), channel_id=1, source_target_pairs={{12,0},{13,1},{14,2},{15,3},{28,16},{29,17},{30,18},{31,19},{44,32... | collective-permute-start | bytes 393224 | tf_op jit(solution)/shard_map/ppermute | solution.py:813
  233.2 10.7 %collective-permute-start.25 = (bf16[4,128,128]{2,1,0:T(8,128)(2,1)S(1)}, bf16[4,128,128]{2,1,0:T(8,128)(2,1)S(1)}, u32[]{:S(2)}, u32[]{:S(2)}) collective-permute-start(bf16[4,128,128]{2,1,0:T(8,128)(2,1)S(1)} %get-tuple-element.162), channel_id=1, source_target_pairs={{8,0},{12,4},{9,1},{13,5},{10,2},{14,6},{11,3},{15,7},{24,16},{28,... | collective-permute-start | bytes 393224 | tf_op jit(solution)/shard_map/ppermute | solution.py:813
  234.5 9.5 %collective-permute-start.24 = (bf16[4,128,128]{2,1,0:T(8,128)(2,1)S(1)}, bf16[4,128,128]{2,1,0:T(8,128)(2,1)S(1)}, u32[]{:S(2)}, u32[]{:S(2)}) collective-permute-start(bf16[4,128,128]{2,1,0:T(8,128)(2,1)S(1)} %get-tuple-element.162), channel_id=1, source_target_pairs={{4,0},{8,4},{12,8},{5,1},{9,5},{13,9},{6,2},{10,6},{14,10},{7,3},{... | collective-permute-start | bytes 393224 | tf_op jit(solution)/shard_map/ppermute | solution.py:813
  261.7 6.3 %collective-permute-start.27 = (f32[8,1536]{1,0:T(8,128)}, f32[8,1536]{1,0:T(8,128)S(1)}, u32[]{:S(2)}, u32[]{:S(2)}) collective-permute-start(f32[8,1536]{1,0:T(8,128)} %get-tuple-element.176), channel_id=1, source_target_pairs={{4,0},{8,4},{12,8},{5,1},{9,5},{13,9},{6,2},{10,6},{14,10},{7,3},{... | collective-permute-start | bytes 147464 | tf_op jit(solution)/shard_map/ppermute | solution.py:813
  268.8 16.5 %collective-permute-start.30 = (bf16[512,64]{1,0:T(8,128)(2,1)S(1)}, bf16[512,64]{1,0:T(8,128)(2,1)S(1)}, u32[]{:S(2)}, u32[]{:S(2)}) collective-permute-start(bf16[512,64]{1,0:T(8,128)(2,1)S(1)} %convolution_convert_fusion.1.p0), channel_id=1, source_target_pairs={{0,1},{1,2},{2,3},{3,0},{4,5},{5,6},{6,7},{7,4},{8,9},{9,10},{10,1... | collective-permute-start | bytes 196616 | tf_op jit(solution)/shard_map/ppermute | solution.py:813
  272.3 13.0 %collective-permute-start.29 = (bf16[512,64]{1,0:T(8,128)(2,1)S(1)}, bf16[512,64]{1,0:T(8,128)(2,1)S(1)}, u32[]{:S(2)}, u32[]{:S(2)}) collective-permute-start(bf16[512,64]{1,0:T(8,128)(2,1)S(1)} %convolution_convert_fusion.1.p0), channel_id=1, source_target_pairs={{0,2},{1,3},{2,0},{3,1},{4,6},{5,7},{6,4},{7,5},{8,10},{9,11},{10,... | collective-permute-start | bytes 196616 | tf_op jit(solution)/shard_map/ppermute | solution.py:813
  272.3 13.0 %collective-permute-start.28 = (bf16[512,64]{1,0:T(8,128)(2,1)S(1)}, bf16[512,64]{1,0:T(8,128)(2,1)S(1)}, u32[]{:S(2)}, u32[]{:S(2)}) collective-permute-start(bf16[512,64]{1,0:T(8,128)(2,1)S(1)} %convolution_convert_fusion.1.p0), channel_id=1, source_target_pairs={{0,3},{1,0},{2,1},{3,2},{4,7},{5,4},{6,5},{7,6},{8,11},{9,8},{10,9... | collective-permute-start | bytes 196616 | tf_op jit(solution)/shard_map/ppermute | solution.py:813
  273.3 23.3 %collective-permute-start.38 = (bf16[128,2048]{1,0:T(8,128)(2,1)S(1)}, bf16[128,2048]{1,0:T(8,128)(2,1)S(1)}, u32[]{:S(2)}, u32[]{:S(2)}) collective-permute-start(bf16[128,2048]{1,0:T(8,128)(2,1)S(1)} %fusion.24.refs_0_), channel_id=1, source_target_pairs={{0,3},{1,0},{2,1},{3,2},{4,7},{5,4},{6,5},{7,6},{8,11},{9,8},{10,9... | collective-permute-start | bytes 1572872 | tf_op jit(solution)/shard_map/ppermute | solution.py:813
  275.8 20.8 %collective-permute-start.37 = (bf16[128,2048]{1,0:T(8,128)(2,1)S(1)}, bf16[128,2048]{1,0:T(8,128)(2,1)}, u32[]{:S(2)}, u32[]{:S(2)}) collective-permute-start(bf16[128,2048]{1,0:T(8,128)(2,1)S(1)} %fusion.24.refs_0_), channel_id=1, source_target_pairs={{0,1},{1,2},{2,3},{3,0},{4,5},{5,6},{6,7},{7,4},{8,9},{9,10},{10,1... | collective-permute-start | bytes 1572872 | tf_op jit(solution)/shard_map/ppermute | solution.py:813
  286.8 7.7 %collective-permute-start.34 = (bf16[16,6016]{1,0:T(8,128)(2,1)S(1)}, bf16[16,6016]{1,0:T(8,128)(2,1)S(1)}, u32[]{:S(2)}, u32[]{:S(2)}) collective-permute-start(bf16[16,6016]{1,0:T(8,128)(2,1)S(1)} %get-tuple-element.191), channel_id=1, source_target_pairs={{0,4},{4,8},{8,12},{12,0},{1,5},{5,9},{9,13},{13,1},{2,6},{6,10},{... | collective-permute-start | bytes 577544 | tf_op jit(solution)/shard_map/ppermute | solution.py:813
  286.8 7.7 %collective-permute-start.35 = (bf16[16,6016]{1,0:T(8,128)(2,1)S(1)}, bf16[16,6016]{1,0:T(8,128)(2,1)S(1)}, u32[]{:S(2)}, u32[]{:S(2)}) collective-permute-start(bf16[16,6016]{1,0:T(8,128)(2,1)S(1)} %get-tuple-element.192), channel_id=1, source_target_pairs={{0,8},{4,12},{8,0},{12,4},{1,9},{5,13},{9,1},{13,5},{2,10},{6,14},... | collective-permute-start | bytes 577544 | tf_op jit(solution)/shard_map/ppermute | solution.py:813
  288.3 8.3 %collective-permute-start.36 = (bf16[16,6016]{1,0:T(8,128)(2,1)S(1)}, bf16[16,6016]{1,0:T(8,128)(2,1)S(1)}, u32[]{:S(2)}, u32[]{:S(2)}) collective-permute-start(bf16[16,6016]{1,0:T(8,128)(2,1)S(1)} %get-tuple-element.193), channel_id=1, source_target_pairs={{0,12},{4,0},{8,4},{12,8},{1,13},{5,1},{9,5},{13,9},{2,14},{6,2},{... | collective-permute-start | bytes 577544 | tf_op jit(solution)/shard_map/ppermute | solution.py:813
  297.4 28.7 %collective-permute-start.31 = (bf16[128,2048]{1,0:T(8,128)(2,1)}, bf16[128,2048]{1,0:T(8,128)(2,1)S(1)}, u32[]{:S(2)}, u32[]{:S(2)}) collective-permute-start(bf16[128,2048]{1,0:T(8,128)(2,1)} %get-tuple-element.181), channel_id=1, source_target_pairs={{0,1},{1,2},{2,3},{3,0},{4,5},{5,6},{6,7},{7,4},{8,9},{9,10},{10,1... | collective-permute-start | bytes 1572872 | tf_op jit(solution)/shard_map/ppermute | solution.py:813
  298.6 27.6 %collective-permute-start.32 = (bf16[128,2048]{1,0:T(8,128)(2,1)}, bf16[128,2048]{1,0:T(8,128)(2,1)S(1)}, u32[]{:S(2)}, u32[]{:S(2)}) collective-permute-start(bf16[128,2048]{1,0:T(8,128)(2,1)} %get-tuple-element.182), channel_id=1, source_target_pairs={{0,2},{1,3},{2,0},{3,1},{4,6},{5,7},{6,4},{7,5},{8,10},{9,11},{10,... | collective-permute-start | bytes 1572872 | tf_op jit(solution)/shard_map/ppermute | solution.py:813
  300.9 25.3 %collective-permute-start.33 = (bf16[128,2048]{1,0:T(8,128)(2,1)}, bf16[128,2048]{1,0:T(8,128)(2,1)S(1)}, u32[]{:S(2)}, u32[]{:S(2)}) collective-permute-start(bf16[128,2048]{1,0:T(8,128)(2,1)} %get-tuple-element.183), channel_id=1, source_target_pairs={{0,3},{1,0},{2,1},{3,2},{4,7},{5,4},{6,5},{7,6},{8,11},{9,8},{10,9... | collective-permute-start | bytes 1572872 | tf_op jit(solution)/shard_map/ppermute | solution.py:813
  301.9 17.4 %collective-permute-start.40 = (bf16[64,2048]{1,0:T(8,128)(2,1)S(1)}, bf16[64,2048]{1,0:T(8,128)(2,1)S(1)}, u32[]{:S(2)}, u32[]{:S(2)}) collective-permute-start(bf16[64,2048]{1,0:T(8,128)(2,1)S(1)} %slice.106), channel_id=1, source_target_pairs={{0,1},{1,2},{2,3},{3,0},{4,5},{5,6},{6,7},{7,4},{8,9},{9,10},{10,1... | collective-permute-start | bytes 786440 | tf_op jit(solution)/shard_map/ppermute | solution.py:813
  305.2 17.0 %collective-permute-start.39 = (bf16[64,2048]{1,0:T(8,128)(2,1)S(1)}, bf16[64,2048]{1,0:T(8,128)(2,1)}, u32[]{:S(2)}, u32[]{:S(2)}) collective-permute-start(bf16[64,2048]{1,0:T(8,128)(2,1)S(1)} %slice.105), channel_id=1, source_target_pairs={{0,3},{1,0},{2,1},{3,2},{4,7},{5,4},{6,5},{7,6},{8,11},{9,8},{10,9... | collective-permute-start | bytes 786440 | tf_op jit(solution)/shard_map/ppermute | solution.py:813
  330.9 12.3 %collective-permute-start.43 = (bf16[128,2048]{1,0:T(8,128)(2,1)}, bf16[128,2048]{1,0:T(8,128)(2,1)S(1)}, u32[]{:S(2)}, u32[]{:S(2)}) collective-permute-start(bf16[128,2048]{1,0:T(8,128)(2,1)} %token_rows.1.refs_0_), channel_id=1, source_target_pairs={{0,1},{1,2},{2,3},{3,0},{4,5},{5,6},{6,7},{7,4},{8,9},{9,10},{10,1... | collective-permute-start | bytes 1572872 | tf_op jit(solution)/shard_map/ppermute | solution.py:813
  331.7 13.5 %collective-permute-start.41 = (bf16[128,2048]{1,0:T(8,128)(2,1)}, bf16[128,2048]{1,0:T(8,128)(2,1)S(1)}, u32[]{:S(2)}, u32[]{:S(2)}) collective-permute-start(bf16[128,2048]{1,0:T(8,128)(2,1)} %token_rows.1.refs_0_), channel_id=1, source_target_pairs={{0,3},{1,0},{2,1},{3,2},{4,7},{5,4},{6,5},{7,6},{8,11},{9,8},{10,9... | collective-permute-start | bytes 1572872 | tf_op jit(solution)/shard_map/ppermute | solution.py:813
  343.2 6.4 %collective-permute-start.44 = (bf16[64,2048]{1,0:T(8,128)(2,1)S(1)}, bf16[64,2048]{1,0:T(8,128)(2,1)S(1)}, u32[]{:S(2)}, u32[]{:S(2)}) collective-permute-start(bf16[64,2048]{1,0:T(8,128)(2,1)S(1)} %slice.119), channel_id=1, source_target_pairs={{0,1},{1,2},{2,3},{3,0},{4,5},{5,6},{6,7},{7,4},{8,9},{9,10},{10,1... | collective-permute-start | bytes 786440 | tf_op jit(solution)/shard_map/ppermute | solution.py:813
  345.2 7.7 %collective-permute-start.42 = (bf16[64,2048]{1,0:T(8,128)(2,1)S(1)}, bf16[64,2048]{1,0:T(8,128)(2,1)S(1)}, u32[]{:S(2)}, u32[]{:S(2)}) collective-permute-start(bf16[64,2048]{1,0:T(8,128)(2,1)S(1)} %slice.118), channel_id=1, source_target_pairs={{0,3},{1,0},{2,1},{3,2},{4,7},{5,4},{6,5},{7,6},{8,11},{9,8},{10,9... | collective-permute-start | bytes 786440 | tf_op jit(solution)/shard_map/ppermute | solution.py:813
  (71 other events, 544.2 us)
Sparse Core Ops, SparseCore 0:
  10.9 56.3 all-gather.4
  69.5 75.0 all-gather.6
  232.6 28.0 reduce-scatter.1
  297.5 48.5 all-gather.8

commit v4 on v3

--- a/solution.py
+++ b/solution.py
@@ -8,7 +8,7 @@
 from jax.sharding import PartitionSpec as P
 
 EPSILON = 1e-06
-HALO = 8
+HALO = 16
 CHUNK = 128
 LANES = 128
 F32 = jnp.float32
@@ -212,8 +212,9 @@
 
 def attend_kernel(
     position_ref, place_ref, op_ref, qp_ref, one_ref, two_ref, map_ref, three_ref, gain_ref, weight_ref,
-    out_ref, att_ref, state_ref, *part_refs,
+    state_ref, *refs,
 ):
+    *part_refs, out_ref = refs
     heads, head_dim = one_ref.shape[0], one_ref.shape[1]
     owners = len(part_refs)
     share = out_ref.shape[0] // owners
@@ -222,8 +223,7 @@
         through = one_ref[head].astype(F32) + dot_low(map_ref[head], three_ref[head])
         state = jnp.where(position_ref[0] == 2, two_ref[head].astype(F32), through)
         state_ref[head] = state.astype(BF16)
-        attended = op_ref[:, columns] + dot_low(qp_ref[:, columns], state)
-        att_ref[:, columns] = attended
+        attended = op_ref[:, columns] + dot_low(qp_ref[:, columns], state_ref[head])
         scale = lax.rsqrt(jnp.mean(attended * attended, axis=-1, keepdims=True) + EPSILON)
         out_ref[:, columns] = (attended * scale * gain_ref[...]).astype(BF16)
     for k, part_ref in enumerate(part_refs):
@@ -239,22 +239,18 @@
     return pl.pallas_call(
         attend_kernel,
         in_specs=[smem] * 2 + [vmem] * 8,
-        out_specs=[vmem] * (3 + owners),
-        out_shape=[
-            jax.ShapeDtypeStruct(op.shape, BF16),
-            jax.ShapeDtypeStruct(op.shape, F32),
-            jax.ShapeDtypeStruct(one.shape, BF16),
-        ]
-        + [part] * owners,
+        out_specs=[vmem] * (1 + owners),
+        out_shape=[jax.ShapeDtypeStruct(one.shape, BF16)] + [part] * owners,
+        scratch_shapes=[pltpu.VMEM(op.shape, BF16)],
         compiler_params=pltpu.CompilerParams(vmem_limit_bytes=14 * MIB),
         name="attend",
     )(position, place, op, qp, one, two, mapped, three, gain, weight)
 
 
 def attend_back_kernel(
-    place_ref, att_ref, qp_ref, gain_ref, weight_ref, *refs
+    place_ref, op_ref, qp_ref, state_ref, gain_ref, weight_ref, *refs
 ):
-    *block_refs, out_ref, own_ref, grad_ref = refs
+    *block_refs, out_ref, own_ref, low_ref, grad_ref, head_ref = refs
     heads, head_dim = own_ref.shape[0], own_ref.shape[1]
     owners = len(block_refs)
     share = out_ref.shape[0] // owners
@@ -265,29 +261,37 @@
         )
     for head in range(heads):
         columns = slice(head * head_dim, (head + 1) * head_dim)
-        attended = att_ref[:, columns]
+        attended = op_ref[:, columns] + dot_low(qp_ref[:, columns], state_ref[head])
         scale = lax.rsqrt(jnp.mean(attended * attended, axis=-1, keepdims=True) + EPSILON)
+        head_ref[:, columns] = (attended * scale * gain_ref[...]).astype(BF16)
         gained = grad_ref[:, columns] * gain_ref[...]
         along = jnp.mean(attended * gained, axis=-1, keepdims=True)
         grad = (scale * gained - attended * (scale * scale * scale * along)).astype(BF16)
         out_ref[:, columns] = grad
         own_ref[head] = dot_low(qp_ref[:, columns], grad, 0, 0).astype(BF16)
-
-
-def attend_back(place, attended, qp, gain, weight, blocks, heads, head_dim):
+    total = 0.0
+    for k, block_ref in enumerate(block_refs):
+        start = lax.rem(place_ref[0] + k, owners) * share
+        rows = head_ref[pl.ds(pl.multiple_of(start, share), share), :]
+        total = total + dot_low(block_ref[:, block_ref.shape[1] - LANES :], rows, 0, 0)
+    low_ref[...] = total[: low_ref.shape[0]]
+
+
+def attend_back(place, op, qp, state, gain, weight, blocks, rank):
     vmem = pl.BlockSpec(memory_space=pltpu.VMEM)
     return pl.pallas_call(
         attend_back_kernel,
-        in_specs=[pl.BlockSpec(memory_space=pltpu.SMEM)] + [vmem] * (4 + len(blocks)),
-        out_specs=[vmem] * 2,
+        in_specs=[pl.BlockSpec(memory_space=pltpu.SMEM)] + [vmem] * (5 + len(blocks)),
+        out_specs=[vmem] * 3,
         out_shape=[
-            jax.ShapeDtypeStruct(attended.shape, BF16),
-            jax.ShapeDtypeStruct((heads, head_dim, head_dim), BF16),
+            jax.ShapeDtypeStruct(op.shape, BF16),
+            jax.ShapeDtypeStruct(state.shape, BF16),
+            jax.ShapeDtypeStruct((rank, op.shape[1]), F32),
         ],
-        scratch_shapes=[pltpu.VMEM(attended.shape, F32)],
+        scratch_shapes=[pltpu.VMEM(op.shape, F32), pltpu.VMEM(op.shape, BF16)],
         compiler_params=pltpu.CompilerParams(vmem_limit_bytes=14 * MIB),
         name="attend_back",
-    )(place, attended, qp, gain, weight, *blocks)
+    )(place, op, qp, state, gain, weight, *blocks)
 
 
 def delta_back_kernel(
@@ -560,20 +564,16 @@
 
 
 def early_kernel(
-    place_ref, g0, g1, g2, g3, x0, x1, x2, x3, head_ref, low_down_ref, cot_ref,
+    g0, g1, g2, g3, x0, x1, x2, x3, heads_ref, low_down_ref, cot_ref,
     out_one, out_two, down_one, down_two, pack_ref, *, rank,
 ):
     model = cot_ref.shape[1]
     hidden_units = down_one.shape[1]
-    owners, share = 4, g0.shape[0]
-    through_g, through_x, through_h = 0.0, 0.0, 0.0
-    for k, (g_ref, x_ref) in enumerate(zip((g0, g1, g2, g3), (x0, x1, x2, x3))):
+    through_g, through_x = 0.0, 0.0
+    for g_ref, x_ref in zip((g0, g1, g2, g3), (x0, x1, x2, x3)):
         low = g_ref[:, model:]
-        start = lax.rem(place_ref[0] + k, owners) * share
-        heads = head_ref[pl.ds(pl.multiple_of(start, share), share), :]
         through_g = through_g + dot_low(low, g_ref[:, :model], 0, 0)
         through_x = through_x + dot_low(low, x_ref[:, :model], 0, 0)
-        through_h = through_h + dot_low(low, heads, 0, 0)
     out_terms = out_one[...] + out_two[...]
     pack_ref[0, :, :model] = through_x[2 * rank : 3 * rank].astype(BF16)
     pack_ref[0, :, model:] = out_terms[:rank, :hidden_units].astype(BF16)
@@ -583,7 +583,7 @@
     pack_ref[2, :, model:] = (down_one[...] + down_two[...]).astype(BF16)
     pack_ref[3, :, :model] = through_g[rank : 2 * rank].astype(BF16)
     pack_ref[3, :, model:] = jnp.zeros((rank, hidden_units), BF16)
-    pack_ref[3, :, model : model + through_h.shape[1]] = through_h[:rank].astype(BF16)
+    pack_ref[3, :, model : model + heads_ref.shape[1]] = heads_ref[...].astype(BF16)
 
 
 def late_kernel(
@@ -597,8 +597,8 @@
     )
     low_grad = total.astype(BF16)
     low_out_ref[...] = low_grad
-    items = dot_low(low_grad, normed_ref[...], 0, 0)
-    blocks = dot_low(low_ref[...], grad_ref[...], 0, 0)
+    items = dot_low(low_grad, normed_ref[HALO:, :], 0, 0)
+    blocks = dot_low(low_ref[HALO:, :], grad_ref[...], 0, 0)
     for part in range(4):
         rows = slice(part * rank, (part + 1) * rank)
         pack_ref[part, :, :model] = items[rows].astype(BF16)
@@ -992,8 +992,6 @@
     picks = picks.astype(jnp.int32)
 
     projected = dot(normed_ext, weight_in) + dot(low_ext, low_in)
-    normed = normed_ext[HALO:]
-    low_attn = low_ext[HALO:]
 
     where = position[None]
     here = place[None]
@@ -1011,7 +1009,7 @@
     two = lax.ppermute(second, "context", [(1, 2)])
     three = lax.ppermute(second, "context", [(1, 3)])
     gain_row = head_norm_gain[None, :]
-    head_low, attended, state, *branch_parts = attend(
+    state, *branch_parts = attend(
         where, here, op, qp, one, two, linear_two, three, gain_row, out_ext, owners
     )
     wide = model + LANES
@@ -1059,8 +1057,8 @@
     low_down = paired_sum(down_low, "tensor").astype(BF16)
     grad_blocks, low_down = lax.optimization_barrier((grad_blocks, low_down))
 
-    grad_attended, own = attend_back(
-        here, attended, qp, gain_row, out_ext, grad_blocks, heads, head_dim
+    grad_attended, own, grad_o_in = attend_back(
+        here, op, qp, state, gain_row, out_ext, grad_blocks, rank
     )
     down_all, own = lax.optimization_barrier((down_all, own))
     down_sum = lax.psum_scatter(down_all, "tensor", scatter_dimension=0, tiled=True).astype(F32)
@@ -1069,8 +1067,8 @@
     own_one = shifted(own, "context", -1, wrap=False)
     early_width = model + hidden_units
     (early,) = span_call(
-        functools.partial(early_kernel, rank=rank), "early_terms", (here,),
-        [*grad_blocks, *ffn_in, head_low, low_down, cotangent, *ffn_out_terms, *down_in_terms],
+        functools.partial(early_kernel, rank=rank), "early_terms", (),
+        [*grad_blocks, *ffn_in, grad_o_in, low_down, cotangent, *ffn_out_terms, *down_in_terms],
         [((4, rank, early_width), BF16)], [], 56,
     )
     own_one, own_two, own_three, early = lax.optimization_barrier(
@@ -1102,7 +1100,7 @@
     late_width = model + features
     low_grad_attn, *quarters = span_call(
         functools.partial(late_kernel, rank=rank), "late_terms", (where,),
-        [*low_parts, normed, low_attn, grad_projected, early],
+        [*low_parts, normed_ext, low_ext, grad_projected, early],
         [((span, 4 * rank), BF16)] + [((rank, early_width + late_width), BF16)] * 4,
         [pltpu.VMEM((4, rank, late_width), BF16)], 24,
     )
@@ -1118,8 +1116,8 @@
         ],
         axis=0,
     )
+    *normed_sent, block_far, picks = lax.optimization_barrier((*normed_sent, block_far, picks))
     block_out = in_place(here, [block_own, block_after, block_far, block_before], model, BF16)
-    *normed_sent, block_out, picks = lax.optimization_barrier((*normed_sent, block_out, picks))
     (grad_tokens,) = owner_call(
         tokens_kernel, "token_rows", here, share,
         [(part, "rows") for part in normed_sent]
@@ -1127,12 +1125,12 @@
            (mixer_norm_gain[None, :], "whole"), (grad_middle, "rows")],
         [((share, model), BF16)],
     )
-    tokens_grad = in_place(here, blocks_by_ring(grad_tokens, "tensor"), model, F32)
+    token_blocks, block_out = blocks_by_ring(grad_tokens, "tensor", block_out)
+    tokens_grad = in_place(here, token_blocks, model, F32)
 
     quarter = sum(part.astype(F32) for part in quarters).astype(BF16)
     terms = lax.all_gather(quarter, everyone, axis=0, tiled=False)
-    sequences = lax.axis_size("weights")
-    terms = terms.reshape(sequences, 4, rank, -1)
+    terms = terms.reshape(lax.axis_size("weights"), 4, rank, -1)
     cuts = (0, model, model + hidden_units, 2 * model + hidden_units)
     sums = totals(
         picks, terms, cuts, adapters, rank, model, features, hidden_units, heads

time: 379 us -> 378 us (level)
  waiting for transfers between devices: 130 us -> 115 us
  starting transfers between devices: 63.2 us -> 72.2 us
    ppermute x41, waiting for transfers between devices: 88.2 us -> 75.4 us  [shifted(): return lax.ppermute(block, axis, route)]
    ppermute x41, starting transfers between devices: 57.7 us -> 66 us  [shifted(): return lax.ppermute(block, axis, route)]
    unnamed x143 -> x153, local copies, waits for them, and re-layouts: 9.09 us -> 11.1 us
where the time goes in v4:
time: 378 us; the launch traced here: 370 us
  waiting for transfers between devices  115 us (30%)
  Pallas kernels  84.1 us (22%)
  starting transfers between devices  72.2 us (19%)
  matrix products  39.7 us (11%)
  local copies, waits for them, and re-layouts  34.6 us (9%)
  between operations  16.3 us (4%)
  other arithmetic  7.96 us (2%)
    ppermute x41, waiting for transfers between devices, shifted(): return lax.ppermute(block, axis, route)  75.4 us
    ppermute x41, starting transfers between devices, shifted(): return lax.ppermute(block, axis, route)  66 us
    all_gather x1, waiting for transfers between devices, on_device(): mixer_all = lax.all_gather(mixer_pack, everyone, axis=0, tiled=True)  33.2 us
    dot_general x6, matrix products, dot_nt(): lax.dot_general(left, right, (((1,), (1,)), ((), ())), preferred_element_...  19.1 us
    dot_general x4, matrix products, dot(): return jnp.dot(left, right, preferred_element_type=F32)  18.1 us
    pallas_call x2, Pallas kernels, ffn_rows(): pl.pallas_call(functools.partial(ffn_kernel, count=count, strip=512), in_...  18 us
    pallas_call x1, Pallas kernels, delta_back(): pl.pallas_call(functools.partial(delta_back_kernel, span=span, heads=head...  17.1 us
    pallas_call x3, Pallas kernels, owner_call(): pl.pallas_call(kernel, grid_spec=pltpu.PrefetchScalarGridSpec(num_scalar_...  11.5 us
  transfers between devices with their start and end apart: 49, of which 21 were waited for; matrix products, arithmetic and copies ran while one was open for 18% of the time, Pallas kernels for 18%

profile of v4, /device:TPU:28, one launch (start us, length us, event | category | flops | bytes accessed | tf_op | source)
XLA Modules:
  0.0 370.1 jit_solution(14455272945632873956)
XLA Ops:
  13.5 3.1 collective-permute-start
  24.1 3.0 convolution_convert_fusion.3
  31.0 2.5 fusion.53
  34.1 33.2 %all-gather.5.cloned.1.call-done = bf16[2048,2176]{1,0:T(8,128)(2,1)} async-done(((bf16[64,2176]{1,0:T(8,128)(2,1)}), bf16[2048,2176]{1,0:T(8,128)(2,1)}) %all-gather.5.cloned.1.call-update) | async-done | bytes 8912912 | tf_op jit(solution)/shard_map/all_gather | solution.py:934
  67.3 8.6 %fusion.15.q_ref.k_ref.v_ref.logit_ref = f32[528,1664]{1,0:T(8,128)S(1)} fusion(f32[528,1664]{1,0:T(8,128)} %fusion.53, bf16[528,2048]{1,0:T(8,128)(2,1)} %copy-done.3, bf16[2048,2176]{1,0:T(8,128)(2,1)} %all-gather.5.cloned.1.call-done), kind=kOutput, calls=%fused_computation.17 | convolution fusion | flops 3599591424 | bytes 16007168 | tf_op jit(solution)/shard_map/dot_general | solution.py:848
  76.1 10.4 %delta_local.1 = (bf16[512,512]{1,0:T(8,128)(2,1)S(1)}, f32[512,512]{1,0:T(8,128)S(1)}, bf16[4,128,128]{2,1,0:T(8,128)(2,1)S(1)}, bf16[4,128,128]{2,1,0:T(8,128)...) custom-call(f32[528,1664]{1,0:T(8,128)S(1)} %fusion.15.q_ref.k_ref.v, ...), custom_call_target="tpu_custom_call" | custom-call | tf_op jit(solution)/shard_map/delta_local/pallas_call | solution.py:181
  87.3 3.3 collective-permute-start.1
  92.5 2.8 collective-permute-done.1.one_ref
  99.9 3.5 collective-permute-done.2.two_ref
  103.5 3.6 attend.1
  108.4 2.4 collective-permute-start.6
  111.5 5.4 %collective-permute-start.8 = (bf16[4,128,128]{2,1,0:T(8,128)(2,1)}, bf16[4,128,128]{2,1,0:T(8,128)(2,1)}, u32[]{:S(2)}, u32[]{:S(2)}) collective-permute-start(bf16[4,128,128]{2,1,0:T(8,128)(2,1)} %get-tuple-element.126), channel_id=1, source_target_pairs={{4,0},{8,4},{12,8},{5,1},{9,5},{13,9},{6,2},{10,6},{14,10},{7,3},{... | collective-permute-start | bytes 393224 | tf_op jit(solution)/shard_map/ppermute | solution.py:813
  116.9 2.3 collective-permute-start.9
  126.9 8.0 %collective-permute-done.7.three_ref = bf16[128,2176]{1,0:T(8,128)(2,1)} collective-permute-done((bf16[128,2176]{1,0:T(8,128)(2,1)S(1)}, bf16[128,2176]{1,0:T(8,128)(2,1)}, u32[]{:S(2)}, u32[]{:S(2)}) %collective-permute-start.7) | collective-permute-done | bytes 557088 | tf_op jit(solution)/shard_map/ppermute | solution.py:813
  134.9 3.8 %middle_rows.1 = (f32[128,2048]{1,0:T(8,128)}, bf16[128,2176]{1,0:T(8,128)(2,1)}, bf16[128,128]{1,0:T(8,128)(2,1)}) custom-call(s32[1]{0:T(128)} %bitcast.place_ref, bf16[128,2176]{1,0:T(8,128)(2,1)} %copy-done.30, bf16[128,2176]{1,0:T(8,128)(2,1)} %collective-permute-done.5.one_ref, bf16[128,2176]{1,0:T(8,128)(2,1)} %collective-permute-done.6.two_ref, ...), custom_call_target="tpu_custom_call" | custom-call | tf_op jit(solution)/shard_map/middle_rows/pallas_call | solution.py:552
  140.8 3.1 all-gather.7.cloned.1.call-done
  143.9 6.5 %fusion.12 = f32[512,1408]{1,0:T(8,128)S(1)} fusion(bf16[512,2048]{1,0:T(8,128)(2,1)} %cot_ref.3, bf16[2048,4224]{1,0:T(8,128)(2,1)} %all-gather.7.cloned.1.call-done), kind=kOutput, calls=%fused_computation.16 | convolution fusion | flops 2952790016 | bytes 10747904 | tf_op jit(solution)/shard_map/dot_general | solution.py:848
  151.0 2.7 collective-permute-done.10.refs_1_.x3
  155.6 2.9 collective-permute-start.13
  159.4 9.4 %ffn_rows.3 = (bf16[256,1408]{1,0:T(8,128)(2,1)S(1)}, bf16[128,2176]{1,0:T(8,128)(2,1)}, bf16[128,2176]{1,0:T(8,128)(2,1)}, f32[32,2816]{1,0:T(8,128)S(1)}, f32[16,1408]{1,0:T(8,128)S(1)}) custom-call(s32[2]{0:T(128)S(1)} %pad_add_fusion.1.place_ref, bf16[2048,2816]{1,0:T(8,128)(2,1)S(1)} %slice.104.weight_ref, bf16[128,2816]{1,0:T(8,128)(2,1)S(1)} %copy-done.28, ...), custom_call_target="tpu_custom_call" | custom-call | flops 6274678784 | bytes 12255232 | tf_op jit(solution)/shard_map/ffn_rows/pallas_call | solution.py:675
  171.1 8.6 %ffn_rows.2 = (bf16[256,1408]{1,0:T(8,128)(2,1)S(1)}, bf16[128,2176]{1,0:T(8,128)(2,1)S(1)}, bf16[128,2176]{1,0:T(8,128)(2,1)S(1)}, f32[32,2816]{1,0:T(8,128)S(1)}, f32[16,1408]{1,0:T(8,128)S(1)}) custom-call(s32[2]{0:T(128)S(1)} %pad_add_fusion.place_ref, bf16[2048,2816]{1,0:T(8,128)(2,1)S(1)} %slice.104.weight_ref, bf16[128,2816]{1,0:T(8,128)(2,1)S(1)} %copy-done.28, ...), custom_call_target="tpu_custom_call" | custom-call | flops 6274678784 | bytes 12255232 | tf_op jit(solution)/shard_map/ffn_rows/pallas_call | solution.py:675
  182.0 4.7 %fusion.21 = bf16[512,2048]{1,0:T(8,128)(2,1)} fusion(bf16[512,1408]{1,0:T(8,128)(2,1)S(1)} %in_place.3, bf16[2048,4224]{1,0:T(8,128)(2,1)S(1)} %copy-done.47), kind=kOutput, calls=%fused_computation.19 | convolution fusion | flops 2953838592 | bytes 9306112 | tf_op jit(solution)/shard_map/dot_general | solution.py:852
  186.7 8.1 %collective-permute-done.16.three_ref = bf16[128,2176]{1,0:T(8,128)(2,1)} collective-permute-done((bf16[128,2176]{1,0:T(8,128)(2,1)}, bf16[128,2176]{1,0:T(8,128)(2,1)}, u32[]{:S(2)}, u32[]{:S(2)}) %collective-permute-start.16) | collective-permute-done | bytes 557088 | tf_op jit(solution)/shard_map/ppermute | solution.py:813
  194.8 4.3 %back_rows.1 = (f32[128,2048]{1,0:T(8,128)}, bf16[128,2176]{1,0:T(8,128)(2,1)}) custom-call(s32[1]{0:T(128)} %bitcast.place_ref, bf16[128,2176]{1,0:T(8,128)(2,1)} %copy-done.29, bf16[128,2176]{1,0:T(8,128)(2,1)} %copy-done.51, bf16[128,2176]{1,0:T(8,128)(2,1)} %collective-permute-done.15.two_ref, bf16[128,2176]{1,0:T(8,128)(2,1)} %collective-permute-done.16.three_ref, ...), custom_call_target="tpu_custom_call" | custom-call | tf_op jit(solution)/shard_map/back_rows/pallas_call | solution.py:552
  201.3 9.3 %collective-permute-done.19.refs_3_.g3 = bf16[128,2176]{1,0:T(8,128)(2,1)S(1)} collective-permute-done((bf16[128,2176]{1,0:T(8,128)(2,1)}, bf16[128,2176]{1,0:T(8,128)(2,1)S(1)}, u32[]{:S(2)}, u32[]{:S(2)}) %collective-permute-start.19) | collective-permute-done | bytes 557088 | tf_op jit(solution)/shard_map/ppermute | solution.py:813
  210.6 3.7 collective-permute-start.20
  214.3 3.2 collective-permute-start.23
  219.2 3.3 collective-permute-done.22
  223.7 2.5 attend_back.1
  230.4 2.8 collective-permute-start.25
  233.8 5.4 %early_terms.1.early_ref = bf16[4,16,3456]{2,1,0:T(8,128)(2,1)} custom-call(bf16[128,2176]{1,0:T(8,128)(2,1)} %get-tuple-element.156.refs_0_.g0, bf16[128,2176]{1,0:T(8,128)(2,1)} %copy-done.9, bf16[128,2176]{1,0:T(8,128)(2,1)} %copy-done.5, bf16[128,2176]{1,0:T(8,128)(2,1)} %copy-done.8, bf16[128,2176]{1,0:T(8,128)(2,1)} %get-tuple-element.138.refs_1_.x0, ...), custom_call_target="tpu_custom_call" | custom-call | tf_op jit(solution)/shard_map/early_terms/pallas_call | solution.py:619
  240.0 17.1 %delta_back.1 = (bf16[512,1664]{1,0:T(8,128)(2,1)}, f32[16,1536]{1,0:T(8,128)}, f32[16,1536]{1,0:T(8,128)}) custom-call(f32[512,512]{1,0:T(8,128)} %copy-done.24, f32[512,512]{1,0:T(8,128)} %copy-done.25, f32[512,512]{1,0:T(8,128)} %copy-done.26, f32[528,1664]{1,0:T(8,128)} %copy-done.2, f32[4,1536]{1,0:T(4,128)} %bitcast.79, f32[4,1536]{1,0:T(4,128)} %bitcast.80, ...), custom_call_target="tpu_custom_call" | custom-call | tf_op jit(solution)/shard_map/delta_back/pallas_call | solution.py:446
  257.1 3.7 collective-permute-start.27
  262.3 3.1 collective-permute-done.27
  268.8 4.2 %collective-permute-start.29 = (bf16[512,64]{1,0:T(8,128)(2,1)S(1)}, bf16[512,64]{1,0:T(8,128)(2,1)S(1)}, u32[]{:S(2)}, u32[]{:S(2)}) collective-permute-start(bf16[512,64]{1,0:T(8,128)(2,1)S(1)} %convolution_convert_fusion.1.p0), channel_id=1, source_target_pairs={{0,2},{1,3},{2,0},{3,1},{4,6},{5,7},{6,4},{7,5},{8,10},{9,11},{10,... | collective-permute-start | bytes 196616 | tf_op jit(solution)/shard_map/ppermute | solution.py:813
  275.4 7.2 %fusion.18 = bf16[512,2048]{1,0:T(8,128)(2,1)S(1)} fusion(bf16[512,1664]{1,0:T(8,128)(2,1)S(1)} %copy-done.16, bf16[2048,2176]{1,0:T(8,128)(2,1)} %all-gather.5.cloned.1.call-done), kind=kOutput, calls=%fused_computation.18 | convolution fusion | flops 3490709504 | bytes 10616832 | tf_op jit(solution)/shard_map/dot_general | solution.py:852
  288.7 2.6 collective-permute-start.36
  298.9 2.3 collective-permute-start.32
  301.3 3.3 collective-permute-start.40
  307.1 13.0 %collective-permute-done.40 = bf16[64,2048]{1,0:T(8,128)(2,1)} collective-permute-done((bf16[64,2048]{1,0:T(8,128)(2,1)S(1)}, bf16[64,2048]{1,0:T(8,128)(2,1)}, u32[]{:S(2)}, u32[]{:S(2)}) %collective-permute-start.40) | collective-permute-done | bytes 262176 | tf_op jit(solution)/shard_map/ppermute | solution.py:813
  320.1 2.9 collective-permute-done.39
  325.2 3.4 token_rows.1.refs_0_
  332.5 7.5 %collective-permute-done.41.refs_3_ = bf16[128,2048]{1,0:T(8,128)(2,1)S(1)} collective-permute-done((bf16[128,2048]{1,0:T(8,128)(2,1)}, bf16[128,2048]{1,0:T(8,128)(2,1)S(1)}, u32[]{:S(2)}, u32[]{:S(2)}) %collective-permute-start.41) | collective-permute-done | bytes 524320 | tf_op jit(solution)/shard_map/ppermute | solution.py:813
  340.5 2.3 collective-permute-start.44
  342.9 4.0 %collective-permute-done.44 = bf16[64,2048]{1,0:T(8,128)(2,1)S(1)} collective-permute-done((bf16[64,2048]{1,0:T(8,128)(2,1)S(1)}, bf16[64,2048]{1,0:T(8,128)(2,1)S(1)}, u32[]{:S(2)}, u32[]{:S(2)}) %collective-permute-start.44) | collective-permute-done | bytes 262176 | tf_op jit(solution)/shard_map/ppermute | solution.py:813
  346.9 3.5 collective-permute-done.43
  350.5 2.5 in_place.5
  353.0 10.1 %totals.1 = (f32[4,8,16,2048]{3,2,1,0:T(8,128)}, f32[3,8,16,512]{3,2,1,0:T(8,128)}, f32[8,4,16]{2,1,0:T(4,128)}, f32[8,16,512]{2,1,0:T(8,128)}, f32[8,16,2048]{2...) custom-call(s32[8]{0:T(128)} %convert_reduce_fusion.pick_ref, ...), custom_call_target="tpu_custom_call" | custom-call | tf_op jit(solution)/shard_map/totals/pallas_call | solution.py:779
  (287 shorter events, 84.7 us)
Async XLA Ops:
  7.2 60.1 %all-gather.5.cloned.1.call-start = ((), (), s32[]{:S(2)}) async-start(), calls=%async_computation.1 | async-start | bytes 9191424 | tf_op jit(solution)/shard_map/all_gather | solution.py:934
  10.6 133.3 %all-gather.7.cloned.1.call-start = ((), (), s32[]{:S(2)}) async-start(), calls=%async_computation.2 | async-start | bytes 17842176 | tf_op jit(solution)/shard_map/all_gather | solution.py:935
  12.6 248.2 %reduce-scatter.2.cloned.1.call-start = ((), (), s32[]{:S(2)}) async-start(), calls=%async_computation.3 | async-start | bytes 2621440 | tf_op jit(solution)/shard_map/reduce_scatter | solution.py:1064
  13.5 14.2 %collective-permute-start = (bf16[16,2048]{1,0:T(8,128)(2,1)S(1)}, bf16[16,2048]{1,0:T(8,128)(2,1)S(1)}, u32[]{:S(2)}, u32[]{:S(2)}) collective-permute-start(bf16[16,2048]{1,0:T(8,128)(2,1)S(1)} %slice.78), channel_id=1, source_target_pairs={{0,4},{4,8},{8,12},{1,5},{5,9},{9,13},{2,6},{6,10},{10,14},{3,7},{... | collective-permute-start | bytes 196616 | tf_op jit(solution)/shard_map/ppermute | solution.py:813
  87.3 8.0 %collective-permute-start.1 = (bf16[4,128,128]{2,1,0:T(8,128)(2,1)S(1)}, bf16[4,128,128]{2,1,0:T(8,128)(2,1)S(1)}, u32[]{:S(2)}, u32[]{:S(2)}) collective-permute-start(bf16[4,128,128]{2,1,0:T(8,128)(2,1)S(1)} %get-tuple-element.125), channel_id=1, source_target_pairs={{0,4},{4,8},{8,12},{1,5},{5,9},{9,13},{2,6},{6,10},{10,14},{3,7},{... | collective-permute-start | bytes 393224 | tf_op jit(solution)/shard_map/ppermute | solution.py:813
  90.6 9.3 %collective-permute-start.3 = (bf16[4,128,128]{2,1,0:T(8,128)(2,1)}, bf16[4,128,128]{2,1,0:T(8,128)(2,1)S(1)}, u32[]{:S(2)}, u32[]{:S(2)}) collective-permute-start(bf16[4,128,128]{2,1,0:T(8,128)(2,1)} %get-tuple-element.126), channel_id=1, source_target_pairs={{8,12},{9,13},{10,14},{11,15},{24,28},{25,29},{26,30},{27,31},{40,... | collective-permute-start | bytes 393224 | tf_op jit(solution)/shard_map/ppermute | solution.py:1002
  96.4 7.0 %collective-permute-start.2 = (bf16[4,128,128]{2,1,0:T(8,128)(2,1)S(1)}, bf16[4,128,128]{2,1,0:T(8,128)(2,1)S(1)}, u32[]{:S(2)}, u32[]{:S(2)}) collective-permute-start(bf16[4,128,128]{2,1,0:T(8,128)(2,1)S(1)} %add_convert_fusion.1), channel_id=1, source_target_pairs={{4,8},{5,9},{6,10},{7,11},{20,24},{21,25},{22,26},{23,27},{36,40},... | collective-permute-start | bytes 393224 | tf_op jit(solution)/shard_map/ppermute | solution.py:1009
  97.8 5.6 %collective-permute-start.4 = (bf16[4,128,128]{2,1,0:T(8,128)(2,1)S(1)}, bf16[4,128,128]{2,1,0:T(8,128)(2,1)S(1)}, u32[]{:S(2)}, u32[]{:S(2)}) collective-permute-start(bf16[4,128,128]{2,1,0:T(8,128)(2,1)S(1)} %add_convert_fusion.1), channel_id=1, source_target_pairs={{4,12},{5,13},{6,14},{7,15},{20,28},{21,29},{22,30},{23,31},{36,44... | collective-permute-start | bytes 393224 | tf_op jit(solution)/shard_map/ppermute | solution.py:1010
  107.9 19.0 %collective-permute-start.5 = (bf16[128,2176]{1,0:T(8,128)(2,1)}, bf16[128,2176]{1,0:T(8,128)(2,1)}, u32[]{:S(2)}, u32[]{:S(2)}) collective-permute-start(bf16[128,2176]{1,0:T(8,128)(2,1)} %get-tuple-element.131), channel_id=1, source_target_pairs={{0,1},{1,2},{2,3},{3,0},{4,5},{5,6},{6,7},{7,4},{8,9},{9,10},{10,1... | collective-permute-start | bytes 1671176 | tf_op jit(solution)/shard_map/ppermute | solution.py:813
  108.4 18.5 %collective-permute-start.6 = (bf16[128,2176]{1,0:T(8,128)(2,1)S(1)}, bf16[128,2176]{1,0:T(8,128)(2,1)}, u32[]{:S(2)}, u32[]{:S(2)}) collective-permute-start(bf16[128,2176]{1,0:T(8,128)(2,1)S(1)} %get-tuple-element.132), channel_id=1, source_target_pairs={{0,2},{1,3},{2,0},{3,1},{4,6},{5,7},{6,4},{7,5},{8,10},{9,11},{10,... | collective-permute-start | bytes 1671176 | tf_op jit(solution)/shard_map/ppermute | solution.py:813
  110.8 24.1 %collective-permute-start.7 = (bf16[128,2176]{1,0:T(8,128)(2,1)S(1)}, bf16[128,2176]{1,0:T(8,128)(2,1)}, u32[]{:S(2)}, u32[]{:S(2)}) collective-permute-start(bf16[128,2176]{1,0:T(8,128)(2,1)S(1)} %get-tuple-element.133), channel_id=1, source_target_pairs={{0,3},{1,0},{2,1},{3,2},{4,7},{5,4},{6,5},{7,6},{8,11},{9,8},{10,9... | collective-permute-start | bytes 1671176 | tf_op jit(solution)/shard_map/ppermute | solution.py:813
  111.5 15.4 %collective-permute-start.8 = (bf16[4,128,128]{2,1,0:T(8,128)(2,1)}, bf16[4,128,128]{2,1,0:T(8,128)(2,1)}, u32[]{:S(2)}, u32[]{:S(2)}) collective-permute-start(bf16[4,128,128]{2,1,0:T(8,128)(2,1)} %get-tuple-element.126), channel_id=1, source_target_pairs={{4,0},{8,4},{12,8},{5,1},{9,5},{13,9},{6,2},{10,6},{14,10},{7,3},{... | collective-permute-start | bytes 393224 | tf_op jit(solution)/shard_map/ppermute | solution.py:813
  116.9 10.0 %collective-permute-start.9 = (bf16[4,128,128]{2,1,0:T(8,128)(2,1)}, bf16[4,128,128]{2,1,0:T(8,128)(2,1)}, u32[]{:S(2)}, u32[]{:S(2)}) collective-permute-start(bf16[4,128,128]{2,1,0:T(8,128)(2,1)} %get-tuple-element.126), channel_id=1, source_target_pairs={{8,0},{9,1},{10,2},{11,3},{24,16},{25,17},{26,18},{27,19},{40,32},... | collective-permute-start | bytes 393224 | tf_op jit(solution)/shard_map/ppermute | solution.py:1018
  138.7 15.0 %collective-permute-start.10 = (bf16[128,2176]{1,0:T(8,128)(2,1)}, bf16[128,2176]{1,0:T(8,128)(2,1)S(1)}, u32[]{:S(2)}, u32[]{:S(2)}) collective-permute-start(bf16[128,2176]{1,0:T(8,128)(2,1)} %get-tuple-element.138.refs_1_.x0), channel_id=1, source_target_pairs={{0,1},{1,2},{2,3},{3,0},{4,5},{5,6},{6,7},{7,4},{8,9},{9,10},{10,1... | collective-permute-start | bytes 1671176 | tf_op jit(solution)/shard_map/ppermute | solution.py:813
  139.8 15.2 %collective-permute-start.11 = (bf16[128,2176]{1,0:T(8,128)(2,1)}, bf16[128,2176]{1,0:T(8,128)(2,1)S(1)}, u32[]{:S(2)}, u32[]{:S(2)}) collective-permute-start(bf16[128,2176]{1,0:T(8,128)(2,1)} %get-tuple-element.138.refs_1_.x0), channel_id=1, source_target_pairs={{0,3},{1,0},{2,1},{3,2},{4,7},{5,4},{6,5},{7,6},{8,11},{9,8},{10,9... | collective-permute-start | bytes 1671176 | tf_op jit(solution)/shard_map/ppermute | solution.py:813
  155.0 16.0 %collective-permute-start.12 = (bf16[64,2176]{1,0:T(8,128)(2,1)S(1)}, bf16[64,2176]{1,0:T(8,128)(2,1)S(1)}, u32[]{:S(2)}, u32[]{:S(2)}) collective-permute-start(bf16[64,2176]{1,0:T(8,128)(2,1)S(1)} %slice.89), channel_id=1, source_target_pairs={{0,3},{1,0},{2,1},{3,2},{4,7},{5,4},{6,5},{7,6},{8,11},{9,8},{10,9... | collective-permute-start | bytes 835592 | tf_op jit(solution)/shard_map/ppermute | solution.py:813
  155.6 15.5 %collective-permute-start.13 = (bf16[64,2176]{1,0:T(8,128)(2,1)S(1)}, bf16[64,2176]{1,0:T(8,128)(2,1)S(1)}, u32[]{:S(2)}, u32[]{:S(2)}) collective-permute-start(bf16[64,2176]{1,0:T(8,128)(2,1)S(1)} %slice.90), channel_id=1, source_target_pairs={{0,1},{1,2},{2,3},{3,0},{4,5},{5,6},{6,7},{7,4},{8,9},{9,10},{10,1... | collective-permute-start | bytes 835592 | tf_op jit(solution)/shard_map/ppermute | solution.py:813
  168.8 17.9 %collective-permute-start.14 = (bf16[128,2176]{1,0:T(8,128)(2,1)}, bf16[128,2176]{1,0:T(8,128)(2,1)S(1)}, u32[]{:S(2)}, u32[]{:S(2)}) collective-permute-start(bf16[128,2176]{1,0:T(8,128)(2,1)} %get-tuple-element.143), channel_id=1, source_target_pairs={{0,1},{1,2},{2,3},{3,0},{4,5},{5,6},{6,7},{7,4},{8,9},{9,10},{10,1... | collective-permute-start | bytes 1671176 | tf_op jit(solution)/shard_map/ppermute | solution.py:813
  168.9 25.9 %collective-permute-start.16 = (bf16[128,2176]{1,0:T(8,128)(2,1)}, bf16[128,2176]{1,0:T(8,128)(2,1)}, u32[]{:S(2)}, u32[]{:S(2)}) collective-permute-start(bf16[128,2176]{1,0:T(8,128)(2,1)} %get-tuple-element.145), channel_id=1, source_target_pairs={{0,3},{1,0},{2,1},{3,2},{4,7},{5,4},{6,5},{7,6},{8,11},{9,8},{10,9... | collective-permute-start | bytes 1671176 | tf_op jit(solution)/shard_map/ppermute | solution.py:813
  179.8 15.0 %collective-permute-start.15 = (bf16[128,2176]{1,0:T(8,128)(2,1)S(1)}, bf16[128,2176]{1,0:T(8,128)(2,1)}, u32[]{:S(2)}, u32[]{:S(2)}) collective-permute-start(bf16[128,2176]{1,0:T(8,128)(2,1)S(1)} %get-tuple-element.144), channel_id=1, source_target_pairs={{0,2},{1,3},{2,0},{3,1},{4,6},{5,7},{6,4},{7,5},{8,10},{9,11},{10,... | collective-permute-start | bytes 1671176 | tf_op jit(solution)/shard_map/ppermute | solution.py:813
  199.2 11.4 %collective-permute-start.19 = (bf16[128,2176]{1,0:T(8,128)(2,1)}, bf16[128,2176]{1,0:T(8,128)(2,1)S(1)}, u32[]{:S(2)}, u32[]{:S(2)}) collective-permute-start(bf16[128,2176]{1,0:T(8,128)(2,1)} %get-tuple-element.156.refs_0_.g0), channel_id=1, source_target_pairs={{0,1},{1,2},{2,3},{3,0},{4,5},{5,6},{6,7},{7,4},{8,9},{9,10},{10,1... | collective-permute-start | bytes 1671176 | tf_op jit(solution)/shard_map/ppermute | solution.py:813
  200.4 13.8 %collective-permute-start.17 = (bf16[128,2176]{1,0:T(8,128)(2,1)}, bf16[128,2176]{1,0:T(8,128)(2,1)S(1)}, u32[]{:S(2)}, u32[]{:S(2)}) collective-permute-start(bf16[128,2176]{1,0:T(8,128)(2,1)} %get-tuple-element.156.refs_0_.g0), channel_id=1, source_target_pairs={{0,3},{1,0},{2,1},{3,2},{4,7},{5,4},{6,5},{7,6},{8,11},{9,8},{10,9... | collective-permute-start | bytes 1671176 | tf_op jit(solution)/shard_map/ppermute | solution.py:813
  210.6 13.1 %collective-permute-start.20 = (bf16[64,2176]{1,0:T(8,128)(2,1)S(1)}, bf16[64,2176]{1,0:T(8,128)(2,1)S(1)}, u32[]{:S(2)}, u32[]{:S(2)}) collective-permute-start(bf16[64,2176]{1,0:T(8,128)(2,1)S(1)} %slice.107), channel_id=1, source_target_pairs={{0,1},{1,2},{2,3},{3,0},{4,5},{5,6},{6,7},{7,4},{8,9},{9,10},{10,1... | collective-permute-start | bytes 835592 | tf_op jit(solution)/shard_map/ppermute | solution.py:813
  214.2 9.4 %collective-permute-start.18 = (bf16[64,2176]{1,0:T(8,128)(2,1)S(1)}, bf16[64,2176]{1,0:T(8,128)(2,1)S(1)}, u32[]{:S(2)}, u32[]{:S(2)}) collective-permute-start(bf16[64,2176]{1,0:T(8,128)(2,1)S(1)} %slice.106), channel_id=1, source_target_pairs={{0,3},{1,0},{2,1},{3,2},{4,7},{5,4},{6,5},{7,6},{8,11},{9,8},{10,9... | collective-permute-start | bytes 835592 | tf_op jit(solution)/shard_map/ppermute | solution.py:813
  217.6 4.9 %collective-permute-start.22 = (bf16[16,512]{1,0:T(8,128)(2,1)S(1)}, bf16[16,512]{1,0:T(8,128)(2,1)S(1)}, u32[]{:S(2)}, u32[]{:S(2)}) collective-permute-start(bf16[16,512]{1,0:T(8,128)(2,1)S(1)} %convolution_convert_fusion.2), channel_id=1, source_target_pairs={{0,3},{1,0},{2,1},{3,2},{4,7},{5,4},{6,5},{7,6},{8,11},{9,8},{10,9... | collective-permute-start | bytes 49160 | tf_op jit(solution)/shard_map/ppermute | solution.py:813
  217.6 5.4 %collective-permute-start.21 = (bf16[16,512]{1,0:T(8,128)(2,1)S(1)}, bf16[16,512]{1,0:T(8,128)(2,1)S(1)}, u32[]{:S(2)}, u32[]{:S(2)}) collective-permute-start(bf16[16,512]{1,0:T(8,128)(2,1)S(1)} %convolution_convert_fusion.2), channel_id=1, source_target_pairs={{0,2},{1,3},{2,0},{3,1},{4,6},{5,7},{6,4},{7,5},{8,10},{9,11},{10,... | collective-permute-start | bytes 49160 | tf_op jit(solution)/shard_map/ppermute | solution.py:813
  228.4 124.6 %all-gather.9.cloned.1.call-start = ((), (), s32[]{:S(2)}) async-start(), calls=%async_computation.4 | async-start | bytes 6352896 | tf_op jit(solution)/shard_map/all_gather | solution.py:1132
  228.4 10.8 %collective-permute-start.24 = (bf16[4,128,128]{2,1,0:T(8,128)(2,1)}, bf16[4,128,128]{2,1,0:T(8,128)(2,1)S(1)}, u32[]{:S(2)}, u32[]{:S(2)}) collective-permute-start(bf16[4,128,128]{2,1,0:T(8,128)(2,1)} %copy-done.45), channel_id=1, source_target_pairs={{4,0},{8,4},{12,8},{5,1},{9,5},{13,9},{6,2},{10,6},{14,10},{7,3},{... | collective-permute-start | bytes 393224 | tf_op jit(solution)/shard_map/ppermute | solution.py:813
  230.4 8.9 %collective-permute-start.25 = (bf16[4,128,128]{2,1,0:T(8,128)(2,1)}, bf16[4,128,128]{2,1,0:T(8,128)(2,1)S(1)}, u32[]{:S(2)}, u32[]{:S(2)}) collective-permute-start(bf16[4,128,128]{2,1,0:T(8,128)(2,1)} %copy-done.45), channel_id=1, source_target_pairs={{8,0},{12,4},{9,1},{13,5},{10,2},{14,6},{11,3},{15,7},{24,16},{28,... | collective-permute-start | bytes 393224 | tf_op jit(solution)/shard_map/ppermute | solution.py:813
  233.1 6.2 %collective-permute-start.26 = (bf16[4,128,128]{2,1,0:T(8,128)(2,1)}, bf16[4,128,128]{2,1,0:T(8,128)(2,1)S(1)}, u32[]{:S(2)}, u32[]{:S(2)}) collective-permute-start(bf16[4,128,128]{2,1,0:T(8,128)(2,1)} %copy-done.45), channel_id=1, source_target_pairs={{12,0},{13,1},{14,2},{15,3},{28,16},{29,17},{30,18},{31,19},{44,32... | collective-permute-start | bytes 393224 | tf_op jit(solution)/shard_map/ppermute | solution.py:813
  257.1 8.2 %collective-permute-start.27 = (f32[16,1536]{1,0:T(8,128)}, f32[16,1536]{1,0:T(8,128)S(1)}, u32[]{:S(2)}, u32[]{:S(2)}) collective-permute-start(f32[16,1536]{1,0:T(8,128)} %get-tuple-element.177), channel_id=1, source_target_pairs={{4,0},{8,4},{12,8},{5,1},{9,5},{13,9},{6,2},{10,6},{14,10},{7,3},{... | collective-permute-start | bytes 294920 | tf_op jit(solution)/shard_map/ppermute | solution.py:813
  268.3 15.7 %collective-permute-start.28 = (bf16[512,64]{1,0:T(8,128)(2,1)S(1)}, bf16[512,64]{1,0:T(8,128)(2,1)S(1)}, u32[]{:S(2)}, u32[]{:S(2)}) collective-permute-start(bf16[512,64]{1,0:T(8,128)(2,1)S(1)} %convolution_convert_fusion.1.p0), channel_id=1, source_target_pairs={{0,3},{1,0},{2,1},{3,2},{4,7},{5,4},{6,5},{7,6},{8,11},{9,8},{10,9... | collective-permute-start | bytes 196616 | tf_op jit(solution)/shard_map/ppermute | solution.py:813
  268.8 15.1 %collective-permute-start.29 = (bf16[512,64]{1,0:T(8,128)(2,1)S(1)}, bf16[512,64]{1,0:T(8,128)(2,1)S(1)}, u32[]{:S(2)}, u32[]{:S(2)}) collective-permute-start(bf16[512,64]{1,0:T(8,128)(2,1)S(1)} %convolution_convert_fusion.1.p0), channel_id=1, source_target_pairs={{0,2},{1,3},{2,0},{3,1},{4,6},{5,7},{6,4},{7,5},{8,10},{9,11},{10,... | collective-permute-start | bytes 196616 | tf_op jit(solution)/shard_map/ppermute | solution.py:813
  273.1 10.9 %collective-permute-start.30 = (bf16[512,64]{1,0:T(8,128)(2,1)S(1)}, bf16[512,64]{1,0:T(8,128)(2,1)S(1)}, u32[]{:S(2)}, u32[]{:S(2)}) collective-permute-start(bf16[512,64]{1,0:T(8,128)(2,1)S(1)} %convolution_convert_fusion.1.p0), channel_id=1, source_target_pairs={{0,1},{1,2},{2,3},{3,0},{4,5},{5,6},{6,7},{7,4},{8,9},{9,10},{10,1... | collective-permute-start | bytes 196616 | tf_op jit(solution)/shard_map/ppermute | solution.py:813
  273.1 23.2 %collective-permute-start.37 = (bf16[128,2048]{1,0:T(8,128)(2,1)S(1)}, bf16[128,2048]{1,0:T(8,128)(2,1)S(1)}, u32[]{:S(2)}, u32[]{:S(2)}) collective-permute-start(bf16[128,2048]{1,0:T(8,128)(2,1)S(1)} %fusion.24.refs_0_), channel_id=1, source_target_pairs={{0,1},{1,2},{2,3},{3,0},{4,5},{5,6},{6,7},{7,4},{8,9},{9,10},{10,1... | collective-permute-start | bytes 1572872 | tf_op jit(solution)/shard_map/ppermute | solution.py:813
  273.6 22.7 %collective-permute-start.38 = (bf16[128,2048]{1,0:T(8,128)(2,1)S(1)}, bf16[128,2048]{1,0:T(8,128)(2,1)S(1)}, u32[]{:S(2)}, u32[]{:S(2)}) collective-permute-start(bf16[128,2048]{1,0:T(8,128)(2,1)S(1)} %fusion.24.refs_0_), channel_id=1, source_target_pairs={{0,3},{1,0},{2,1},{3,2},{4,7},{5,4},{6,5},{7,6},{8,11},{9,8},{10,9... | collective-permute-start | bytes 1572872 | tf_op jit(solution)/shard_map/ppermute | solution.py:813
  286.5 5.6 %collective-permute-start.34 = (bf16[16,6016]{1,0:T(8,128)(2,1)S(1)}, bf16[16,6016]{1,0:T(8,128)(2,1)S(1)}, u32[]{:S(2)}, u32[]{:S(2)}) collective-permute-start(bf16[16,6016]{1,0:T(8,128)(2,1)S(1)} %get-tuple-element.191), channel_id=1, source_target_pairs={{0,4},{4,8},{8,12},{12,0},{1,5},{5,9},{9,13},{13,1},{2,6},{6,10},{... | collective-permute-start | bytes 577544 | tf_op jit(solution)/shard_map/ppermute | solution.py:813
  286.5 7.8 %collective-permute-start.35 = (bf16[16,6016]{1,0:T(8,128)(2,1)S(1)}, bf16[16,6016]{1,0:T(8,128)(2,1)S(1)}, u32[]{:S(2)}, u32[]{:S(2)}) collective-permute-start(bf16[16,6016]{1,0:T(8,128)(2,1)S(1)} %get-tuple-element.192), channel_id=1, source_target_pairs={{0,8},{4,12},{8,0},{12,4},{1,9},{5,13},{9,1},{13,5},{2,10},{6,14},... | collective-permute-start | bytes 577544 | tf_op jit(solution)/shard_map/ppermute | solution.py:813
  288.7 7.6 %collective-permute-start.36 = (bf16[16,6016]{1,0:T(8,128)(2,1)S(1)}, bf16[16,6016]{1,0:T(8,128)(2,1)S(1)}, u32[]{:S(2)}, u32[]{:S(2)}) collective-permute-start(bf16[16,6016]{1,0:T(8,128)(2,1)S(1)} %get-tuple-element.193), channel_id=1, source_target_pairs={{0,12},{4,0},{8,4},{12,8},{1,13},{5,1},{9,5},{13,9},{2,14},{6,2},{... | collective-permute-start | bytes 577544 | tf_op jit(solution)/shard_map/ppermute | solution.py:813
  297.1 26.9 %collective-permute-start.31 = (bf16[128,2048]{1,0:T(8,128)(2,1)}, bf16[128,2048]{1,0:T(8,128)(2,1)S(1)}, u32[]{:S(2)}, u32[]{:S(2)}) collective-permute-start(bf16[128,2048]{1,0:T(8,128)(2,1)} %get-tuple-element.182), channel_id=1, source_target_pairs={{0,1},{1,2},{2,3},{3,0},{4,5},{5,6},{6,7},{7,4},{8,9},{9,10},{10,1... | collective-permute-start | bytes 1572872 | tf_op jit(solution)/shard_map/ppermute | solution.py:813
  298.9 25.2 %collective-permute-start.32 = (bf16[128,2048]{1,0:T(8,128)(2,1)}, bf16[128,2048]{1,0:T(8,128)(2,1)S(1)}, u32[]{:S(2)}, u32[]{:S(2)}) collective-permute-start(bf16[128,2048]{1,0:T(8,128)(2,1)} %get-tuple-element.183), channel_id=1, source_target_pairs={{0,2},{1,3},{2,0},{3,1},{4,6},{5,7},{6,4},{7,5},{8,10},{9,11},{10,... | collective-permute-start | bytes 1572872 | tf_op jit(solution)/shard_map/ppermute | solution.py:813
  301.2 22.9 %collective-permute-start.33 = (bf16[128,2048]{1,0:T(8,128)(2,1)}, bf16[128,2048]{1,0:T(8,128)(2,1)S(1)}, u32[]{:S(2)}, u32[]{:S(2)}) collective-permute-start(bf16[128,2048]{1,0:T(8,128)(2,1)} %get-tuple-element.184), channel_id=1, source_target_pairs={{0,3},{1,0},{2,1},{3,2},{4,7},{5,4},{6,5},{7,6},{8,11},{9,8},{10,9... | collective-permute-start | bytes 1572872 | tf_op jit(solution)/shard_map/ppermute | solution.py:813
  301.3 18.8 %collective-permute-start.40 = (bf16[64,2048]{1,0:T(8,128)(2,1)S(1)}, bf16[64,2048]{1,0:T(8,128)(2,1)}, u32[]{:S(2)}, u32[]{:S(2)}) collective-permute-start(bf16[64,2048]{1,0:T(8,128)(2,1)S(1)} %slice.98), channel_id=1, source_target_pairs={{0,1},{1,2},{2,3},{3,0},{4,5},{5,6},{6,7},{7,4},{8,9},{9,10},{10,1... | collective-permute-start | bytes 786440 | tf_op jit(solution)/shard_map/ppermute | solution.py:813
  305.3 17.7 %collective-permute-start.39 = (bf16[64,2048]{1,0:T(8,128)(2,1)}, bf16[64,2048]{1,0:T(8,128)(2,1)}, u32[]{:S(2)}, u32[]{:S(2)}) collective-permute-start(bf16[64,2048]{1,0:T(8,128)(2,1)} %slice.97), channel_id=1, source_target_pairs={{0,3},{1,0},{2,1},{3,2},{4,7},{5,4},{6,5},{7,6},{8,11},{9,8},{10,9... | collective-permute-start | bytes 786440 | tf_op jit(solution)/shard_map/ppermute | solution.py:813
  328.6 11.5 %collective-permute-start.41 = (bf16[128,2048]{1,0:T(8,128)(2,1)}, bf16[128,2048]{1,0:T(8,128)(2,1)S(1)}, u32[]{:S(2)}, u32[]{:S(2)}) collective-permute-start(bf16[128,2048]{1,0:T(8,128)(2,1)} %token_rows.1.refs_0_), channel_id=1, source_target_pairs={{0,1},{1,2},{2,3},{3,0},{4,5},{5,6},{6,7},{7,4},{8,9},{9,10},{10,1... | collective-permute-start | bytes 1572872 | tf_op jit(solution)/shard_map/ppermute | solution.py:813
  329.3 11.2 %collective-permute-start.42 = (bf16[128,2048]{1,0:T(8,128)(2,1)}, bf16[128,2048]{1,0:T(8,128)(2,1)S(1)}, u32[]{:S(2)}, u32[]{:S(2)}) collective-permute-start(bf16[128,2048]{1,0:T(8,128)(2,1)} %token_rows.1.refs_0_), channel_id=1, source_target_pairs={{0,3},{1,0},{2,1},{3,2},{4,7},{5,4},{6,5},{7,6},{8,11},{9,8},{10,9... | collective-permute-start | bytes 1572872 | tf_op jit(solution)/shard_map/ppermute | solution.py:813
  340.5 6.4 %collective-permute-start.44 = (bf16[64,2048]{1,0:T(8,128)(2,1)S(1)}, bf16[64,2048]{1,0:T(8,128)(2,1)S(1)}, u32[]{:S(2)}, u32[]{:S(2)}) collective-permute-start(bf16[64,2048]{1,0:T(8,128)(2,1)S(1)} %slice.101), channel_id=1, source_target_pairs={{0,1},{1,2},{2,3},{3,0},{4,5},{5,6},{6,7},{7,4},{8,9},{9,10},{10,1... | collective-permute-start | bytes 786440 | tf_op jit(solution)/shard_map/ppermute | solution.py:813
  342.8 7.7 %collective-permute-start.43 = (bf16[64,2048]{1,0:T(8,128)(2,1)S(1)}, bf16[64,2048]{1,0:T(8,128)(2,1)S(1)}, u32[]{:S(2)}, u32[]{:S(2)}) collective-permute-start(bf16[64,2048]{1,0:T(8,128)(2,1)S(1)} %slice.100), channel_id=1, source_target_pairs={{0,3},{1,0},{2,1},{3,2},{4,7},{5,4},{6,5},{7,6},{8,11},{9,8},{10,9... | collective-permute-start | bytes 786440 | tf_op jit(solution)/shard_map/ppermute | solution.py:813
  (76 other events, 765.9 us)
Sparse Core Ops, SparseCore 0:
  10.9 56.3 all-gather.4
  69.5 74.3 all-gather.6
  228.5 29.9 reduce-scatter.1
  297.2 51.6 all-gather.8
